TPU v7x, 128 devices: a whole 4x4x4 slice. The times are simulated.
128 devices in a mesh: dp: 4 (over x), blk: 8 (over y_lo, z), mp: 4 (over y_hi, core).
Axes of the slice: x: 4, y: 4 (y_hi: 2, y_lo: 2; y = y_hi * 2 + y_lo), z: 4, core: 2. Of those that a mesh axis runs over, the one named last changes fastest.
Arguments:
- tokens: bfloat16 [8192, 1024], P(('dp', 'blk')), may hold values from -6 to 6
- cotangent: bfloat16 [8192, 1024], P(('dp', 'blk')), may hold values from -6 to 6
- seg_ids: int32 [8192], P(('dp', 'blk')), may hold values from 0 to 15, as said below
- token_boxes: int32 [4, 8192], P(None, ('dp', 'blk')), may hold values from 0 to 500, as said below
- norm1_gain: bfloat16 [1024], P('blk'), may hold values from 0.5 to 1.5
- w_query: bfloat16 [1024, 1024], P('blk', 'mp'), may hold values from -0.1875 to 0.1875
- w_key: bfloat16 [1024, 1024], P('blk', 'mp'), may hold values from -0.1875 to 0.1875
- w_value: bfloat16 [1024, 1024], P('blk', 'mp'), may hold values from -0.1875 to 0.1875
- w_out_t: bfloat16 [1024, 1024], P('blk', 'mp'), may hold values from -0.75 to 0.75
- bias_table: bfloat16 [96, 16], P('blk', 'mp'), may hold values from -3 to 3
- norm2_gain: bfloat16 [1024], P('blk'), may hold values from 0.5 to 1.5
- w_gate: bfloat16 [1024, 2816], P('blk', 'mp'), may hold values from -0.1875 to 0.1875
- w_up: bfloat16 [1024, 2816], P('blk', 'mp'), may hold values from -0.1875 to 0.1875
- w_down_t: bfloat16 [1024, 2816], P('blk', 'mp'), may hold values from -0.109375 to 0.109375
Outputs:
- mixed: bfloat16 [8192, 1024], P(('dp', 'blk'))
- grad_tokens: float32 [8192, 1024], P(('dp', 'blk'))
- grad_norm1_gain: float32 [1024], P('blk')
- grad_w_query: float32 [1024, 1024], P('blk', 'mp')
- grad_w_key: float32 [1024, 1024], P('blk', 'mp')
- grad_w_value: float32 [1024, 1024], P('blk', 'mp')
- grad_w_out_t: float32 [1024, 1024], P('blk', 'mp')
- grad_bias_table: float32 [96, 16], P('blk', 'mp')
- grad_norm2_gain: float32 [1024], P('blk')
- grad_w_gate: float32 [1024, 2816], P('blk', 'mp')
- grad_w_up: float32 [1024, 2816], P('blk', 'mp')
- grad_w_down_t: float32 [1024, 2816], P('blk', 'mp')
Inputs may be any that keep to these rules, and one draw needn't show every extreme that they name: `seg_ids`: within a group ids never fall, the first token has id 0 and the last id 15; one document of each group spans from the group's first 256 tokens to its last. `token_boxes`: x0 <= x1 and y0 <= y1.
All inputs are finite; a program needn't handle non-finite values.
Results may differ from a plain program's by a relative error of at most 0.025.
Values may be sent and summed in bfloat16 or wider, within the bound.
No kernel may reach another device: no remote copies, remote signals or barrier semaphores. Data moves between devices by JAX's collectives and lax.ppermute only.
A program may use at most 64 MiB of HBM per device.

v0:
```python
import jax
import jax.numpy as jnp
from jax import lax
from jax.sharding import PartitionSpec as P

HEAD_DIM = 64


EPS = 1e-06
SEQ_EDGES = (1, 2, 3, 4, 5, 6, 7, 8, 12, 16, 23, 32, 46, 64, 91)
BOX_EDGES = (2, 4, 6, 8, 12, 16, 24, 32, 48, 64, 96, 128, 192, 256, 384)


def bucket_of(offset, edge_list):
    magnitude = jnp.abs(offset)
    result = jnp.zeros(offset.shape, jnp.int32)
    for border in edge_list:
        result = result + (magnitude >= border).astype(jnp.int32)
    return result + 16 * (offset > 0).astype(jnp.int32)


def bucket_table(query_meta, key_meta, table_rows):
    seq_bucket = bucket_of(key_meta[3][None, :] - query_meta[3][:, None], SEQ_EDGES)
    hor_bucket = bucket_of(key_meta[1][None, :] - query_meta[1][:, None], BOX_EDGES) + 32
    ver_bucket = bucket_of(key_meta[2][None, :] - query_meta[2][:, None], BOX_EDGES) + 64
    levels = jnp.arange(table_rows, dtype=jnp.int32)
    onehot = (
        (seq_bucket[..., None] == levels)
        | (hor_bucket[..., None] == levels)
        | (ver_bucket[..., None] == levels)
    )
    return onehot.astype(jnp.bfloat16)


def rms_scale(values):
    return lax.rsqrt(jnp.mean(values * values, axis=-1, keepdims=True) + EPS)


def contract_rows(left, right):
    return lax.dot_general(
        left, right, (((0,), (0,)), ((), ())), preferred_element_type=jnp.float32
    )


def contract_cols(left, right):
    return lax.dot_general(
        left, right, (((1,), (1,)), ((), ())), preferred_element_type=jnp.float32
    )


def gated_unit(gate, upward):
    return jax.nn.gelu(gate, approximate=True) * upward


def norm_back(inputs, scale_rows, gain, normed_grad):
    gain_grad = jnp.sum(normed_grad * inputs * scale_rows, axis=0)
    weighted = normed_grad * gain
    cubed = scale_rows * scale_rows * scale_rows
    input_grad = scale_rows * weighted - inputs * cubed * jnp.mean(
        weighted * inputs, axis=1, keepdims=True
    )
    return (gain_grad, input_grad)


def shards(
    tokens,
    cotangent,
    seg_ids,
    token_boxes,
    norm1_gain,
    w_query,
    w_key,
    w_value,
    w_out_t,
    bias_table,
    norm2_gain,
    w_gate,
    w_up,
    w_down_t,
):
    gain_one, query_w, key_w, value_w, out_w, table = (
        lax.all_gather(norm1_gain, "blk", axis=0, tiled=True),
        lax.all_gather(w_query, "blk", axis=0, tiled=True),
        lax.all_gather(w_key, "blk", axis=0, tiled=True),
        lax.all_gather(w_value, "blk", axis=0, tiled=True),
        lax.all_gather(w_out_t, "blk", axis=0, tiled=True),
        lax.all_gather(bias_table, "blk", axis=0, tiled=True),
    )
    gain_two, gate_w, upward_w, down_w = (
        lax.all_gather(norm2_gain, "blk", axis=0, tiled=True),
        lax.all_gather(w_gate, "blk", axis=0, tiled=True),
        lax.all_gather(w_up, "blk", axis=0, tiled=True),
        lax.all_gather(w_down_t, "blk", axis=0, tiled=True),
    )
    rows = tokens.shape[0]
    local_heads = query_w.shape[1] // HEAD_DIM
    score_scale = HEAD_DIM ** (-0.5)
    inputs = tokens.astype(jnp.float32)
    scale_one = rms_scale(inputs)
    normed_one = (inputs * scale_one * gain_one.astype(jnp.float32)).astype(jnp.bfloat16)
    queries = jnp.dot(normed_one, query_w, preferred_element_type=jnp.float32).astype(jnp.bfloat16)
    keys_local = jnp.dot(normed_one, key_w, preferred_element_type=jnp.float32).astype(jnp.bfloat16)
    values_local = jnp.dot(normed_one, value_w, preferred_element_type=jnp.float32).astype(
        jnp.bfloat16
    )
    centre_x = token_boxes[0] + token_boxes[2]
    centre_y = token_boxes[1] + token_boxes[3]
    first_place = lax.axis_index("blk") * rows
    query_meta = jnp.stack(
        [seg_ids, centre_x, centre_y, first_place + jnp.arange(rows, dtype=jnp.int32)]
    )
    key_info = lax.all_gather(jnp.stack([seg_ids, centre_x, centre_y]), "blk", axis=1, tiled=True)
    length = key_info.shape[1]
    meta_all = jnp.concatenate([key_info, jnp.arange(length, dtype=jnp.int32)[None, :]], axis=0)
    keys_all, values_all = (
        lax.all_gather(keys_local, "blk", axis=0, tiled=True),
        lax.all_gather(values_local, "blk", axis=0, tiled=True),
    )
    width = min(128, length)
    pieces = length // width
    query_heads = queries.reshape(rows, local_heads, HEAD_DIM)

    def scores_at(key_source, index):
        start = index * width
        key_piece = lax.dynamic_slice_in_dim(key_source, start, width, 0).reshape(
            width, local_heads, HEAD_DIM
        )
        key_meta = lax.dynamic_slice_in_dim(meta_all, start, width, 1)
        onehot = bucket_table(query_meta, key_meta, table.shape[0])
        raw_scores = (
            jnp.einsum("qhd,khd->hqk", query_heads, key_piece, preferred_element_type=jnp.float32)
            * score_scale
        )
        bias = jnp.einsum("qkj,jh->hqk", onehot, table, preferred_element_type=jnp.float32)
        allowed = (key_meta[0][None, :] == query_meta[0][:, None])[None]
        return (raw_scores + bias, allowed, onehot, key_piece)

    def max_step(index, carry):
        running_max, running_sum = carry
        scores, allowed, onehot, key_piece = scores_at(keys_all, index)
        masked = jnp.where(allowed, scores, -1e30)
        new_max = jnp.maximum(running_max, jnp.max(masked, axis=2))
        weights = jnp.where(allowed, jnp.exp(masked - new_max[:, :, None]), 0.0)
        return (new_max, running_sum * jnp.exp(running_max - new_max) + jnp.sum(weights, axis=2))

    start_max = jnp.full((local_heads, rows), -1e30, jnp.float32)
    start_sum = jnp.zeros((local_heads, rows), jnp.float32)
    running_max, running_sum = lax.fori_loop(0, pieces, max_step, (start_max, start_sum))
    log_total = running_max + jnp.log(running_sum)

    def value_step(index, total):
        scores, allowed, onehot, key_piece = scores_at(keys_all, index)
        probs = jnp.where(allowed, jnp.exp(scores - log_total[:, :, None]), 0.0).astype(
            jnp.bfloat16
        )
        value_piece = lax.dynamic_slice_in_dim(values_all, index * width, width, 0).reshape(
            width, local_heads, HEAD_DIM
        )
        return total + jnp.einsum(
            "hqk,khd->qhd", probs, value_piece, preferred_element_type=jnp.float32
        )

    attn_exact = lax.fori_loop(
        0, pieces, value_step, jnp.zeros((rows, local_heads, HEAD_DIM), jnp.float32)
    )
    attended = attn_exact.reshape(rows, -1).astype(jnp.bfloat16)
    branch = lax.psum(contract_cols(attended, out_w).astype(jnp.bfloat16), "mp").astype(jnp.float32)
    middle = inputs + branch
    scale_two = rms_scale(middle)
    normed_two = (middle * scale_two * gain_two.astype(jnp.float32)).astype(jnp.bfloat16)
    gate = jnp.dot(normed_two, gate_w, preferred_element_type=jnp.float32)
    upward = jnp.dot(normed_two, upward_w, preferred_element_type=jnp.float32)
    gated_vals, pull_back = jax.vjp(gated_unit, gate, upward)
    hidden = gated_vals.astype(jnp.bfloat16)
    ffn_out = lax.psum(contract_cols(hidden, down_w).astype(jnp.bfloat16), "mp").astype(jnp.float32)
    mixed = (middle + ffn_out).astype(jnp.bfloat16)
    down_grad_w = contract_rows(cotangent, hidden)
    hidden_grad = jnp.dot(cotangent, down_w, preferred_element_type=jnp.float32)
    gate_grad, upward_grad = pull_back(hidden_grad)
    gate_low = gate_grad.astype(jnp.bfloat16)
    upward_low = upward_grad.astype(jnp.bfloat16)
    gate_grad_w = contract_rows(normed_two, gate_low)
    upward_grad_w = contract_rows(normed_two, upward_low)
    normed_two_grad = lax.psum(
        (contract_cols(gate_low, gate_w) + contract_cols(upward_low, upward_w)).astype(
            jnp.bfloat16
        ),
        "mp",
    ).astype(jnp.float32)
    gain_two_grad, middle_part = norm_back(
        middle, scale_two, gain_two.astype(jnp.float32), normed_two_grad
    )
    middle_grad = cotangent.astype(jnp.float32) + middle_part
    branch_low = middle_grad.astype(jnp.bfloat16)
    out_grad_w = contract_rows(branch_low, attended)
    attended_grad = jnp.dot(branch_low, out_w, preferred_element_type=jnp.float32).astype(
        jnp.bfloat16
    )
    grad_heads = attended_grad.reshape(rows, local_heads, HEAD_DIM)
    row_delta = jnp.transpose(jnp.sum(grad_heads.astype(jnp.float32) * attn_exact, axis=2))
    keys_back, values_back = (keys_all, values_all)

    def grad_step(index, carry):
        query_sum, key_grad, value_grad, table_grad = carry
        start = index * width
        scores, allowed, onehot, key_piece = scores_at(keys_back, index)
        probs = jnp.where(allowed, jnp.exp(scores - log_total[:, :, None]), 0.0)
        probs_low = probs.astype(jnp.bfloat16)
        value_piece = lax.dynamic_slice_in_dim(values_back, start, width, 0).reshape(
            width, local_heads, HEAD_DIM
        )
        prob_grad = jnp.einsum(
            "qhd,khd->hqk", grad_heads, value_piece, preferred_element_type=jnp.float32
        )
        score_grad = (probs * (prob_grad - row_delta[:, :, None])).astype(jnp.bfloat16)
        query_sum = query_sum + jnp.einsum(
            "hqk,khd->qhd", score_grad, key_piece, preferred_element_type=jnp.float32
        )
        key_piece_grad = (
            jnp.einsum("hqk,qhd->khd", score_grad, query_heads, preferred_element_type=jnp.float32)
            * score_scale
        )
        value_piece_grad = jnp.einsum(
            "hqk,qhd->khd", probs_low, grad_heads, preferred_element_type=jnp.float32
        )
        key_grad = lax.dynamic_update_slice_in_dim(key_grad, key_piece_grad, start, 0)
        value_grad = lax.dynamic_update_slice_in_dim(value_grad, value_piece_grad, start, 0)
        table_grad = table_grad + jnp.einsum(
            "qkj,hqk->jh", onehot, score_grad, preferred_element_type=jnp.float32
        )
        return (query_sum, key_grad, value_grad, table_grad)

    zero_keys = jnp.zeros((length, local_heads, HEAD_DIM), jnp.float32)
    start_carry = (
        jnp.zeros((rows, local_heads, HEAD_DIM), jnp.float32),
        zero_keys,
        zero_keys,
        jnp.zeros(table.shape, jnp.float32),
    )
    query_sum, key_grad, value_grad, table_grad = lax.fori_loop(0, pieces, grad_step, start_carry)
    key_share, value_share = (
        lax.psum_scatter(
            key_grad.reshape(length, -1).astype(jnp.bfloat16),
            "blk",
            scatter_dimension=0,
            tiled=True,
        ).astype(jnp.float32),
        lax.psum_scatter(
            value_grad.reshape(length, -1).astype(jnp.bfloat16),
            "blk",
            scatter_dimension=0,
            tiled=True,
        ).astype(jnp.float32),
    )
    query_low = (query_sum * score_scale).reshape(rows, -1).astype(jnp.bfloat16)
    key_low = key_share.astype(jnp.bfloat16)
    value_low = value_share.astype(jnp.bfloat16)
    query_grad_w = contract_rows(normed_one, query_low)
    key_grad_w = contract_rows(normed_one, key_low)
    value_grad_w = contract_rows(normed_one, value_low)
    normed_partial = (
        contract_cols(query_low, query_w)
        + contract_cols(key_low, key_w)
        + contract_cols(value_low, value_w)
    )
    normed_one_grad = lax.psum(normed_partial.astype(jnp.bfloat16), "mp").astype(jnp.float32)
    gain_one_grad, input_part = norm_back(
        inputs, scale_one, gain_one.astype(jnp.float32), normed_one_grad
    )
    tokens_grad = middle_grad + input_part
    (
        part_g1,
        part_wq,
        part_wk,
        part_wv,
        part_wo,
        part_tab,
        part_g2,
        part_gate,
        part_up,
        part_down,
    ) = (
        lax.psum_scatter(
            gain_one_grad.astype(jnp.bfloat16), "blk", scatter_dimension=0, tiled=True
        ).astype(jnp.float32),
        lax.psum_scatter(
            query_grad_w.astype(jnp.bfloat16), "blk", scatter_dimension=0, tiled=True
        ).astype(jnp.float32),
        lax.psum_scatter(
            key_grad_w.astype(jnp.bfloat16), "blk", scatter_dimension=0, tiled=True
        ).astype(jnp.float32),
        lax.psum_scatter(
            value_grad_w.astype(jnp.bfloat16), "blk", scatter_dimension=0, tiled=True
        ).astype(jnp.float32),
        lax.psum_scatter(
            out_grad_w.astype(jnp.bfloat16), "blk", scatter_dimension=0, tiled=True
        ).astype(jnp.float32),
        lax.psum_scatter(
            table_grad.astype(jnp.bfloat16), "blk", scatter_dimension=0, tiled=True
        ).astype(jnp.float32),
        lax.psum_scatter(
            gain_two_grad.astype(jnp.bfloat16), "blk", scatter_dimension=0, tiled=True
        ).astype(jnp.float32),
        lax.psum_scatter(
            gate_grad_w.astype(jnp.bfloat16), "blk", scatter_dimension=0, tiled=True
        ).astype(jnp.float32),
        lax.psum_scatter(
            upward_grad_w.astype(jnp.bfloat16), "blk", scatter_dimension=0, tiled=True
        ).astype(jnp.float32),
        lax.psum_scatter(
            down_grad_w.astype(jnp.bfloat16), "blk", scatter_dimension=0, tiled=True
        ).astype(jnp.float32),
    )
    (
        final_g1,
        final_wq,
        final_wk,
        final_wv,
        final_wo,
        final_tab,
        final_g2,
        final_gate,
        final_up,
        final_down,
    ) = (
        lax.psum(part_g1.astype(jnp.bfloat16), "dp").astype(jnp.float32),
        lax.psum(part_wq.astype(jnp.bfloat16), "dp").astype(jnp.float32),
        lax.psum(part_wk.astype(jnp.bfloat16), "dp").astype(jnp.float32),
        lax.psum(part_wv.astype(jnp.bfloat16), "dp").astype(jnp.float32),
        lax.psum(part_wo.astype(jnp.bfloat16), "dp").astype(jnp.float32),
        lax.psum(part_tab.astype(jnp.bfloat16), "dp").astype(jnp.float32),
        lax.psum(part_g2.astype(jnp.bfloat16), "dp").astype(jnp.float32),
        lax.psum(part_gate.astype(jnp.bfloat16), "dp").astype(jnp.float32),
        lax.psum(part_up.astype(jnp.bfloat16), "dp").astype(jnp.float32),
        lax.psum(part_down.astype(jnp.bfloat16), "dp").astype(jnp.float32),
    )
    return (
        mixed,
        tokens_grad,
        final_g1,
        final_wq,
        final_wk,
        final_wv,
        final_wo,
        final_tab,
        final_g2,
        final_gate,
        final_up,
        final_down,
    )


def solution(mesh):
    in_specs = (
        P(("dp", "blk"), None),
        P(("dp", "blk"), None),
        P(("dp", "blk")),
        P(None, ("dp", "blk")),
        P("blk"),
        P("blk", "mp"),
        P("blk", "mp"),
        P("blk", "mp"),
        P("blk", "mp"),
        P("blk", "mp"),
        P("blk"),
        P("blk", "mp"),
        P("blk", "mp"),
        P("blk", "mp"),
    )
    out_specs = (
        P(("dp", "blk"), None),
        P(("dp", "blk"), None),
        P("blk"),
        P("blk", "mp"),
        P("blk", "mp"),
        P("blk", "mp"),
        P("blk", "mp"),
        P("blk", "mp"),
        P("blk"),
        P("blk", "mp"),
        P("blk", "mp"),
        P("blk", "mp"),
    )
    return jax.shard_map(shards, mesh=mesh, in_specs=in_specs, out_specs=out_specs, check_vma=False)
```

profile of v0, /device:TPU:0, one launch (start us, length us, event | category | flops | bytes accessed | tf_op | source)
XLA Modules:
  0.0 1283.5 jit_solution(1759583248528265200)
XLA Ops:
  7.2 20.3 %all-gather = bf16[8,1,128]{2,1,0:T(2,128)(2,1)S(1)} all-gather(bf16[1,1,128]{2,1,0:T(2,128)(2,1)} %bitcast.281), channel_id=1, replica_groups=mesh['dp'=4,'blk'=8,'mp'=4] {'blk'}, dimensions={0}, use_global_device_ids=true | all-gather | bytes 2304 | tf_op jit(solution)/shard_map/all_gather | solution.py:82
  29.3 29.5 %all_gather.43 = bf16[1024,256]{1,0:T(8,128)(2,1)S(1)} all-gather(bf16[128,256]{1,0:T(8,128)(2,1)} %param.26), channel_id=1, replica_groups=mesh['dp'=4,'blk'=8,'mp'=4] {'blk'}, dimensions={0}, use_global_device_ids=true | all-gather | bytes 589824 | tf_op jit(solution)/shard_map/all_gather | solution.py:84
  61.1 29.7 %all_gather.40 = bf16[1024,256]{1,0:T(8,128)(2,1)S(1)} all-gather(bf16[128,256]{1,0:T(8,128)(2,1)S(1)} %copy-done.35), channel_id=1, replica_groups=mesh['dp'=4,'blk'=8,'mp'=4] {'blk'}, dimensions={0}, use_global_device_ids=true | all-gather | bytes 589824 | tf_op jit(solution)/shard_map/all_gather | solution.py:85
  92.0 28.1 %all_gather.42 = s32[3,2048]{1,0:T(4,128)S(1)} all-gather(s32[3,256]{1,0:T(4,128)S(1)} %pad_add_fusion.1), channel_id=1, replica_groups=mesh['dp'=4,'blk'=8,'mp'=4] {'blk'}, dimensions={1}, use_global_device_ids=true | all-gather | bytes 27648 | tf_op jit(solution)/shard_map/all_gather | solution.py:112
  120.1 29.5 %all_gather.45 = bf16[1024,256]{1,0:T(8,128)(2,1)S(1)} all-gather(bf16[128,256]{1,0:T(8,128)(2,1)S(1)} %copy-done.36), channel_id=1, replica_groups=mesh['dp'=4,'blk'=8,'mp'=4] {'blk'}, dimensions={0}, use_global_device_ids=true | all-gather | bytes 589824 | tf_op jit(solution)/shard_map/all_gather | solution.py:83
  165.3 28.8 %all_gather.47 = bf16[1024,256]{1,0:T(8,128)(2,1)S(1)} all-gather(bf16[128,256]{1,0:T(8,128)(2,1)S(1)} %copy-done.37), channel_id=1, replica_groups=mesh['dp'=4,'blk'=8,'mp'=4] {'blk'}, dimensions={0}, use_global_device_ids=true | all-gather | bytes 589824 | tf_op jit(solution)/shard_map/all_gather | solution.py:86
  196.6 96.0 %while.50 = (s32[]{:T(128)}, f32[4,256]{1,0:T(4,128)S(1)}, f32[4,256]{1,0:T(4,128)S(1)}, s32[4,2048]{1,0:T(4,128)S(1)}, s32[256]{0:T(256)S(1)}, /*index=5*/bf16[...) while((s32[]{:T(128)}, f32[4,256]{1,0:T(4,128)S(1)}, ...), condition=%wide.region_4.5_spmd.clone, body=%wide.region_1.4_spmd.clone.sunk | while | flops 63509764 | bytes 4427738 | solution.py:148
  294.9 97.2 %while.51 = (s32[]{:T(128)}, f32[256,4,64]{0,2,1:T(8,128)S(1)}, bf16[2048,256]{0,1:T(8,128)(2,1)}, s32[4,2048]{1,0:T(4,128)S(1)}, s32[256]{0:T(256)S(1)}, /*inde...) while((s32[]{:T(128)}, f32[256,4,64]{0,2,1:T(8,128)S(1)}, ...), condition=%wide.region_6.7_spmd.clone, body=%wide.region_5.6_spmd.clone.sunk | while | flops 80150784 | bytes 4018145 | solution.py:163
  412.3 22.6 %all-reduce.12.cloned.1.call-done = bf16[256,1024]{1,0:T(8,128)(2,1)} async-done(((bf16[256,1024]{1,0:T(8,128)(2,1)}), bf16[256,1024]{1,0:T(8,128)(2,1)}) %all-reduce.12.cloned.1.call-update) | async-done | bytes 524304 | tf_op jit(solution)/shard_map/psum | solution.py:167
  437.4 38.4 %all-gather.13.cloned.1.call-done = bf16[1024,704]{0,1:T(8,128)(2,1)} async-done(((bf16[128,704]{0,1:T(8,128)(2,1)}), bf16[1024,704]{0,1:T(8,128)(2,1)}) %all-gather.13.cloned.1.call-update) | async-done | bytes 1441808 | tf_op jit(solution)/shard_map/all_gather | solution.py:91
  478.6 40.2 %all-gather.15.cloned.1.call-done = bf16[1024,704]{0,1:T(8,128)(2,1)} async-done(((bf16[128,704]{0,1:T(8,128)(2,1)}), bf16[1024,704]{0,1:T(8,128)(2,1)}) %all-gather.15.cloned.1.call-update) | async-done | bytes 1441808 | tf_op jit(solution)/shard_map/all_gather | solution.py:92
  521.6 40.2 %all-gather.17.cloned.1.call-done = bf16[1024,704]{0,1:T(8,128)(2,1)} async-done(((bf16[128,704]{0,1:T(8,128)(2,1)}), bf16[1024,704]{0,1:T(8,128)(2,1)}) %all-gather.17.cloned.1.call-update) | async-done | bytes 1441808 | tf_op jit(solution)/shard_map/all_gather | solution.py:93
  568.4 43.6 %all-reduce.14.cloned.1.call-done = bf16[256,1024]{1,0:T(8,128)(2,1)} async-done(((bf16[256,1024]{1,0:T(8,128)(2,1)}), bf16[256,1024]{1,0:T(8,128)(2,1)}) %all-reduce.14.cloned.1.call-update) | async-done | bytes 524304 | tf_op jit(solution)/shard_map/psum | solution.py:184
  617.6 191.9 %while.52 = (s32[]{:T(128)}, f32[256,4,64]{0,2,1:T(8,128)S(1)}, bf16[2048,4,64]{0,2,1:T(8,128)(2,1)}, bf16[2048,4,64]{0,2,1:T(8,128)(2,1)}, f32[96,4]{0,1:T(4,12...) while((s32[]{:T(128)}, f32[256,4,64]{0,2,1:T(8,128)S(1)}, ...), condition=%wide.region_14.15_spmd.clone, body=%wide.region_13.14_spmd.clone.sunk | while | flops 171803648 | bytes 9858234 | solution.py:240
  827.1 21.4 %reduce-scatter.17.cloned.1.call-done = bf16[256,256]{0,1:T(8,128)(2,1)} async-done(((bf16[2048,256]{0,1:T(8,128)(2,1)}), bf16[256,256]{0,1:T(8,128)(2,1)}) %reduce-scatter.17.cloned.1.call-update) | async-done | bytes 131088 | tf_op jit(solution)/shard_map/reduce_scatter | solution.py:242
  850.7 38.1 %reduce-scatter.19.cloned.1.call-done = bf16[256,256]{0,1:T(8,128)(2,1)} async-done(((bf16[2048,256]{0,1:T(8,128)(2,1)}), bf16[256,256]{0,1:T(8,128)(2,1)}) %reduce-scatter.19.cloned.1.call-update) | async-done | bytes 131088 | tf_op jit(solution)/shard_map/reduce_scatter | solution.py:248
  898.5 32.2 %reduce-scatter.29.cloned.1.call-done = bf16[128,704]{1,0:T(8,128)(2,1)} async-done(((bf16[1024,704]{1,0:T(8,128)(2,1)}), bf16[128,704]{1,0:T(8,128)(2,1)}) %reduce-scatter.29.cloned.1.call-update) | async-done | bytes 180240
  932.5 40.4 %reduce-scatter.31.cloned.1.call-done = bf16[128,704]{1,0:T(8,128)(2,1)} async-done(((bf16[1024,704]{1,0:T(8,128)(2,1)}), bf16[128,704]{1,0:T(8,128)(2,1)}) %reduce-scatter.31.cloned.1.call-update) | async-done | bytes 180240
  974.7 40.4 %reduce-scatter.33.cloned.1.call-done = bf16[128,704]{1,0:T(8,128)(2,1)} async-done(((bf16[1024,704]{1,0:T(8,128)(2,1)}), bf16[128,704]{1,0:T(8,128)(2,1)}) %reduce-scatter.33.cloned.1.call-update) | async-done | bytes 180240
  1016.8 37.4 %reduce-scatter.21.cloned.1.call-done = bf16[128,256]{1,0:T(8,128)(2,1)} async-done(((bf16[1024,256]{1,0:T(8,128)(2,1)}), bf16[128,256]{1,0:T(8,128)(2,1)}) %reduce-scatter.21.cloned.1.call-update) | async-done | bytes 65552 | tf_op jit(solution)/shard_map/reduce_scatter | solution.py:286
  1054.2 39.0 %reduce-scatter.27.cloned.1.call-done = bf16[128,256]{1,0:T(8,128)(2,1)} async-done(((bf16[1024,256]{1,0:T(8,128)(2,1)}), bf16[128,256]{1,0:T(8,128)(2,1)}) %reduce-scatter.27.cloned.1.call-update) | async-done | bytes 65552 | tf_op jit(solution)/shard_map/reduce_scatter | solution.py:295
  1093.2 38.8 %reduce-scatter.23.cloned.1.call-done = bf16[128,256]{1,0:T(8,128)(2,1)} async-done(((bf16[1024,256]{1,0:T(8,128)(2,1)}), bf16[128,256]{1,0:T(8,128)(2,1)}) %reduce-scatter.23.cloned.1.call-update) | async-done | bytes 65552 | tf_op jit(solution)/shard_map/reduce_scatter | solution.py:289
  1132.0 39.0 %reduce-scatter.25.cloned.1.call-done = bf16[128,256]{1,0:T(8,128)(2,1)} async-done(((bf16[1024,256]{1,0:T(8,128)(2,1)}), bf16[128,256]{1,0:T(8,128)(2,1)}) %reduce-scatter.25.cloned.1.call-update) | async-done | bytes 65552 | tf_op jit(solution)/shard_map/reduce_scatter | solution.py:292
  1171.0 46.8 %all-reduce.16.cloned.1.call-done = (bf16[256,1024]{1,0:T(8,128)(2,1)}, bf16[256,1024]{1,0:T(8,128)(2,1)}) async-done(((bf16[256,1024]{1,0:T(8,128)(2,1)}, bf16[256,1024]{1,0:T(8,128)(2,1)}), (bf16[256,1024]{1,0:T(8,128)(2,1)}, bf16[256,1024]{1,0:T(8,128)(2,1)})) %all-reduce.16.cloned.1.call-update) | async-done | bytes 1048592 | tf_op jit(solution)/shard_map/psum | solution.py:175
  (1002 shorter events, 538.6 us)
Async XLA Ops:
  7.2 187.0 %all-gather.11.cloned.1.call-start = ((), (), s32[]{:S(2)}) async-start(), calls=%async_computation.10 | async-start | bytes 1179648 | tf_op jit(solution)/shard_map/all_gather | solution.py:116
  27.5 122.1 %copy-start.38 = (f32[8,1,128]{2,1,0:T(1,128)}, f32[8,1,128]{2,1,0:T(1,128)S(1)}, u32[]{:S(2)}) copy-start(f32[8,1,128]{2,1,0:T(1,128)S(1)} %convert_element_type.1780) | copy-start | bytes 12292
  29.3 120.3 %copy-start.40 = (f32[256]{0:T(256)}, f32[256]{0:T(256)S(1)}, u32[]{:S(2)}) copy-start(f32[256]{0:T(256)S(1)} %get-tuple-element.1069) | copy-start | bytes 3076
  61.1 231.5 %all-gather.9.cloned.1.call-start = ((), (), s32[]{:S(2)}) async-start(), calls=%async_computation.9 | async-start | bytes 1179648 | tf_op jit(solution)/shard_map/all_gather | solution.py:117
  91.9 343.0 %all-reduce.12.cloned.1.call-start = ((), (), s32[]{:S(2)}) async-start(), calls=%async_computation.11 | async-start | bytes 1048576 | tf_op jit(solution)/shard_map/psum | solution.py:167
  194.1 198.0 %copy-start.6 = (bf16[1024,256]{1,0:T(8,128)(2,1)}, bf16[1024,256]{1,0:T(8,128)(2,1)S(1)}, u32[]{:S(2)}) copy-start(bf16[1024,256]{1,0:T(8,128)(2,1)S(1)} %all_gather.47) | copy-start | bytes 1572868
  393.3 82.5 %all-gather.13.cloned.1.call-start = ((), (), s32[]{:S(2)}) async-start(), calls=%async_computation.12 | async-start | bytes 1622016 | tf_op jit(solution)/shard_map/all_gather | solution.py:91
  393.9 124.9 %all-gather.15.cloned.1.call-start = ((), (), s32[]{:S(2)}) async-start(), calls=%async_computation.13 | async-start | bytes 1622016 | tf_op jit(solution)/shard_map/all_gather | solution.py:92
  394.5 167.3 %all-gather.17.cloned.1.call-start = ((), (), s32[]{:S(2)}) async-start(), calls=%async_computation.14 | async-start | bytes 1622016 | tf_op jit(solution)/shard_map/all_gather | solution.py:93
  395.1 216.9 %all-reduce.14.cloned.1.call-start = ((), (), s32[]{:S(2)}) async-start(), calls=%async_computation.15 | async-start | bytes 1048576 | tf_op jit(solution)/shard_map/psum | solution.py:184
  437.4 84.2 %copy-start.2 = (bf16[256,1024]{1,0:T(8,128)(2,1)}, bf16[256,1024]{1,0:T(8,128)(2,1)S(1)}, u32[]{:S(2)}) copy-start(bf16[256,1024]{1,0:T(8,128)(2,1)S(1)} %multiply_convert_fusion) | copy-start | bytes 1572868
  478.6 83.2 %copy-start.17 = (bf16[256,1024]{1,0:T(8,128)(2,1)S(1)}, bf16[256,1024]{1,0:T(8,128)(2,1)}, u32[]{:S(2)}) copy-start(bf16[256,1024]{1,0:T(8,128)(2,1)} %param.21) | copy-start | bytes 1572868
  568.3 280.1 %reduce-scatter.17.cloned.1.call-start = ((), (), s32[]{:S(2)}) async-start(), calls=%async_computation.16 | async-start | bytes 1179648 | tf_op jit(solution)/shard_map/reduce_scatter | solution.py:242
  809.6 79.2 %reduce-scatter.19.cloned.1.call-start = ((), (), s32[]{:S(2)}) async-start(), calls=%async_computation.17 | async-start | bytes 1179648 | tf_op jit(solution)/shard_map/reduce_scatter | solution.py:248
  810.3 120.4 %reduce-scatter.29.cloned.1.call-start = ((), (), s32[]{:S(2)}) async-start(), calls=%async_computation.22 | async-start | bytes 1769472
  815.0 157.9 %reduce-scatter.31.cloned.1.call-start = ((), (), s32[]{:S(2)}) async-start(), calls=%async_computation.23 | async-start | bytes 1769472
  819.5 195.6 %reduce-scatter.33.cloned.1.call-start = ((), (), s32[]{:S(2)}) async-start(), calls=%async_computation.24 | async-start | bytes 1769472
  823.8 230.4 %reduce-scatter.21.cloned.1.call-start = ((), (), s32[]{:S(2)}) async-start(), calls=%async_computation.18 | async-start | bytes 589824 | tf_op jit(solution)/shard_map/reduce_scatter | solution.py:286
  825.8 267.4 %reduce-scatter.27.cloned.1.call-start = ((), (), s32[]{:S(2)}) async-start(), calls=%async_computation.21 | async-start | bytes 589824 | tf_op jit(solution)/shard_map/reduce_scatter | solution.py:295
  827.0 305.0 %reduce-scatter.23.cloned.1.call-start = ((), (), s32[]{:S(2)}) async-start(), calls=%async_computation.19 | async-start | bytes 589824 | tf_op jit(solution)/shard_map/reduce_scatter | solution.py:289
  850.6 320.3 %reduce-scatter.25.cloned.1.call-start = ((), (), s32[]{:S(2)}) async-start(), calls=%async_computation.20 | async-start | bytes 589824 | tf_op jit(solution)/shard_map/reduce_scatter | solution.py:292
  890.9 326.9 %all-reduce.16.cloned.1.call-start = ((), (), s32[]{:S(2)}) async-start(), calls=%async_computation.25 | async-start | bytes 2097152 | tf_op jit(solution)/shard_map/psum | solution.py:175
  896.5 354.0 %copy-start.43 = (f32[256]{0:T(256)S(1)}, f32[256]{0:T(256)}, u32[]{:S(2)}) copy-start(f32[256]{0:T(256)} %get-tuple-element.1068) | copy-start | bytes 3076
  896.6 369.9 %all-reduce.18.cloned.1.call-start = ((), (), s32[]{:S(2)}) async-start(), calls=%async_computation.26 | async-start | bytes 1605632 | tf_op jit(solution)/shard_map/psum | solution.py:327
  (133 other events, 990.2 us)
Sparse Core Ops, SparseCore 0:
  61.2 38.2 all-gather.10
  101.7 38.3 all-gather.8
  393.4 41.3 all-reduce.11
  436.3 39.4 all-gather.12
  477.2 41.5 all-gather.14
  520.2 41.5 all-gather.16
  568.4 43.4 all-reduce.13
  809.7 38.6 reduce-scatter.16
  850.8 37.8 reduce-scatter.18
  891.0 39.6 reduce-scatter.28
  933.2 39.7 reduce-scatter.30
  975.2 39.8 reduce-scatter.32
  1017.4 36.7 reduce-scatter.20
  1056.5 36.5 reduce-scatter.26
  1095.4 36.5 reduce-scatter.22
  1134.3 36.5 reduce-scatter.24
  1173.9 43.8 all-reduce.15
  1221.3 45.0 all-reduce.17
where the time goes:
time: 1290 us; the launch traced here: 1280 us
  waiting for transfers between devices  574 us (44%)
  matrix products  307 us (24%)
  blocking collectives  228 us (18%)
  local copies, waits for them, and re-layouts  84.6 us (7%)
  other arithmetic  68.6 us (5%)
  between operations  16.1 us (1%)
    dot_general x48, matrix products, scores_at(): jnp.einsum('qkj,jh->hqk', onehot, table, preferred_element_type=jnp.float32)  168 us
    unnamed x21, waiting for transfers between devices  116 us
    dot_general x16, matrix products, grad_step(): jnp.einsum('qkj,hqk->jh', onehot, score_grad, preferred_element_type=jnp....  53.8 us
    psum x1, waiting for transfers between devices, shards(): lax.psum(contract_cols(hidden, down_w).astype(jnp.bfloat16), 'mp')  46.8 us
    psum x1, waiting for transfers between devices, shards(): lax.psum((contract_cols(gate_low, gate_w) + contract_cols(upward_low, upw...  43.6 us
    all_gather x1, waiting for transfers between devices, shards(): lax.all_gather(w_down_t, 'blk', axis=0, tiled=True)  40.2 us
    all_gather x1, waiting for transfers between devices, shards(): lax.all_gather(w_up, 'blk', axis=0, tiled=True)  40.2 us
    reduce_scatter x1, waiting for transfers between devices, shards(): lax.psum_scatter(value_grad_w.astype(jnp.bfloat16), 'blk', scatter_dimens...  39 us
  transfers between devices with their start and end apart: 18, of which 16 were waited for; matrix products, arithmetic and copies ran while one was open for 11% of the time, Pallas kernels for 0%

commit v1 on v0

v1 whole, which is shorter than its diff:
```python
import functools

import jax
import jax.numpy as jnp
from jax import lax
from jax.experimental import pallas as pl
from jax.experimental.pallas import tpu as pltpu
from jax.sharding import PartitionSpec as P

HEAD_DIM = 64
EPS = 1e-06
SEQ_EDGES = (1, 2, 3, 4, 5, 6, 7, 8, 12, 16, 23, 32, 46, 64, 91)
BOX_EDGES = (2, 4, 6, 8, 12, 16, 24, 32, 48, 64, 96, 128, 192, 256, 384)
BF16 = jnp.bfloat16
F32 = jnp.float32
LANES = 128
MIB = 2**20
VMEM = pl.BlockSpec(memory_space=pltpu.VMEM)


def params(mib, steps=1):
    return pltpu.CompilerParams(
        vmem_limit_bytes=mib * MIB, dimension_semantics=("arbitrary",) * steps
    )


def rms_scale(values):
    return lax.rsqrt(jnp.mean(values * values, axis=-1, keepdims=True) + EPS)


def contract_rows(left, right):
    return lax.dot_general(
        left, right, (((0,), (0,)), ((), ())), preferred_element_type=jnp.float32
    )


def contract_cols(left, right):
    return lax.dot_general(
        left, right, (((1,), (1,)), ((), ())), preferred_element_type=jnp.float32
    )


def gated_unit(gate, upward):
    return jax.nn.gelu(gate, approximate=True) * upward


def norm_back(inputs, scale_rows, gain, normed_grad):
    gain_grad = jnp.sum(normed_grad * inputs * scale_rows, axis=0)
    weighted = normed_grad * gain
    cubed = scale_rows * scale_rows * scale_rows
    input_grad = scale_rows * weighted - inputs * cubed * jnp.mean(
        weighted * inputs, axis=1, keepdims=True
    )
    return (gain_grad, input_grad)


def count_edges(magnitude, edge_list):
    result = jnp.zeros(magnitude.shape, jnp.int32)
    for border in edge_list:
        result = result + (magnitude >= border).astype(jnp.int32)
    return result


def box_cell(offset):
    half = jnp.abs(offset) >> 1
    cell = jnp.where(half < 64, (half >> 2) + 6, (half >> 5) + 20)
    cell = jnp.where(half < 8, half, cell)
    return cell + jnp.where(offset > 0, 64, 0)


def cell_bucket(cell):
    low = cell & 63
    half = jnp.where(low < 22, (low - 6) << 2, (low - 20) << 5)
    half = jnp.where(low < 8, low, half)
    return count_edges(half * 2, BOX_EDGES) + jnp.where(cell >= 64, 16, 0)


def lookup(table, index):
    return jnp.take_along_axis(table, index, axis=1, mode="promise_in_bounds")


def bias_kernel(blk_ref, query_ref, key_ref, table_ref, bias_ref):
    heads, rows, width = bias_ref.shape
    chunk = 32
    step = pl.program_id(0)
    ahead = (step - blk_ref[0]) * width
    lane = lax.broadcasted_iota(jnp.int32, (8, LANES), 1)
    buckets = cell_bucket(lane)
    table = table_ref[...]
    hor = lookup(table, buckets + 32)
    ver = lookup(table, buckets + 64)
    far_bucket = jnp.where(ahead > 0, 31, 15) + jnp.zeros((8, LANES), jnp.int32)
    far = lookup(table, far_bucket)
    near = jnp.abs(ahead) <= width

    def piece(at, column, with_near):
        here = pl.ds(pl.multiple_of(at * chunk, chunk), chunk)
        there = slice(column * LANES, (column + 1) * LANES)
        meta = query_ref[here, :]
        keys = key_ref[:, there]
        hor_cell = box_cell(keys[1:2, :] - meta[:, 1:2])
        ver_cell = box_cell(keys[2:3, :] - meta[:, 2:3])
        same = keys[0:1, :] == meta[:, 0:1]
        if with_near:
            first = at * chunk
            row = lax.broadcasted_iota(jnp.int32, (chunk, LANES), 0) + first
            col = lax.broadcasted_iota(jnp.int32, (chunk, LANES), 1) + (ahead + column * LANES)
            offset = col - row
            seq = count_edges(jnp.abs(offset), SEQ_EDGES) + jnp.where(offset > 0, 16, 0)
        for head in range(heads):
            spread = lambda values: jnp.broadcast_to(values[head : head + 1, :], (chunk, LANES))
            if with_near:
                total = lookup(spread(hor), hor_cell) + lookup(spread(table), seq)
            else:
                total = lookup(spread(hor + far), hor_cell)
            total = total + lookup(spread(ver), ver_cell)
            bias_ref[head, here, there] = jnp.where(same, total, -1e30)

    def all_pieces(with_near):
        def body(at, carry):
            for column in range(width // LANES):
                piece(at, column, with_near)
            return carry

        lax.fori_loop(0, rows // chunk, body, 0)

    @pl.when(near)
    def _():
        all_pieces(True)

    @pl.when(jnp.logical_not(near))
    def _():
        all_pieces(False)


def bias_scores(blk, query_meta, key_meta, table, heads):
    rows = query_meta.shape[0]
    length = key_meta.shape[1]
    return pl.pallas_call(
        bias_kernel,
        grid=(length // rows,),
        in_specs=[
            pl.BlockSpec(memory_space=pltpu.SMEM),
            pl.BlockSpec((rows, 8), lambda s: (0, 0)),
            pl.BlockSpec((8, rows), lambda s: (0, s)),
            pl.BlockSpec((8, LANES), lambda s: (0, 0)),
        ],
        out_specs=pl.BlockSpec((heads, rows, rows), lambda s: (0, 0, s)),
        out_shape=jax.ShapeDtypeStruct((heads, rows, length), F32),
        compiler_params=params(32),
        name="bias_scores",
    )(blk, query_meta, key_meta, table)


def attend_kernel(query_ref, pair_ref, bias_ref, probs_ref, exact_ref, low_ref):
    blocks, width, _ = pair_ref.shape
    heads = bias_ref.shape[0]
    features = heads * HEAD_DIM
    outs = []
    for head in range(heads):
        cols = slice(head * HEAD_DIM, (head + 1) * HEAD_DIM)
        vcols = slice(features + head * HEAD_DIM, features + (head + 1) * HEAD_DIM)
        query = query_ref[:, cols]
        scores = []
        for block in range(blocks):
            span = slice(block * width, (block + 1) * width)
            scores.append(contract_cols(query, pair_ref[block, :, cols]) + bias_ref[head, :, span])
        top = functools.reduce(jnp.maximum, scores)
        top = jnp.max(top, axis=1, keepdims=True)
        weights = [jnp.exp(score - top) for score in scores]
        total = functools.reduce(jnp.add, weights)
        inverse = 1.0 / jnp.sum(total, axis=1, keepdims=True)
        result = None
        for block in range(blocks):
            span = slice(block * width, (block + 1) * width)
            low = (weights[block] * inverse).astype(BF16)
            probs_ref[head, :, span] = low
            part = jnp.dot(low, pair_ref[block, :, vcols], preferred_element_type=F32)
            result = part if result is None else result + part
        outs.append(result)
    exact = jnp.concatenate(outs, axis=1)
    exact_ref[...] = exact
    low_ref[...] = exact.astype(BF16)


def attend(queries, pairs, bias):
    heads, rows, length = bias.shape
    blocks, width, both = pairs.shape
    tile = 128
    return pl.pallas_call(
        attend_kernel,
        grid=(rows // tile,),
        in_specs=[
            pl.BlockSpec((tile, both // 2), lambda s: (s, 0)),
            pl.BlockSpec((blocks, width, both), lambda s: (0, 0, 0)),
            pl.BlockSpec((heads, tile, length), lambda s: (0, s, 0)),
        ],
        out_specs=[
            pl.BlockSpec((heads, tile, length), lambda s: (0, s, 0)),
            pl.BlockSpec((tile, both // 2), lambda s: (s, 0)),
            pl.BlockSpec((tile, both // 2), lambda s: (s, 0)),
        ],
        out_shape=[
            jax.ShapeDtypeStruct((heads, rows, length), BF16),
            jax.ShapeDtypeStruct((rows, both // 2), F32),
            jax.ShapeDtypeStruct((rows, both // 2), BF16),
        ],
        compiler_params=params(56),
        name="attend",
    )(queries, pairs, bias)


def attend_back_kernel(
    query_ref, grad_ref, exact_ref, pair_ref, probs_ref, score_ref, pair_grad_ref, query_grad_ref, sums
):
    heads, rows, width = probs_ref.shape
    features = heads * HEAD_DIM
    step = pl.program_id(0)

    @pl.when(step == 0)
    def _():
        sums[...] = jnp.zeros_like(sums)

    for head in range(heads):
        cols = slice(head * HEAD_DIM, (head + 1) * HEAD_DIM)
        vcols = slice(features + head * HEAD_DIM, features + (head + 1) * HEAD_DIM)
        grad = grad_ref[:, cols]
        delta = jnp.sum(grad.astype(F32) * exact_ref[:, cols], axis=1, keepdims=True)
        probs = probs_ref[head]
        prob_grad = contract_cols(grad, pair_ref[0, :, vcols])
        score_grad = (probs.astype(F32) * (prob_grad - delta)).astype(BF16)
        score_ref[head] = score_grad
        sums[:, cols] += jnp.dot(score_grad, pair_ref[0, :, cols], preferred_element_type=F32)
        pair_grad_ref[0, cols, :] = contract_rows(query_ref[:, cols], score_grad).astype(BF16)
        pair_grad_ref[0, vcols, :] = contract_rows(grad, probs).astype(BF16)

    @pl.when(step == pl.num_programs(0) - 1)
    def _():
        query_grad_ref[...] = (sums[...] * HEAD_DIM ** (-0.5)).astype(BF16)


def attend_back(queries, grads, exact, pairs, probs):
    heads, rows, length = probs.shape
    blocks, width, both = pairs.shape
    whole = pl.BlockSpec((rows, both // 2), lambda s: (0, 0))
    return pl.pallas_call(
        attend_back_kernel,
        grid=(blocks,),
        in_specs=[
            whole,
            whole,
            whole,
            pl.BlockSpec((1, width, both), lambda s: (s, 0, 0)),
            pl.BlockSpec((heads, rows, width), lambda s: (0, 0, s)),
        ],
        out_specs=[
            pl.BlockSpec((heads, rows, width), lambda s: (0, 0, s)),
            pl.BlockSpec((1, both, width), lambda s: (s, 0, 0)),
            whole,
        ],
        out_shape=[
            jax.ShapeDtypeStruct((heads, rows, length), BF16),
            jax.ShapeDtypeStruct((blocks, both, width), BF16),
            jax.ShapeDtypeStruct((rows, both // 2), BF16),
        ],
        scratch_shapes=[pltpu.VMEM((rows, both // 2), F32)],
        compiler_params=params(32),
        name="attend_back",
    )(queries, grads, exact, pairs, probs)


BOX_SPAN = 1024
SEQ_SPAN = 512
TILE = 512


def threshold_row(edge_list, far, lane):
    borders = [-far] + [1 - edge for edge in reversed(edge_list)] + [1] + list(edge_list)
    result = jnp.zeros(lane.shape, jnp.int32)
    for at, border in enumerate(borders):
        result = jnp.where(lane == at, border, result)
    return result


def table_grad_kernel(query_ref, key_ref, score_ref, out_ref):
    heads, rows, length = score_ref.shape
    step = pl.program_id(0)
    axis = step // 2
    row = jnp.where(axis == 0, 1, jnp.where(axis == 1, 2, 3))
    offset = jnp.where(axis == 2, 0, (step % 2) * TILE)
    lane = lax.broadcasted_iota(jnp.int32, (rows, LANES), 1)
    box = threshold_row(BOX_EDGES, 4096, lane[:1])
    seq = threshold_row(SEQ_EDGES, 4096, lane[:1])
    mine = jnp.where(
        axis == 0, query_ref[:, 1:2], jnp.where(axis == 1, query_ref[:, 2:3], query_ref[:, 3:4])
    )
    thresholds = jnp.where(axis == 2, seq, box)
    index = jnp.clip(mine + thresholds, 0, BOX_SPAN - 1)
    index = jnp.where(axis == 2, jnp.minimum(index, SEQ_SPAN - 1), index)
    column = index & (LANES - 1)
    block = (index - offset) >> 7
    level = lax.broadcasted_iota(jnp.int32, (TILE, 1), 0) + offset
    reached = (key_ref[pl.ds(row, 1), :] >= level).astype(F32).astype(BF16)

    @pl.when((step == 0) | (step == 2) | (step == 4))
    def _():
        out_ref[...] = jnp.zeros_like(out_ref)

    for head in range(heads):
        sums = contract_cols(score_ref[head], reached)
        picked = jnp.zeros((rows, LANES), F32)
        for at in range(TILE // LANES):
            found = lookup(sums[:, at * LANES : (at + 1) * LANES], column)
            picked = picked + jnp.where(block == at, found, 0.0)
        out_ref[0, head : head + 1, :] += jnp.sum(picked, axis=0, keepdims=True)


def table_grad_sums(query_meta, key_meta, score_grad):
    heads, rows, length = score_grad.shape
    return pl.pallas_call(
        table_grad_kernel,
        grid=(5,),
        in_specs=[
            pl.BlockSpec((rows, 8), lambda s: (0, 0)),
            pl.BlockSpec((8, length), lambda s: (0, 0)),
            pl.BlockSpec((heads, rows, length), lambda s: (0, 0, 0)),
        ],
        out_specs=pl.BlockSpec((1, 8, LANES), lambda s: (s // 2, 0, 0)),
        out_shape=jax.ShapeDtypeStruct((3, 8, LANES), F32),
        compiler_params=params(56),
        name="table_grad",
    )(query_meta, key_meta, score_grad)


def table_from_sums(sums, heads):
    sums = jnp.concatenate([sums[2:], sums[:2]], axis=0)[:, :heads, :32]
    after = jnp.concatenate([sums[:, :, 1:], jnp.zeros_like(sums[:, :, :1])], axis=2)
    part = sums - after
    part = jnp.concatenate([part[:, :, :16][:, :, ::-1], part[:, :, 16:]], axis=2)
    return jnp.transpose(part, (0, 2, 1)).reshape(96, heads)


def spread_gather(values, axis_name, count):
    return lax.all_to_all(
        jnp.broadcast_to(values[None], (count,) + values.shape), axis_name, 0, 0, tiled=False
    )


def swap(values, axis_name, count, bit):
    return lax.ppermute(values, axis_name, [(at, at ^ bit) for at in range(count)])


def sum_mp(values):
    half = values.shape[0] // 2
    core = lax.axis_index("mp") % 2
    mine = lax.dynamic_slice_in_dim(values, core * half, half, 0)
    other = lax.dynamic_slice_in_dim(values, (1 - core) * half, half, 0)
    got = swap(other.astype(BF16), "mp", 4, 1)
    part = (mine.astype(F32) + got.astype(F32)).astype(BF16)
    got = swap(part, "mp", 4, 2)
    total = (part.astype(F32) + got.astype(F32)).astype(BF16)
    got = swap(total, "mp", 4, 1)
    first = jnp.where(core == 0, total, got)
    second = jnp.where(core == 0, got, total)
    return jnp.concatenate([first, second], axis=0)


def sum_dp(values):
    total = values.astype(F32)
    low = values.astype(BF16)
    for hop in (1, 2, 3):
        got = lax.ppermute(low, "dp", [(at, (at + hop) % 4) for at in range(4)])
        total = total + got.astype(F32)
    return total


def shards(
    tokens,
    cotangent,
    seg_ids,
    token_boxes,
    norm1_gain,
    w_query,
    w_key,
    w_value,
    w_out_t,
    bias_table,
    norm2_gain,
    w_gate,
    w_up,
    w_down_t,
):
    rows, model = tokens.shape
    blocks = 8
    length = rows * blocks
    features = w_query.shape[1]
    units = w_gate.shape[1]
    heads = features // HEAD_DIM
    blk = lax.axis_index("blk")

    centre_x = token_boxes[0] + token_boxes[2]
    centre_y = token_boxes[1] + token_boxes[3]
    pad = rows - bias_table.size
    small = jnp.stack(
        [
            seg_ids.astype(BF16),
            (centre_x >> 8).astype(BF16),
            (centre_x & 255).astype(BF16),
            (centre_y >> 8).astype(BF16),
            (centre_y & 255).astype(BF16),
            jnp.concatenate([norm1_gain, norm2_gain]),
            jnp.concatenate([bias_table.reshape(-1), jnp.zeros((pad,), BF16)]),
        ]
    )
    small = jnp.concatenate([small, jnp.zeros((9, rows), BF16)], axis=0)
    small_all = spread_gather(small, "blk", blocks)
    gain_one = small_all[:, 5, :LANES].reshape(1, model).astype(F32)
    gain_two = small_all[:, 5, LANES:].reshape(1, model).astype(F32)
    table = small_all[:, 6, : bias_table.size].reshape(96, heads).astype(F32)
    table = jnp.pad(table.T, ((0, 8 - heads), (0, LANES - 96)))
    places = jnp.transpose(small_all[:, :5, :], (1, 0, 2)).reshape(5, length).astype(jnp.int32)
    key_place = jnp.clip(
        jnp.arange(length, dtype=jnp.int32) - blk * rows + SEQ_SPAN // 4, 0, SEQ_SPAN - 1
    )
    zero_row = jnp.zeros((length,), jnp.int32)
    key_meta = jnp.stack(
        [
            places[0],
            places[1] * 256 + places[2],
            places[3] * 256 + places[4],
            key_place,
            zero_row,
            zero_row,
            zero_row,
            zero_row,
        ]
    )
    own_place = jnp.arange(rows, dtype=jnp.int32) + SEQ_SPAN // 4
    query_meta = jnp.stack([seg_ids, centre_x, centre_y, own_place], axis=1)
    query_meta = jnp.pad(query_meta, ((0, 0), (0, 4)))

    late = jnp.concatenate([w_out_t, w_gate, w_up, w_down_t], axis=1)
    late_all = lax.all_gather(late, "blk", axis=0, tiled=True)
    early = jnp.concatenate([w_query, w_key, w_value], axis=1)
    early_all = spread_gather(early, "blk", blocks).reshape(model, 3 * features)

    bias = bias_scores(blk.reshape(1), query_meta, key_meta, table, heads)

    inputs = tokens.astype(F32)
    scale_one = rms_scale(inputs)
    normed_one = (inputs * scale_one * gain_one).astype(BF16)
    projected = jnp.dot(normed_one, early_all, preferred_element_type=F32).astype(BF16)
    queries = projected[:, :features] * jnp.asarray(HEAD_DIM ** (-0.5), BF16)
    pairs = spread_gather(projected[:, features:], "blk", blocks)
    probs, attn_exact, attended = attend(queries, pairs, bias)

    out_w = late_all[:, :features]
    gate_w = late_all[:, features : features + units]
    upward_w = late_all[:, features + units : features + 2 * units]
    down_w = late_all[:, features + 2 * units :]
    branch = sum_mp(contract_cols(attended, out_w).astype(BF16)).astype(F32)
    middle = inputs + branch
    scale_two = rms_scale(middle)
    normed_two = (middle * scale_two * gain_two).astype(BF16)
    gate = jnp.dot(normed_two, gate_w, preferred_element_type=F32)
    upward = jnp.dot(normed_two, upward_w, preferred_element_type=F32)
    gated_vals, pull_back = jax.vjp(gated_unit, gate, upward)
    hidden = gated_vals.astype(BF16)
    hidden_grad = jnp.dot(cotangent, down_w, preferred_element_type=F32)
    gate_grad, upward_grad = pull_back(hidden_grad)
    gate_low = gate_grad.astype(BF16)
    upward_low = upward_grad.astype(BF16)
    normed_two_grad = sum_mp(
        (contract_cols(gate_low, gate_w) + contract_cols(upward_low, upward_w)).astype(BF16)
    ).astype(F32)
    ffn_out = sum_mp(contract_cols(hidden, down_w).astype(BF16)).astype(F32)
    mixed = (middle + ffn_out).astype(BF16)
    ffn_grads = jnp.concatenate(
        [
            contract_rows(normed_two, gate_low).astype(BF16),
            contract_rows(normed_two, upward_low).astype(BF16),
            contract_rows(cotangent, hidden).astype(BF16),
        ],
        axis=1,
    )
    ffn_part = lax.psum_scatter(ffn_grads, "blk", scatter_dimension=0, tiled=True)
    ffn_final = lax.psum(ffn_part, "dp").astype(F32)

    gain_two_grad, middle_part = norm_back(middle, scale_two, gain_two, normed_two_grad)
    middle_grad = cotangent.astype(F32) + middle_part
    branch_low = middle_grad.astype(BF16)
    out_grad_w = contract_rows(branch_low, attended).astype(BF16)
    attended_grad = jnp.dot(branch_low, out_w, preferred_element_type=F32).astype(BF16)
    score_grad, pair_grad, query_low = attend_back(
        queries, attended_grad, attn_exact, pairs, probs
    )
    sums = table_grad_sums(query_meta, key_meta, score_grad)
    table_grad = table_from_sums(sums, heads)
    pair_parts = lax.all_to_all(pair_grad, "blk", 0, 0, tiled=False)
    pair_low = jnp.sum(pair_parts.astype(F32), axis=0).astype(BF16)

    pair_t = pair_low.T
    triple = jnp.concatenate([query_low, pair_t], axis=1)
    triple_grad_w = contract_rows(normed_one, triple).astype(BF16)
    normed_partial = contract_cols(triple, early_all)
    normed_one_grad = sum_mp(normed_partial.astype(BF16)).astype(F32)
    gain_one_part = jnp.sum(normed_partial * inputs * scale_one, axis=0)
    _, input_part = norm_back(inputs, scale_one, gain_one, normed_one_grad)
    tokens_grad = middle_grad + input_part

    table_cols = jnp.pad(table_grad.reshape(blocks, 12, heads), ((0, 0), (0, LANES - 12), (0, 0)))
    extra = jnp.concatenate(
        [gain_one_part[:, None], gain_two_grad[:, None], table_cols.reshape(model, heads)], axis=1
    )
    extra = jnp.pad(extra, ((0, 0), (0, LANES - extra.shape[1]))).astype(BF16)
    bundle = jnp.concatenate([triple_grad_w, out_grad_w, extra], axis=1)
    bundle = lax.all_to_all(bundle.reshape(blocks, LANES, -1), "blk", 0, 0, tiled=False)
    bundle = jnp.sum(bundle.astype(F32), axis=0).astype(BF16)
    final = sum_dp(bundle)
    small_final = final[:, 4 * features :]
    gain_one_low = small_final[:, 0].reshape(1, LANES)
    gain_one_low = jnp.broadcast_to(gain_one_low, (16, LANES))
    gain_one_sum = gain_one_low.astype(F32)
    for bit in (1, 2):
        gain_one_sum = gain_one_sum + swap(gain_one_sum.astype(BF16), "mp", 4, bit).astype(F32)
    return (
        mixed,
        tokens_grad,
        gain_one_sum[0],
        final[:, :features],
        final[:, features : 2 * features],
        final[:, 2 * features : 3 * features],
        final[:, 3 * features : 4 * features],
        small_final[:12, 2 : 2 + heads],
        small_final[:, 1],
        ffn_final[:, :units],
        ffn_final[:, units : 2 * units],
        ffn_final[:, 2 * units :],
    )


def solution(mesh):
    rows = P(("dp", "blk"), None)
    weight = P("blk", "mp")
    in_specs = (
        rows,
        rows,
        P(("dp", "blk")),
        P(None, ("dp", "blk")),
        P("blk"),
        weight,
        weight,
        weight,
        weight,
        weight,
        P("blk"),
        weight,
        weight,
        weight,
    )
    out_specs = (
        rows,
        rows,
        P("blk"),
        weight,
        weight,
        weight,
        weight,
        weight,
        P("blk"),
        weight,
        weight,
        weight,
    )
    return jax.shard_map(shards, mesh=mesh, in_specs=in_specs, out_specs=out_specs, check_vma=False)
```

time: 1290 us -> 369 us (0.29)
  waiting for transfers between devices: 574 us -> 151 us
  matrix products: 307 us -> 14.9 us
  blocking collectives: 228 us -> 33.4 us
  Pallas kernels: 0 us -> 64.6 us
  local copies, waits for them, and re-layouts: 84.6 us -> 30.8 us
  other arithmetic: 68.6 us -> 19.8 us
  starting transfers between devices: 0.95 us -> 38.4 us
    dot_general x183 -> x5, matrix products: 287 us -> 6.49 us  [the longest x1 2.16 us: shards(): jnp.dot(branch_low, out_w, preferred_element_type=F32).astype(BF16)]
    reduce_scatter x6 -> x0, waiting for transfers between devices: 214 us -> none  [the longest x1 39 us: shards(): lax.psum_scatter(value_grad_w.astype(jnp.bfloat16), 'blk', scatter_dimens...]
    all_gather x8 -> x0, blocking collectives: 198 us -> none  [the longest x1 29.7 us: shards(): lax.all_gather(w_value, 'blk', axis=0, tiled=True)]
    all_gather x5 -> x1, waiting for transfers between devices: 119 us -> 0.01 us  [shards(): late_all = lax.all_gather(late, 'blk', axis=0, tiled=True)]
    unnamed x21 -> x4, waiting for transfers between devices: 116 us -> 0.05 us
    psum x4 -> x1, waiting for transfers between devices: 126 us -> 35.3 us  [shards(): ffn_final = lax.psum(ffn_part, 'dp').astype(F32)]
    all_to_all x0 -> x4, waiting for transfers between devices: none -> 81.8 us  [the longest x3 49 us: spread_gather(): lax.all_to_all(jnp.broadcast_to(values[None], (count,) + values.shape), a...]
    pallas_call x0 -> x4, Pallas kernels: none -> 64.6 us  [the longest x1 24.3 us: bias_scores(): pl.pallas_call(bias_kernel, grid=(length // rows,), in_specs=[pl.BlockSpe...]
  transfers between devices with their start and end apart: 18 -> 24, of which waited for: 16 -> 15; matrix products, arithmetic and copies ran while one was open for 11% -> 13% of each run, Pallas kernels for 0% -> 18%
where the time goes in v1:
time: 369 us; the launch traced here: 368 us
  waiting for transfers between devices  151 us (41%)
  Pallas kernels  64.6 us (18%)
  starting transfers between devices  38.4 us (10%)
  blocking collectives  33.4 us (9%)
  local copies, waits for them, and re-layouts  30.8 us (8%)
  other arithmetic  19.8 us (5%)
  matrix products  14.9 us (4%)
  between operations  14.5 us (4%)
    all_to_all x3, waiting for transfers between devices, spread_gather(): lax.all_to_all(jnp.broadcast_to(values[None], (count,) + values.shape), a...  49 us
    psum x1, waiting for transfers between devices, shards(): ffn_final = lax.psum(ffn_part, 'dp').astype(F32)  35.3 us
    all_to_all x1, blocking collectives, shards(): lax.all_to_all(bundle.reshape(blocks, LANES, -1), 'blk', 0, 0, tiled=False)  33.4 us
    all_to_all x1, waiting for transfers between devices, shards(): pair_parts = lax.all_to_all(pair_grad, 'blk', 0, 0, tiled=False)  32.7 us
    pallas_call x1, Pallas kernels, bias_scores(): pl.pallas_call(bias_kernel, grid=(length // rows,), in_specs=[pl.BlockSpe...  24.3 us
    ppermute x14, waiting for transfers between devices, swap(): lax.ppermute(values, axis_name, [(at, at ^ bit) for at in range(count)])  22.5 us
    unnamed x50, local copies, waits for them, and re-layouts  20.8 us
    pallas_call x1, Pallas kernels, table_grad_sums(): pl.pallas_call(table_grad_kernel, grid=(5,), in_specs=[pl.BlockSpec((rows...  17.7 us
  transfers between devices with their start and end apart: 24, of which 15 were waited for; matrix products, arithmetic and copies ran while one was open for 13% of the time, Pallas kernels for 18%

profile of v1, /device:TPU:0, one launch (start us, length us, event | category | flops | bytes accessed | tf_op | source)
XLA Modules:
  0.0 367.7 jit_solution(17803020274578175723)
XLA Ops:
  14.1 6.4 %all-to-all-start = ((bf16[8,16,256]{2,1,0:T(8,128)(2,1)}), bf16[8,16,256]{2,1,0:T(8,128)(2,1)S(1)}, u32[]{:S(2)}, u32[]{:S(2)}) async-start(bf16[8,16,256]{2,1,0:T(8,128)(2,1)} %broadcast_in_dim.21), calls=%async_computation | async-start | bytes 131072 | tf_op jit(solution)/shard_map/all_to_all | solution.py:344
  21.5 5.5 %all-to-all-done = bf16[8,16,256]{2,1,0:T(8,128)(2,1)S(1)} async-done(((bf16[8,16,256]{2,1,0:T(8,128)(2,1)}), bf16[8,16,256]{2,1,0:T(8,128)(2,1)S(1)}, u32[]{:S(2)}, u32[]{:S(2)}) %all-to-all-start) | async-done | bytes 65568 | tf_op jit(solution)/shard_map/all_to_all | solution.py:344
  28.3 3.6 all-to-all-start.1
  32.6 28.2 %all-to-all-done.1 = bf16[8,128,768]{2,1,0:T(8,128)(2,1)S(1)} async-done(((bf16[8,128,768]{2,1,0:T(8,128)(2,1)}), bf16[8,128,768]{2,1,0:T(8,128)(2,1)S(1)}, u32[]{:S(2)}, u32[]{:S(2)}) %all-to-all-start.1) | async-done | bytes 1572896 | tf_op jit(solution)/shard_map/all_to_all | solution.py:344
  63.0 3.7 %all-to-all-start.2 = ((bf16[8,256,512]{2,1,0:T(8,128)(2,1)}), bf16[8,256,512]{2,1,0:T(8,128)(2,1)S(1)}, u32[]{:S(2)}, u32[]{:S(2)}) async-start(bf16[8,256,512]{2,1,0:T(8,128)(2,1)} %broadcast_in_dim.46), calls=%async_computation.2 | async-start | bytes 4194304 | tf_op jit(solution)/shard_map/all_to_all | solution.py:344
  67.5 24.3 %bias_scores.1.bias_ref = f32[4,256,2048]{2,1,0:T(8,128)S(1)} custom-call(s32[1]{0:T(128)} %bitcast.2.blk_ref, s32[256,8]{1,0:T(8,128)S(1)} %pad.22.query_ref, s32[8,2048]{1,0:T(8,128)S(1)} %stack.37.key_ref, f32[8,128]{1,0:T(8,128)S(1)} %pad_convert_fusion.table_ref), custom_call_target="tpu_custom_call" | custom-call | tf_op jit(solution)/shard_map/bias_scores/pallas_call | solution.py:139
  91.7 3.3 copy-done
  95.7 15.3 %all-to-all-done.2.pair_ref = bf16[8,256,512]{2,1,0:T(8,128)(2,1)S(1)} async-done(((bf16[8,256,512]{2,1,0:T(8,128)(2,1)}), bf16[8,256,512]{2,1,0:T(8,128)(2,1)S(1)}, u32[]{:S(2)}, u32[]{:S(2)}) %all-to-all-start.2) | async-done | bytes 2097184 | tf_op jit(solution)/shard_map/all_to_all | solution.py:344
  112.3 10.5 %attend.1 = (bf16[4,256,2048]{2,1,0:T(8,128)(2,1)}, f32[256,256]{1,0:T(8,128)}, bf16[256,256]{1,0:T(8,128)(2,1)}) custom-call(bf16[256,256]{1,0:T(8,128)(2,1)} %slice_multiply_fusion.query_ref, bf16[8,256,512]{2,1,0:T(8,128)(2,1)} %copy-done.1, f32[4,256,2048]{2,1,0:T(8,128)} %copy-done), custom_call_target="tpu_custom_call" | custom-call | tf_op jit(solution)/shard_map/attend/pallas_call | solution.py:190
  126.0 4.3 %collective-permute-start.1 = (bf16[128,1024]{1,0:T(8,128)(2,1)S(1)}, bf16[128,1024]{1,0:T(8,128)(2,1)S(1)}, u32[]{:S(2)}, u32[]{:S(2)}) collective-permute-start(bf16[128,1024]{1,0:T(8,128)(2,1)S(1)} %add_convert_fusion.8), channel_id=1, source_target_pairs={{0,2},{1,3},{2,0},{3,1},{4,6},{5,7},{6,4},{7,5},{8,10},{9,11},{10,... | collective-permute-start | bytes 786440 | tf_op jit(solution)/shard_map/ppermute | solution.py:350
  130.3 6.6 %collective-permute-done.1 = bf16[128,1024]{1,0:T(8,128)(2,1)S(1)} collective-permute-done((bf16[128,1024]{1,0:T(8,128)(2,1)S(1)}, bf16[128,1024]{1,0:T(8,128)(2,1)S(1)}, u32[]{:S(2)}, u32[]{:S(2)}) %collective-permute-start.1) | collective-permute-done | bytes 262176 | tf_op jit(solution)/shard_map/ppermute | solution.py:350
  145.4 3.3 collective-permute-start.7
  149.7 6.4 %collective-permute-done.7 = bf16[128,1024]{1,0:T(8,128)(2,1)S(1)} collective-permute-done((bf16[128,1024]{1,0:T(8,128)(2,1)S(1)}, bf16[128,1024]{1,0:T(8,128)(2,1)S(1)}, u32[]{:S(2)}, u32[]{:S(2)}) %collective-permute-start.7) | collective-permute-done | bytes 262176 | tf_op jit(solution)/shard_map/ppermute | solution.py:350
  158.6 6.4 %copy.56 = bf16[1024,2112]{1,0:T(8,128)(2,1)} copy(bf16[1024,2112]{0,1:T(8,128)(2,1)} %pad_maximum_fusion) | data formatting | bytes 8650752
  170.3 12.1 %attend_back.1 = (bf16[4,256,2048]{2,1,0:T(8,128)(2,1)S(1)}, bf16[8,512,256]{2,1,0:T(8,128)(2,1)}, bf16[256,256]{1,0:T(8,128)(2,1)S(1)}) custom-call(bf16[256,256]{1,0:T(8,128)(2,1)S(1)} %copy-done.6, bf16[256,256]{1,0:T(8,128)(2,1)S(1)} %convolution_convert_fusion.8.grad_ref, f32[256,256]{1,0:T(8,128)S(1)} %copy-done.8, bf16[8,256,512]{2,1,0:T(8,128)(2,1)S(1)} %copy-done.2, ...), custom_call_target="tpu_custom_call" | custom-call | tf_op jit(solution)/shard_map/attend_back/pallas_call | solution.py:246
  184.5 4.3 %all-to-all-start.3 = ((bf16[8,512,256]{2,1,0:T(8,128)(2,1)}), bf16[8,512,256]{2,1,0:T(8,128)(2,1)}, u32[]{:S(2)}, u32[]{:S(2)}) async-start(bf16[8,512,256]{2,1,0:T(8,128)(2,1)} %get-tuple-element.22), calls=%async_computation.3 | async-start | bytes 4194304 | tf_op jit(solution)/shard_map/all_to_all | solution.py:499
  188.9 17.7 %table_grad.1 = f32[3,8,128]{2,1,0:T(8,128)} custom-call(s32[256,8]{1,0:T(8,128)} %copy-done.5, s32[8,2048]{1,0:T(8,128)} %copy-done.7, bf16[4,256,2048]{2,1,0:T(8,128)(2,1)} %copy-done.3), custom_call_target="tpu_custom_call" | custom-call | tf_op jit(solution)/shard_map/table_grad/pallas_call | solution.py:320
  209.0 32.7 %all-to-all-done.3 = bf16[8,512,256]{2,1,0:T(8,128)(2,1)} async-done(((bf16[8,512,256]{2,1,0:T(8,128)(2,1)}), bf16[8,512,256]{2,1,0:T(8,128)(2,1)}, u32[]{:S(2)}, u32[]{:S(2)}) %all-to-all-start.3) | async-done | bytes 2097184 | tf_op jit(solution)/shard_map/all_to_all | solution.py:499
  248.8 3.4 collective-permute-start.10
  253.4 5.3 %collective-permute-done.10 = bf16[128,1024]{1,0:T(8,128)(2,1)S(1)} collective-permute-done((bf16[128,1024]{1,0:T(8,128)(2,1)S(1)}, bf16[128,1024]{1,0:T(8,128)(2,1)S(1)}, u32[]{:S(2)}, u32[]{:S(2)}) %collective-permute-start.10) | collective-permute-done | bytes 262176 | tf_op jit(solution)/shard_map/ppermute | solution.py:350
  261.6 33.4 %all_to_all.25 = bf16[8,128,1152]{1,2,0:T(8,128)(2,1)} all-to-all(bf16[8,128,1152]{1,2,0:T(8,128)(2,1)S(1)} %copy_bitcast_fusion), channel_id=1, replica_groups=mesh['dp'=4,'blk'=8,'mp'=4] {'blk'}, dimensions={0} | all-to-all | bytes 4718592 | tf_op jit(solution)/shard_map/all_to_all | solution.py:517
  302.3 7.9 %collective-permute-done.14 = bf16[128,1152]{0,1:T(8,128)(2,1)S(1)} collective-permute-done((bf16[128,1152]{0,1:T(8,128)(2,1)S(1)}, bf16[128,1152]{0,1:T(8,128)(2,1)S(1)}, u32[]{:S(2)}, u32[]{:S(2)}) %collective-permute-start.14) | collective-permute-done | bytes 294944 | tf_op jit(solution)/shard_map/ppermute | solution.py:372
  310.4 3.5 collective-permute-done.12
  323.7 35.3 %all-reduce.8.cloned.1.call-done = bf16[128,2112]{0,1:T(8,128)(2,1)} async-done(((bf16[128,2112]{0,1:T(8,128)(2,1)}), bf16[128,2112]{0,1:T(8,128)(2,1)}) %all-reduce.8.cloned.1.call-update) | async-done | bytes 540688 | tf_op jit(solution)/shard_map/psum | solution.py:487
  (181 shorter events, 69.6 us)
Async XLA Ops:
  7.2 115.6 %all-gather.2.cloned.1.call-start = ((), (), s32[]{:S(2)}) async-start(), calls=%async_computation.6 | async-start | bytes 5455872 | tf_op jit(solution)/shard_map/all_gather | solution.py:443
  14.1 12.9 %all-to-all-start = ((bf16[8,16,256]{2,1,0:T(8,128)(2,1)}), bf16[8,16,256]{2,1,0:T(8,128)(2,1)S(1)}, u32[]{:S(2)}, u32[]{:S(2)}) async-start(bf16[8,16,256]{2,1,0:T(8,128)(2,1)} %broadcast_in_dim.21), calls=%async_computation | async-start | bytes 131072 | tf_op jit(solution)/shard_map/all_to_all | solution.py:344
  28.3 32.6 %all-to-all-start.1 = ((bf16[8,128,768]{2,1,0:T(8,128)(2,1)}), bf16[8,128,768]{2,1,0:T(8,128)(2,1)S(1)}, u32[]{:S(2)}, u32[]{:S(2)}) async-start(bf16[8,128,768]{2,1,0:T(8,128)(2,1)} %broadcast_in_dim.22), calls=%async_computation.1 | async-start | bytes 3145728 | tf_op jit(solution)/shard_map/all_to_all | solution.py:344
  63.0 48.0 %all-to-all-start.2 = ((bf16[8,256,512]{2,1,0:T(8,128)(2,1)}), bf16[8,256,512]{2,1,0:T(8,128)(2,1)S(1)}, u32[]{:S(2)}, u32[]{:S(2)}) async-start(bf16[8,256,512]{2,1,0:T(8,128)(2,1)} %broadcast_in_dim.46), calls=%async_computation.2 | async-start | bytes 4194304 | tf_op jit(solution)/shard_map/all_to_all | solution.py:344
  66.7 247.9 %reduce-scatter.4.cloned.1.call-start = ((), (), s32[]{:S(2)}) async-start(), calls=%async_computation.8 | async-start | bytes 5013504
  124.3 1.6 collective-permute-start
  126.0 10.9 %collective-permute-start.1 = (bf16[128,1024]{1,0:T(8,128)(2,1)S(1)}, bf16[128,1024]{1,0:T(8,128)(2,1)S(1)}, u32[]{:S(2)}, u32[]{:S(2)}) collective-permute-start(bf16[128,1024]{1,0:T(8,128)(2,1)S(1)} %add_convert_fusion.8), channel_id=1, source_target_pairs={{0,2},{1,3},{2,0},{3,1},{4,6},{5,7},{6,4},{7,5},{8,10},{9,11},{10,... | collective-permute-start | bytes 786440 | tf_op jit(solution)/shard_map/ppermute | solution.py:350
  136.9 2.2 collective-permute-start.2
  142.7 2.6 collective-permute-start.6
  144.5 4.8 %collective-permute-start.3 = (bf16[128,1024]{1,0:T(8,128)(2,1)S(1)}, bf16[128,1024]{1,0:T(8,128)(2,1)S(1)}, u32[]{:S(2)}, u32[]{:S(2)}) collective-permute-start(bf16[128,1024]{1,0:T(8,128)(2,1)S(1)} %constant_dynamic-slice_fusion.2), channel_id=1, source_target_pairs={{0,1},{1,0},{2,3},{3,2},{4,5},{5,4},{6,7},{7,6},{8,9},{9,8},{10,11... | collective-permute-start | bytes 786440 | tf_op jit(solution)/shard_map/ppermute | solution.py:350
  145.4 10.7 %collective-permute-start.7 = (bf16[128,1024]{1,0:T(8,128)(2,1)S(1)}, bf16[128,1024]{1,0:T(8,128)(2,1)S(1)}, u32[]{:S(2)}, u32[]{:S(2)}) collective-permute-start(bf16[128,1024]{1,0:T(8,128)(2,1)S(1)} %add_convert_fusion.4), channel_id=1, source_target_pairs={{0,2},{1,3},{2,0},{3,1},{4,6},{5,7},{6,4},{7,5},{8,10},{9,11},{10,... | collective-permute-start | bytes 786440 | tf_op jit(solution)/shard_map/ppermute | solution.py:350
  149.3 15.6 %collective-permute-start.4 = (bf16[128,1024]{1,0:T(8,128)(2,1)S(1)}, bf16[128,1024]{1,0:T(8,128)(2,1)S(1)}, u32[]{:S(2)}, u32[]{:S(2)}) collective-permute-start(bf16[128,1024]{1,0:T(8,128)(2,1)S(1)} %add_convert_fusion.6), channel_id=1, source_target_pairs={{0,2},{1,3},{2,0},{3,1},{4,6},{5,7},{6,4},{7,5},{8,10},{9,11},{10,... | collective-permute-start | bytes 786440 | tf_op jit(solution)/shard_map/ppermute | solution.py:350
  156.1 9.5 %collective-permute-start.8 = (bf16[128,1024]{1,0:T(8,128)(2,1)S(1)}, bf16[128,1024]{1,0:T(8,128)(2,1)S(1)}, u32[]{:S(2)}, u32[]{:S(2)}) collective-permute-start(bf16[128,1024]{1,0:T(8,128)(2,1)S(1)} %add_convert_fusion.3), channel_id=1, source_target_pairs={{0,1},{1,0},{2,3},{3,2},{4,5},{5,4},{6,7},{7,6},{8,9},{9,8},{10,11... | collective-permute-start | bytes 786440 | tf_op jit(solution)/shard_map/ppermute | solution.py:350
  165.0 1.7 collective-permute-start.5
  184.5 57.2 %all-to-all-start.3 = ((bf16[8,512,256]{2,1,0:T(8,128)(2,1)}), bf16[8,512,256]{2,1,0:T(8,128)(2,1)}, u32[]{:S(2)}, u32[]{:S(2)}) async-start(bf16[8,512,256]{2,1,0:T(8,128)(2,1)} %get-tuple-element.22), calls=%async_computation.3 | async-start | bytes 4194304 | tf_op jit(solution)/shard_map/all_to_all | solution.py:499
  188.8 170.2 %all-reduce.8.cloned.1.call-start = ((), (), s32[]{:S(2)}) async-start(), calls=%async_computation.7 | async-start | bytes 1081344 | tf_op jit(solution)/shard_map/psum | solution.py:487
  246.2 1.6 collective-permute-start.9
  248.8 10.0 %collective-permute-start.10 = (bf16[128,1024]{1,0:T(8,128)(2,1)S(1)}, bf16[128,1024]{1,0:T(8,128)(2,1)S(1)}, u32[]{:S(2)}, u32[]{:S(2)}) collective-permute-start(bf16[128,1024]{1,0:T(8,128)(2,1)S(1)} %add_convert_fusion.2), channel_id=1, source_target_pairs={{0,2},{1,3},{2,0},{3,1},{4,6},{5,7},{6,4},{7,5},{8,10},{9,11},{10,... | collective-permute-start | bytes 786440 | tf_op jit(solution)/shard_map/ppermute | solution.py:350
  258.9 1.8 collective-permute-start.11
  297.1 13.1 %collective-permute-start.14 = (bf16[128,1152]{0,1:T(8,128)(2,1)S(1)}, bf16[128,1152]{0,1:T(8,128)(2,1)S(1)}, u32[]{:S(2)}, u32[]{:S(2)}) collective-permute-start(bf16[128,1152]{0,1:T(8,128)(2,1)S(1)} %reduce_sum.85), channel_id=1, source_target_pairs={{0,96},{32,0},{64,32},{96,64},{1,97},{33,1},{65,33},{97,65},{2,98}... | collective-permute-start | bytes 884744 | tf_op jit(solution)/shard_map/ppermute | solution.py:372
  299.0 11.5 %collective-permute-start.13 = (bf16[128,1152]{0,1:T(8,128)(2,1)S(1)}, bf16[128,1152]{0,1:T(8,128)(2,1)S(1)}, u32[]{:S(2)}, u32[]{:S(2)}) collective-permute-start(bf16[128,1152]{0,1:T(8,128)(2,1)S(1)} %reduce_sum.85), channel_id=1, source_target_pairs={{0,64},{32,96},{64,0},{96,32},{1,65},{33,97},{65,1},{97,33},{2,66}... | collective-permute-start | bytes 884744 | tf_op jit(solution)/shard_map/ppermute | solution.py:372
  300.5 13.4 %collective-permute-start.12 = (bf16[128,1152]{0,1:T(8,128)(2,1)S(1)}, bf16[128,1152]{0,1:T(8,128)(2,1)S(1)}, u32[]{:S(2)}, u32[]{:S(2)}) collective-permute-start(bf16[128,1152]{0,1:T(8,128)(2,1)S(1)} %reduce_sum.85), channel_id=1, source_target_pairs={{0,32},{32,64},{64,96},{96,0},{1,33},{33,65},{65,97},{97,1},{2,34}... | collective-permute-start | bytes 884744 | tf_op jit(solution)/shard_map/ppermute | solution.py:372
  314.1 2.7 collective-permute-start.15
  316.8 6.4 %collective-permute-start.16 = (bf16[16,128]{1,0:T(8,128)(2,1)S(1)}, bf16[16,128]{1,0:T(8,128)(2,1)S(1)}, u32[]{:S(2)}, u32[]{:S(2)}) collective-permute-start(bf16[16,128]{1,0:T(8,128)(2,1)S(1)} %get-tuple-element.95), channel_id=1, source_target_pairs={{0,2},{1,3},{2,0},{3,1},{4,6},{5,7},{6,4},{7,5},{8,10},{9,11},{10,... | collective-permute-start | bytes 12296 | tf_op jit(solution)/shard_map/ppermute | solution.py:350
  (20 other events, 203.0 us)
Sparse Core Ops, SparseCore 0:
  10.3 110.0 all-gather.1
  165.1 80.0 reduce-scatter.3
  316.9 42.1 all-reduce.7

commit v2 on v1

v2 whole, which is shorter than its diff:
```python
import functools

import jax
import jax.numpy as jnp
from jax import lax
from jax.experimental import pallas as pl
from jax.experimental.pallas import tpu as pltpu
from jax.sharding import PartitionSpec as P

HEAD_DIM = 64
EPS = 1e-06
SEQ_EDGES = (1, 2, 3, 4, 5, 6, 7, 8, 12, 16, 23, 32, 46, 64, 91)
BOX_EDGES = (2, 4, 6, 8, 12, 16, 24, 32, 48, 64, 96, 128, 192, 256, 384)
BF16 = jnp.bfloat16
F32 = jnp.float32
LANES = 128
MIB = 2**20
VMEM_MIB = 32
SMEM = pl.BlockSpec(memory_space=pltpu.SMEM)


def whole(*arrays):
    return [pl.BlockSpec(item.shape, lambda s, rank=len(item.shape): (0,) * rank) for item in arrays]


def shape(dims, kind):
    return jax.ShapeDtypeStruct(dims, kind)


HBM = pl.BlockSpec(memory_space=pl.ANY)


def simple(kernel, name, out, args, place=None, deps=(), micros=0.05):
    count = len(args) + (place is not None)

    def body(*refs):
        kernel(*refs[:count], *refs[count + len(deps) :])

    single = not isinstance(out, list)
    specs = whole(*([out] if single else out))
    return pl.pallas_call(
        body,
        grid=(1,),
        in_specs=[SMEM] * (place is not None) + whole(*args) + [HBM] * len(deps),
        out_specs=specs[0] if single else specs,
        out_shape=out,
        compiler_params=params(),
        cost_estimate=cost(micros),
        name=name,
    )(*([place] if place is not None else []), *args, *deps)


def add_kernel(a_ref, b_ref, out_ref):
    out_ref[...] = (a_ref[...].astype(F32) + b_ref[...].astype(F32)).astype(BF16)


def add(a, b, deps=()):
    return simple(add_kernel, "add", shape(a.shape, BF16), (a, b), deps=deps)


def stack_kernel(*refs):
    for at, ref in enumerate(refs[:-1]):
        refs[-1][at] = ref[...]


def stack(parts, deps=()):
    out = shape((len(parts),) + parts[0].shape, BF16)
    return simple(stack_kernel, "stack", out, parts, deps=deps)


def both_halves(own, got, first):
    return jnp.where(first, own, got), jnp.where(first, got, own)


def keep_and_send(values, core, keep_ref, send_ref):
    half = values.shape[0] // 2
    first, second = values[:half], values[half:]
    keep_ref[...] = jnp.where(core == 0, first, second)
    send_ref[...] = jnp.where(core == 0, second, first)


def params(mib=VMEM_MIB):
    return pltpu.CompilerParams(
        vmem_limit_bytes=mib * MIB, dimension_semantics=("arbitrary",)
    )


def cost(micros):
    return pl.CostEstimate(flops=int(micros * 1.1e9), bytes_accessed=int(micros * 1e5), transcendentals=0)


def contract_rows(left, right):
    return lax.dot_general(
        left, right, (((0,), (0,)), ((), ())), preferred_element_type=jnp.float32
    )


def contract_cols(left, right):
    return lax.dot_general(
        left, right, (((1,), (1,)), ((), ())), preferred_element_type=jnp.float32
    )


def count_edges(magnitude, edge_list):
    result = jnp.zeros(magnitude.shape, jnp.int32)
    for border in edge_list:
        result = result + (magnitude >= border).astype(jnp.int32)
    return result


def box_cell(offset):
    half = jnp.abs(offset) >> 1
    cell = jnp.where(half < 32, half, (half >> 4) + 30)
    return cell + jnp.where(offset > 0, 64, 0)


def cell_bucket(cell):
    low = cell & 63
    half = jnp.where(low < 32, low, (low - 30) << 4)
    return count_edges(half * 2, BOX_EDGES) + jnp.where(cell >= 64, 16, 0)


def lookup(table, index):
    return jnp.take_along_axis(table, index, axis=1, mode="promise_in_bounds")


SMALL = 16


def pack_kernel(
    place_ref, seg_hbm, box_hbm, one_hbm, two_hbm, table_hbm, query_hbm, key_hbm, value_hbm, gate_hbm, up_hbm, down_hbm, early_ref, late_ref, *rest
):
    refs, sems = rest[:-1], rest[-1]
    units = gate_hbm.shape[0] // 4
    mine = pl.ds(pl.multiple_of(place_ref[2] * units, 16), units)
    sources = [seg_hbm, box_hbm, one_hbm, two_hbm, table_hbm, query_hbm, key_hbm, value_hbm]
    copies = [pltpu.make_async_copy(src, dst, sems.at[at]) for at, (src, dst) in enumerate(zip(sources, refs))]
    for at, src in enumerate((gate_hbm, up_hbm, down_hbm)):
        spot = late_ref.at[at * units : (at + 1) * units, :]
        copies.append(pltpu.make_async_copy(src.at[mine, :], spot, sems.at[len(sources) + at]))
    for copy in copies:
        copy.start()
    for copy in copies:
        copy.wait()
    seg_ref, box_ref, one_ref, two_ref, table_ref, query_ref, key_ref, value_ref = refs
    width = seg_ref.shape[1]
    pair = query_ref.shape[1] // 2
    row = lax.broadcasted_iota(jnp.int32, (SMALL, width), 0)
    boxes = box_ref[...]
    centre_x = boxes[0:1] + boxes[2:3]
    centre_y = boxes[1:2] + boxes[3:4]
    gains = jnp.concatenate([one_ref[...], two_ref[...]], axis=1).astype(F32)
    small = table_ref[...].astype(F32)
    for at, values in enumerate(
        (seg_ref[...], centre_x >> 8, centre_x & 255, centre_y >> 8, centre_y & 255, gains)
    ):
        small = jnp.where(row == at, values.astype(F32), small)
    small = small.astype(BF16)
    small = jnp.concatenate([small, jnp.zeros((SMALL, 3 * pair - width), BF16)], axis=1)
    for block in range(early_ref.shape[0]):
        half = block // 4
        cols = slice(half * pair, (half + 1) * pair)
        for at, ref in enumerate((query_ref, key_ref, value_ref)):
            early_ref[block, :LANES, at * pair : (at + 1) * pair] = ref[:, cols]
        early_ref[block, LANES:, :] = small


def pack(place, small, weights, late):
    pair = weights[0].shape[1] // 2
    args = small + weights
    out = [
        shape((8, LANES + SMALL, 3 * pair), BF16),
        shape((3 * late[0].shape[0] // 4, LANES), BF16),
    ]
    return pl.pallas_call(
        pack_kernel,
        grid=(1,),
        in_specs=[SMEM] + [HBM] * (len(args) + 3),
        out_specs=whole(*out),
        out_shape=out,
        scratch_shapes=[pltpu.VMEM(item.shape, item.dtype) for item in args]
        + [pltpu.SemaphoreType.DMA((len(args) + 3,))],
        compiler_params=params(64),
        cost_estimate=cost(0.05),
        name="pack",
    )(place, *args, *late)


def unfold_rows(values):
    return jnp.concatenate(jnp.split(values, 4, axis=0), axis=1)


def fold_rows(values):
    return jnp.concatenate(jnp.split(values, 4, axis=1), axis=0)


def project_kernel(
    place_ref, early_ref, own_ref, other_ref, out_w_ref, normed_ref, query_ref, pair_ref, gain_ref, key_ref, meta_ref, table_ref
):
    rows, model = own_ref.shape
    pair = query_ref.shape[1]
    side, depth = place_ref[0], place_ref[1]
    small = [early_ref[block, LANES:, :rows].astype(F32) for block in range(8)]
    for at in range(2):
        lanes = slice(at * LANES, (at + 1) * LANES)
        gain = jnp.concatenate([part[5:6, lanes] for part in small], axis=1)
        gain_ref[at : at + 1, :] = gain
        if at == 0:
            gain_one = gain

    out_w_other = fold_rows(other_ref[rows:, :])
    for values, half in ((out_w_ref[...], side), (out_w_other, 1 - side)):
        here = pl.ds(pl.multiple_of(2 * rows + half * LANES, LANES), LANES)
        for copy in range(4):
            pair_ref[copy, here, :] = values
    weight = jnp.concatenate([early_ref[block, :LANES, :] for block in range(8)], axis=0)
    for ref, half in ((own_ref, side), (other_ref, 1 - side)):
        inputs = ref[:rows, :].astype(F32)
        scale = lax.rsqrt(jnp.mean(inputs * inputs, axis=1, keepdims=True) + EPS)
        normed = (inputs * scale * gain_one).astype(BF16)
        here = pl.ds(pl.multiple_of(half * rows, rows), rows)
        normed_ref[here, :] = normed
        result = jnp.dot(normed, weight, preferred_element_type=F32).astype(BF16)
        query_ref[here, :] = result[:, :pair] * jnp.asarray(HEAD_DIM ** (-0.5), BF16)
        for copy in range(4):
            pair_ref[copy, here, :] = result[:, pair:]

    time = lax.broadcasted_iota(jnp.int32, (1, rows), 1)
    for block in range(8):
        part = small[block]
        at = (block % 4) * 2 + block // 4
        there = slice(at * rows, (at + 1) * rows)
        key_ref[0:1, there] = part[0:1].astype(jnp.int32)
        key_ref[1:2, there] = (part[1:2] * 256.0 + part[2:3]).astype(jnp.int32)
        key_ref[2:3, there] = (part[3:4] * 256.0 + part[4:5]).astype(jnp.int32)
        for half in range(2):
            ahead = (block - depth - 4 * half) * rows + SEQ_SPAN // 4
            key_ref[3 + half : 4 + half, there] = jnp.clip(time + ahead, 0, SEQ_SPAN - 1)
        key_ref[5:8, there] = jnp.zeros((3, rows), jnp.int32)

    for half in range(2):
        part = early_ref[depth + 4 * half, LANES:, :rows].astype(F32)
        columns = jnp.transpose(part)
        seg = columns[:, 0:1]
        centre_x = columns[:, 1:2] * 256.0 + columns[:, 2:3]
        centre_y = columns[:, 3:4] * 256.0 + columns[:, 4:5]
        for at, values in enumerate((seg, centre_x, centre_y)):
            wide = jnp.broadcast_to(values.astype(jnp.int32), (rows, LANES))
            meta_ref[at, half * rows : (half + 1) * rows, :] = wide

    lane = lax.broadcasted_iota(jnp.int32, (8, LANES), 1)
    table = jnp.zeros((8, LANES), F32)
    for block in range(8):
        entries = jnp.where(side == 0, small[block][6:8, :LANES], small[block][8:10, :LANES])
        entries = jnp.concatenate([entries, jnp.zeros((6, LANES), F32)], axis=0)
        index = jnp.clip(lane - 12 * block, 0, LANES - 1)
        found = lookup(entries, index)
        table = jnp.where((lane >= 12 * block) & (lane < 12 * block + 12), found, table)
    table_ref[...] = table


def project(place, early, own, other, out_w, deps):
    rows, model = own.shape
    pair = early.shape[2] // 3
    out = [
        shape((2 * rows, model), BF16),
        shape((2 * rows, pair), BF16),
        shape((4, 2 * rows + 2 * LANES, 2 * pair), BF16),
        shape((2, model), F32),
        shape((8, 8 * rows), jnp.int32),
        shape((3, 2 * rows, LANES), jnp.int32),
        shape((8, LANES), F32),
    ]
    return simple(
        project_kernel, "project", out, (early, own, other, out_w), place, deps
    )


STEPS = 3600.0
SHIFT = 10800.0
MASKED = -(2**31)


def bias_kernel(place_ref, meta_ref, key_ref, table_ref, *refs):
    bias_ref = refs[-1]
    chunk, length = bias_ref.shape
    width = TOKENS_BLOCK
    step = pl.program_id(0)
    half = step // (2 * width // chunk // 2)
    first_row = lax.rem(step * chunk, width)
    query_block = place_ref[1] + 4 * half
    lane = lax.broadcasted_iota(jnp.int32, (8, LANES), 1)
    buckets = cell_bucket(lane)
    table = table_ref[...]

    def packed(index):
        found = lookup(table, index)
        high = jnp.round(found[0:1, :] * STEPS).astype(jnp.int32)
        low = jnp.round(found[1:2, :] * STEPS + SHIFT).astype(jnp.int32)
        return (high << 16) + low

    def spread(values):
        return jnp.broadcast_to(values, (chunk, LANES))

    hor = packed(buckets + 32)
    ver = spread(packed(buckets + 64))
    seq_count = count_edges(jnp.abs(lane - 64), SEQ_EDGES) + jnp.where(lane > 64, 16, 0)
    seq = spread(packed(seq_count))
    behind, middle, beyond = [packed(jnp.full((8, LANES), at, jnp.int32)) for at in (15, 30, 31)]

    def key_block(at):
        return at // 2 + 4 * lax.rem(at, 2)

    def block_of_keys(at, with_near):
        ahead = key_block(at) * width - query_block * width - first_row
        far = spread(hor if with_near else hor + jnp.where(ahead > 0, beyond, behind))
        for column in range(width // LANES):
            there = pl.ds(pl.multiple_of(at * width + column * LANES, LANES), LANES)
            keys = key_ref[:, there]
            total = lookup(far, box_cell(keys[1:2, :] - meta_ref[1]))
            total = total + lookup(ver, box_cell(keys[2:3, :] - meta_ref[2]))
            if with_near:
                row = lax.broadcasted_iota(jnp.int32, (chunk, LANES), 0)
                col = lax.broadcasted_iota(jnp.int32, (chunk, LANES), 1)
                offset = col - row + (ahead + column * LANES)
                found = lookup(seq, jnp.clip(offset + 64, 0, LANES - 1))
                found = jnp.where(offset >= 64, middle, found)
                found = jnp.where(offset >= 91, beyond, found)
                total = total + jnp.where(offset <= -91, behind, found)
            bias_ref[:, there] = jnp.where(keys[0:1, :] == meta_ref[0], total, MASKED)

    def body(at, carry):
        near = jnp.abs(key_block(at) - query_block) <= 1
        pl.when(near)(functools.partial(block_of_keys, at, True))
        pl.when(jnp.logical_not(near))(functools.partial(block_of_keys, at, False))
        return carry

    lax.fori_loop(0, length // width, body, 0)


TOKENS_BLOCK = 256


def bias_scores(place, meta, key_meta, table, deps):
    rows = meta.shape[1]
    length = key_meta.shape[1]
    chunk = 128
    return pl.pallas_call(
        bias_kernel,
        grid=(rows // chunk,),
        in_specs=[
            pl.BlockSpec(memory_space=pltpu.SMEM),
            pl.BlockSpec((3, chunk, LANES), lambda s: (0, s, 0)),
            pl.BlockSpec((8, length), lambda s: (0, 0)),
            pl.BlockSpec((8, LANES), lambda s: (0, 0)),
        ]
        + [HBM] * len(deps),
        out_specs=pl.BlockSpec((chunk, length), lambda s: (s, 0)),
        out_shape=jax.ShapeDtypeStruct((rows, length), jnp.int32),
        compiler_params=params(),
        cost_estimate=cost(10),
        name="bias_scores",
    )(place, meta, key_meta, table, *deps)


def head_masks(shape):
    lane = lax.broadcasted_iota(jnp.int32, shape, 1)
    return lane < HEAD_DIM, lane >= HEAD_DIM


def attend_kernel(place_ref, query_ref, bias_ref, pair_ref, *refs):
    probs_ref, exact_ref, mine_ref, other_ref = refs[-4:]
    count, _, both = pair_ref.shape
    width = bias_ref.shape[1] // count
    features = both // 2
    rows = query_ref.shape[0]
    masks = head_masks((rows, features))
    query = query_ref[...]
    allowed = []
    codes = []
    for at in range(count):
        code = bias_ref[:, at * width : (at + 1) * width]
        codes.append(code)
        allowed.append(code != MASKED)
    outs = []
    for head in range(2):
        mine = jnp.where(masks[head], query, jnp.zeros_like(query))
        scores = []
        for at in range(count):
            code = (codes[at] >> 16) if head == 0 else (codes[at] & 65535)
            score = contract_cols(mine, pair_ref[at, :width, :features])
            score = score + code.astype(F32) * (1.0 / STEPS)
            scores.append(jnp.where(allowed[at], score, -1e30))
        top = functools.reduce(jnp.maximum, scores)
        top = jnp.max(top, axis=1, keepdims=True)
        weights = [jnp.exp(score - top) for score in scores]
        total = functools.reduce(jnp.add, weights)
        inverse = 1.0 / jnp.sum(total, axis=1, keepdims=True)
        result = None
        for at in range(count):
            low = (weights[at] * inverse).astype(BF16)
            probs_ref[head, :, at * width : (at + 1) * width] = low
            part = jnp.dot(low, pair_ref[at, :width, features:], preferred_element_type=F32)
            result = part if result is None else result + part
        outs.append(result)
    exact = jnp.where(masks[0], outs[0], outs[1])
    exact_ref[...] = exact
    low = exact.astype(BF16)
    tiles = mine_ref.shape[0] // rows
    step = pl.program_id(0)
    here = pl.ds(pl.multiple_of(lax.rem(step, tiles) * rows, rows), rows)
    own = step // tiles == place_ref[0]

    @pl.when(own)
    def _():
        mine_ref[here, :] = low

    @pl.when(jnp.logical_not(own))
    def _():
        other_ref[here, :] = low


def attend(place, queries, pairs, bias, deps):
    rows, length = bias.shape
    both = pairs.shape[2]
    tile = 128
    features = both // 2
    slim = pl.BlockSpec((tile, features), lambda s: (s, 0))
    half = shape((rows // 2, features), BF16)
    return pl.pallas_call(
        attend_kernel,
        grid=(rows // tile,),
        in_specs=[SMEM, slim, pl.BlockSpec((tile, length), lambda s: (s, 0))]
        + whole(pairs)
        + [HBM] * len(deps),
        out_specs=[pl.BlockSpec((2, tile, length), lambda s: (0, s, 0)), slim] + whole(half, half),
        out_shape=[
            shape((2, rows, length), BF16),
            shape((rows, features), F32),
            half,
            half,
        ],
        compiler_params=params(),
        cost_estimate=cost(9),
        name="attend",
    )(place, queries, bias, pairs, *deps)


def out_weight(pair_ref):
    start = pair_ref.shape[1] - 2 * LANES
    parts = []
    for block in range(8):
        first = start + block // 4 * LANES
        parts.append(pair_ref[block % 4, first : first + LANES, :])
    return jnp.concatenate(parts, axis=0)


def branch_kernel(place_ref, mine_ref, got_ref, pair_ref, keep_ref, send_ref):
    parts = both_halves(mine_ref[...], got_ref[...], place_ref[0] == 0)
    attended = jnp.concatenate(parts, axis=1)
    result = contract_cols(attended, out_weight(pair_ref)).astype(BF16)
    keep_and_send(result, place_ref[3], keep_ref, send_ref)


def branch_part(place, mine, got, pairs, deps):
    half = shape((mine.shape[0] // 2, 8 * LANES), BF16)
    return simple(branch_kernel, "branch_part", [half, half], (mine, got, pairs), place, deps, 2)


def gelu_parts(gate):
    rate = 0.7978845608028654
    square = gate * gate
    slope = jnp.tanh(rate * gate * (1.0 + 0.044715 * square))
    half = 0.5 * (1.0 + slope)
    inner = rate * (1.0 + 3.0 * 0.044715 * square)
    return gate * half, half + 0.5 * gate * (1.0 - slope * slope) * inner


def piece_copies(place_ref, piece_refs, held, sems, hop, first):
    side, depth = place_ref[0], place_ref[1]
    height = held.shape[1]
    copies = []
    for far in range(2):
        for turn in range(4):
            block = (side + far * (1 - 2 * side)) * 4 + lax.rem(depth + turn, 4)
            lanes = pl.ds(pl.multiple_of(block * LANES, LANES), LANES)
            copies.append(
                pltpu.make_async_copy(
                    piece_refs[2 * hop + far].at[turn, pl.ds(first, height), :],
                    held.at[hop, :, lanes],
                    sems.at[hop, 4 * far + turn],
                )
            )
    return copies


def ffn_prepare_kernel(place_ref, dy_ref, *refs):
    piece_refs, (weight_ref, grad_ref, sems) = refs[:8], refs[8:]
    copies = [piece_copies(place_ref, piece_refs, weight_ref, sems, hop, 0) for hop in range(4)]
    units = weight_ref.shape[1] // 3
    for group in copies:
        for copy in group:
            copy.start()
    for hop in range(4):
        for copy in copies[hop]:
            copy.wait()
        grad_ref[hop] = contract_cols(weight_ref[hop, 2 * units :, :], dy_ref[...])


def ffn_prepare(place, dy, pieces):
    rows, model = dy.shape
    height = pieces[0].shape[1]
    out = [shape((4, height, model), BF16), shape((4, height // 3, rows), F32)]
    return pl.pallas_call(
        ffn_prepare_kernel,
        grid=(1,),
        in_specs=[SMEM] + whole(dy) + [HBM] * 8,
        out_specs=whole(*out),
        out_shape=out,
        scratch_shapes=[pltpu.SemaphoreType.DMA((4, 8))],
        compiler_params=params(),
        cost_estimate=cost(4),
        name="ffn_prepare",
    )(place, dy, *pieces)


def middle_of(tokens_ref, total_ref, got_ref, core):
    branch = jnp.concatenate(both_halves(total_ref[...], got_ref[...], core == 0), axis=0)
    return tokens_ref[...].astype(F32) + branch.astype(F32)


def rms_scale(values):
    return lax.rsqrt(jnp.mean(values * values, axis=1, keepdims=True) + EPS)


def ffn_kernel(
    place_ref, tokens_ref, total_ref, got_ref, gain_ref, hidden_grad_ref, weight_ref, normed_ref, parts_ref, keep_ref, send_ref, sums, turned
):
    units = weight_ref.shape[1] // 2
    step = pl.program_id(0)

    @pl.when(step == 0)
    def _():
        middle = middle_of(tokens_ref, total_ref, got_ref, place_ref[3])
        normed = (middle * rms_scale(middle) * gain_ref[1:2, :]).astype(BF16)
        normed_ref[...] = normed
        turned[...] = jnp.transpose(normed)
        sums[...] = jnp.zeros_like(sums)

    gates = jnp.dot(weight_ref[0], turned[...], preferred_element_type=F32)
    gate, upward = gates[:units], gates[units:]
    hidden_grad = hidden_grad_ref[0]
    value, slope = gelu_parts(gate)
    grads = jnp.concatenate([hidden_grad * upward * slope, hidden_grad * value], axis=0).astype(BF16)
    parts_ref[0, : 2 * units, :] = grads
    parts_ref[0, 2 * units :, :] = (value * upward).astype(BF16)
    sums[...] += contract_rows(grads, weight_ref[0])

    @pl.when(step == pl.num_programs(0) - 1)
    def _():
        keep_and_send(sums[...].astype(BF16), place_ref[3], keep_ref, send_ref)


def ffn_forward(place, tokens, total, got, gains, hidden_grad, weights):
    rows, model = tokens.shape
    hops, height, _ = weights.shape
    half = shape((rows // 2, model), BF16)
    out = [shape((rows, model), BF16), shape((hops, height, rows), BF16), half, half]

    def chunk(item):
        return pl.BlockSpec((1,) + item.shape[1:], lambda s: (s, 0, 0))

    return pl.pallas_call(
        ffn_kernel,
        grid=(hops,),
        in_specs=[SMEM]
        + whole(tokens, total, got, gains)
        + [chunk(hidden_grad), pl.BlockSpec((1, height // 3 * 2, model), lambda s: (s, 0, 0))],
        out_specs=whole(out[0]) + [chunk(out[1])] + whole(half, half),
        out_shape=out,
        scratch_shapes=[pltpu.VMEM((rows, model), F32), pltpu.VMEM((model, rows), BF16)],
        compiler_params=params(),
        cost_estimate=cost(5),
        name="ffn_forward",
    )(place, tokens, total, got, gains, hidden_grad, weights)


def ffn_back_kernel(place_ref, parts_ref, normed_ref, dy_ref, *refs):
    grad_ref = refs[-1]
    units = parts_ref.shape[1] // 3
    grad_ref[0, : 2 * units, :] = jnp.dot(
        parts_ref[0, : 2 * units, :], normed_ref[...], preferred_element_type=F32
    ).astype(BF16)
    grad_ref[0, 2 * units :, :] = jnp.dot(
        parts_ref[0, 2 * units :, :], dy_ref[...], preferred_element_type=F32
    ).astype(BF16)


def ffn_output_kernel(place_ref, parts_ref, weight_ref, *refs):
    keep_ref, send_ref, sums = refs[-3:]
    step = pl.program_id(0)
    part = contract_rows(parts_ref[0], weight_ref[0])

    @pl.when(step == 0)
    def _():
        sums[...] = part

    @pl.when(step > 0)
    def _():
        sums[...] += part

    @pl.when(step == pl.num_programs(0) - 1)
    def _():
        keep_and_send(sums[...].astype(BF16), place_ref[3], keep_ref, send_ref)


def ffn_output(place, parts, weights, deps):
    hops, height, rows = parts.shape
    model = weights.shape[2]
    half = shape((rows // 2, model), BF16)
    return pl.pallas_call(
        ffn_output_kernel,
        grid=(hops,),
        in_specs=[
            SMEM,
            pl.BlockSpec((1, height // 3, rows), lambda s: (s, 2, 0)),
            pl.BlockSpec((1, height // 3, model), lambda s: (s, 2, 0)),
        ]
        + [HBM] * len(deps),
        out_specs=whole(half, half),
        out_shape=[half, half],
        scratch_shapes=[pltpu.VMEM((rows, model), F32)],
        compiler_params=params(),
        cost_estimate=cost(3),
        name="ffn_output",
    )(place, parts, weights, *deps)


def norm_back(inputs, gain, normed_grad):
    scale = rms_scale(inputs)
    gain_grad = jnp.sum(normed_grad * inputs * scale, axis=0, keepdims=True)
    weighted = normed_grad * gain
    mean = jnp.mean(weighted * inputs, axis=1, keepdims=True)
    return scale * weighted - inputs * (scale * scale * scale) * mean, gain_grad


def middle_kernel(
    place_ref, tokens_ref, total_ref, got_ref, dy_ref, gain_ref, grad_ref, grad_got_ref, pair_ref, middle_ref, low_ref, two_ref, mine_ref, other_ref
):
    core = place_ref[3]
    middle = middle_of(tokens_ref, total_ref, got_ref, core)
    parts = both_halves(grad_ref[...], grad_got_ref[...], core == 0)
    normed_grad = jnp.concatenate(parts, axis=0).astype(F32)
    result, gain_grad = norm_back(middle, gain_ref[1:2, :], normed_grad)
    result = dy_ref[...].astype(F32) + result
    middle_ref[...] = result
    low = result.astype(BF16)
    low_ref[...] = low
    two_ref[...] = gain_grad
    attended = jnp.dot(low, out_weight(pair_ref), preferred_element_type=F32).astype(BF16)
    pair = attended.shape[1] // 2
    first = place_ref[0] == 0
    mine_ref[...] = jnp.where(first, attended[:, :pair], attended[:, pair:])
    other_ref[...] = jnp.where(first, attended[:, pair:], attended[:, :pair])


def middle_back(place, tokens, total, got, dy, gains, grad, grad_got, pairs):
    rows, model = tokens.shape
    half = shape((rows, pairs.shape[2] // 2), BF16)
    out = [shape((rows, model), F32), shape((rows, model), BF16), shape((1, model), F32), half, half]
    args = (tokens, total, got, dy, gains, grad, grad_got, pairs)
    return simple(middle_kernel, "middle_back", out, args, place, micros=3)


def tokens_kernel(place_ref, tokens_ref, gain_ref, grad_ref, grad_got_ref, middle_ref, out_ref):
    parts = both_halves(grad_ref[...], grad_got_ref[...], place_ref[3] == 0)
    normed_grad = jnp.concatenate(parts, axis=0).astype(F32)
    result, _ = norm_back(tokens_ref[...].astype(F32), gain_ref[0:1, :], normed_grad)
    out_ref[...] = middle_ref[...] + result


def tokens_back(place, tokens, gains, grad, grad_got, middle_grad):
    out = shape(tokens.shape, F32)
    return simple(
        tokens_kernel, "tokens_back", out, (tokens, gains, grad, grad_got, middle_grad), place, micros=2
    )


def mixed_kernel(place_ref, tokens_ref, total_ref, got_ref, out_total_ref, out_got_ref, out_ref):
    core = place_ref[3]
    middle = middle_of(tokens_ref, total_ref, got_ref, core)
    parts = both_halves(out_total_ref[...], out_got_ref[...], core == 0)
    out_ref[...] = (middle + jnp.concatenate(parts, axis=0).astype(F32)).astype(BF16)


HOPS = (0, 1, 3, 2)


def ffn_back(place, parts, normed, dy, deps):
    rows, model = normed.shape
    hops, height, _ = parts.shape

    def owner(step, place_ref):
        hop = jnp.where(step == 0, 0, jnp.where(step == 1, 1, jnp.where(step == 2, 3, 2)))
        return lax.rem(place_ref[2] - hop + 4, 4)

    def same(*arrays):
        return [pl.BlockSpec(item.shape, lambda s, p: (0, 0)) for item in arrays]

    return pl.pallas_call(
        ffn_back_kernel,
        grid_spec=pltpu.PrefetchScalarGridSpec(
            num_scalar_prefetch=1,
            grid=(hops,),
            in_specs=[pl.BlockSpec((1, height, rows), lambda s, p: (s, 0, 0))]
            + same(normed, dy)
            + [HBM] * len(deps),
            out_specs=pl.BlockSpec((1, height, model), lambda s, p: (owner(s, p), 0, 0)),
        ),
        out_shape=shape((hops, height, model), BF16),
        compiler_params=params(),
        cost_estimate=cost(4),
        name="ffn_back",
    )(place, parts, normed, dy, *deps)


def fold_kernel(place_ref, parts_ref, *refs):
    out_ref = refs[-1]
    for block in range(4):
        lanes = slice(block * LANES, (block + 1) * LANES)
        total = parts_ref[0, :, lanes].astype(F32)
        for at in range(1, parts_ref.shape[0]):
            total = total + parts_ref[at, :, lanes].astype(F32)
        out_ref[0, lax.rem(block - place_ref[1] + 4, 4)] = total.astype(BF16)


def fold_to_blocks(place, parts, deps):
    count, height, model = parts.shape
    return pl.pallas_call(
        fold_kernel,
        grid_spec=pltpu.PrefetchScalarGridSpec(
            num_scalar_prefetch=1,
            grid=(2,),
            in_specs=[pl.BlockSpec((count, height, model // 2), lambda s, p: (0, 0, s))]
            + [HBM] * len(deps),
            out_specs=pl.BlockSpec(
                (1, 4, height, LANES), lambda s, p: (jnp.where(s == p[0], 0, 1), 0, 0, 0)
            ),
        ),
        out_shape=shape((2, 4, height, LANES), BF16),
        compiler_params=params(),
        cost_estimate=cost(4),
        name="fold_to_blocks",
    )(place, parts, *deps)


def attend_back_kernel(place_ref, query_ref, mine_ref, got_ref, exact_ref, probs_ref, pair_ref, *refs):
    score_ref, pair_grad_refs = refs[-9], refs[-8:-4]
    query_grad_ref, sums, delta, grads = refs[-4:]
    _, rows, width = probs_ref.shape
    features = query_ref.shape[1]
    step = pl.program_id(0)
    masks = head_masks((rows, features))
    query = query_ref[...]

    @pl.when(step == 0)
    def _():
        sums[...] = jnp.zeros_like(sums)
        parts = both_halves(mine_ref[...], got_ref[...], place_ref[0] == 0)
        grads[...] = jnp.concatenate(parts, axis=0)
        product = grads[...].astype(F32) * exact_ref[...]
        for head in range(2):
            row = jnp.sum(jnp.where(masks[head], product, 0.0), axis=1, keepdims=True)
            delta[head] = jnp.broadcast_to(row, (rows, LANES))

    grad = grads[...]
    keys = pair_ref[0, :, :features]
    values = pair_ref[0, :, features:]
    parts = []
    key_grads = []
    value_grads = []
    for head in range(2):
        cols = slice(head * HEAD_DIM, (head + 1) * HEAD_DIM)
        mine = jnp.where(masks[head], grad, jnp.zeros_like(grad))
        probs = probs_ref[head]
        prob_grad = contract_cols(mine, values)
        offset = jnp.concatenate([delta[head]] * (width // LANES), axis=1)
        score_grad = (probs.astype(F32) * (prob_grad - offset)).astype(BF16)
        score_ref[head] = score_grad
        parts.append(jnp.dot(score_grad, keys, preferred_element_type=F32))
        key_grads.append(contract_rows(query[:, cols], score_grad).astype(BF16))
        value_grads.append(contract_rows(grad[:, cols], probs).astype(BF16))
    for at in range(4):

        @pl.when(step == at)
        def _():
            for spot, part in enumerate(key_grads + value_grads):
                pair_grad_refs[at][spot * HEAD_DIM : (spot + 1) * HEAD_DIM, :] = part

    sums[...] += jnp.where(masks[0], parts[0], parts[1])

    @pl.when(step == pl.num_programs(0) - 1)
    def _():
        query_grad_ref[...] = (sums[...] * HEAD_DIM ** (-0.5)).astype(BF16)


def attend_back(place, queries, mine, got, exact, pairs, probs, deps):
    _, rows, length = probs.shape
    features = queries.shape[1]
    width, both = rows, pairs.shape[2]

    def spot(step, place_ref):
        return lax.rem(place_ref[1] + step, 4)

    def same(*arrays):
        return [pl.BlockSpec(item.shape, lambda s, p: (0, 0)) for item in arrays]

    slab = pl.BlockSpec((2, rows, width), lambda s, p: (0, 0, spot(s, p)))
    pair_grads = [shape((both, width), BF16)] * 4
    query_grad = shape((rows, features), BF16)
    return pl.pallas_call(
        attend_back_kernel,
        grid_spec=pltpu.PrefetchScalarGridSpec(
            num_scalar_prefetch=1,
            grid=(4,),
            in_specs=same(queries, mine, got, exact)
            + [slab, pl.BlockSpec((1, width, both), lambda s, p: (spot(s, p), 0, 0))]
            + [HBM] * len(deps),
            out_specs=[slab] + same(*pair_grads, query_grad),
            scratch_shapes=[
                pltpu.VMEM((rows, features), F32),
                pltpu.VMEM((2, rows, LANES), F32),
                pltpu.VMEM((rows, features), BF16),
            ],
        ),
        out_shape=[shape((2, rows, length), BF16)] + pair_grads + [query_grad],
        compiler_params=params(),
        cost_estimate=cost(4),
        name="attend_back",
    )(place, queries, mine, got, exact, probs, pairs, *deps)


BOX_SPAN = 1024
SEQ_SPAN = 512
TILE = 512


def threshold_row(edge_list, far, lane):
    borders = [-far] + [1 - edge for edge in reversed(edge_list)] + [1] + list(edge_list)
    result = jnp.zeros(lane.shape, jnp.int32)
    for at, border in enumerate(borders):
        result = jnp.where(lane == at, border, result)
    return result


def table_grad_kernel(meta_ref, key_ref, score_ref, *refs):
    out_ref, sums_ref = refs[-2:]
    _, rows, length = score_ref.shape
    half = rows // 2
    step = pl.program_id(0)
    lane = lax.broadcasted_iota(jnp.int32, (1, LANES), 1)
    level = lax.broadcasted_iota(jnp.int32, (TILE, 1), 0)

    def add(place, key_row, mine, edges, top, offset, span):
        index = jnp.clip(mine + threshold_row(edges, 4096, lane), 0, top)
        column = index & (LANES - 1)
        block = (index - offset) >> 7
        reached = (key_ref[pl.ds(key_row, 1), :] >= level + offset).astype(F32).astype(BF16)
        for head in range(2):
            sums = contract_cols(score_ref[head, span, :], reached)
            picked = jnp.zeros(column.shape, F32)
            for at in range(TILE // LANES):
                found = lookup(sums[:, at * LANES : (at + 1) * LANES], column)
                picked = picked + jnp.where(block == at, found, 0.0)
            sums_ref[place, head : head + 1, :] += jnp.sum(picked, axis=0, keepdims=True)

    @pl.when(step == 0)
    def _():
        sums_ref[...] = jnp.zeros_like(sums_ref)

    @pl.when(step < 4)
    def _():
        axis = step // 2
        mine = meta_ref[1 + axis]
        add(1 + axis, 1 + axis, mine, BOX_EDGES, BOX_SPAN - 1, (step % 2) * TILE, slice(None))

    @pl.when(step >= 4)
    def _():
        part = step - 4
        span = pl.ds(pl.multiple_of(part * half, half), half)
        mine = lax.broadcasted_iota(jnp.int32, (half, LANES), 0) + SEQ_SPAN // 4
        add(0, 3 + part, mine, SEQ_EDGES, SEQ_SPAN - 1, 0, span)

    @pl.when(step == pl.num_programs(0) - 1)
    def _():
        lanes = lax.broadcasted_iota(jnp.int32, (8, LANES), 1)
        bucket = lanes & 31
        first = jnp.where(bucket < 16, 15 - bucket, bucket)
        result = jnp.zeros((8, LANES), F32)
        for axis in range(3):
            sums = sums_ref[axis]
            part = lookup(sums, first) - jnp.where(first == 31, 0.0, lookup(sums, first + 1))
            result = jnp.where((lanes >> 5) == axis, part, result)
        out_ref[...] = result


def table_grad_sums(meta, key_meta, score_grad, deps):
    _, rows, length = score_grad.shape
    return pl.pallas_call(
        table_grad_kernel,
        grid=(6,),
        in_specs=whole(meta, key_meta, score_grad) + [HBM] * len(deps),
        out_specs=pl.BlockSpec((8, LANES), lambda s: (0, 0)),
        out_shape=shape((8, LANES), F32),
        scratch_shapes=[pltpu.VMEM((3, 8, LANES), F32)],
        compiler_params=params(),
        cost_estimate=cost(8),
        name="table_grad",
    )(meta, key_meta, score_grad, *deps)


def weight_grads_kernel(
    place_ref, query_ref, normed_ref, early_ref, gain_ref, mine_ref, got_ref, low_ref, two_ref, table_ref, *refs
):
    pair_refs, (bundle_ref, small_ref, one_ref, keep_ref, send_ref) = refs[:4], refs[4:]
    side, core = place_ref[0], place_ref[3]
    attended = jnp.concatenate(both_halves(mine_ref[...], got_ref[...], side == 0), axis=1)
    grad_out = contract_rows(attended, low_ref[...]).astype(BF16)
    total = pair_refs[0][...].astype(F32)
    for ref in pair_refs[1:]:
        total = total + ref[...].astype(F32)
    low = total.astype(BF16)
    query = query_ref[...]
    normed = normed_ref[...]
    pair = query.shape[1]
    grad_query = contract_rows(query, normed).astype(BF16)
    grad_pair = jnp.dot(low, normed, preferred_element_type=F32).astype(BF16)
    bundle_ref[:pair, :] = grad_query
    bundle_ref[pair : 3 * pair, :] = grad_pair
    bundle_ref[3 * pair : 5 * pair, :] = grad_out
    triple = jnp.concatenate([query, jnp.transpose(low)], axis=1)
    row = lax.broadcasted_iota(jnp.int32, (SMALL, LANES), 0)
    lane = lax.broadcasted_iota(jnp.int32, (8, LANES), 1)
    table = table_ref[...]
    for block in range(8):
        lanes = slice(block * LANES, (block + 1) * LANES)
        partial = contract_cols(triple, early_ref[block, :LANES, :])
        sides = both_halves(*jnp.split(partial.astype(BF16), 2, axis=0), side == 0)
        half = sides[0].shape[0] // 2
        for far in range(2):
            first, second = sides[far][:half], sides[far][half:]
            keep_ref[far, :, lanes] = jnp.where(core == 0, first, second)
            send_ref[far, :, lanes] = jnp.where(core == 0, second, first)
        one = jnp.sum(partial * normed[:, lanes].astype(F32), axis=0, keepdims=True)
        one_ref[:, lanes] = jnp.where(row == 0, one / gain_ref[0:1, lanes], 0.0).astype(BF16)
        extra = jnp.where(row == 1, two_ref[:, lanes], 0.0)
        part = lookup(table, jnp.minimum(lane + 12 * block, LANES - 1))
        for head in range(2):
            extra = jnp.where(row == 2 + head + 2 * side, part[head : head + 1], extra)
        small_ref[:, lanes] = extra.astype(BF16)


def weight_grads(place, pair_parts, query, normed, early, gains, mine, got, low, two, table):
    rows, pair = query.shape
    args = (query, normed, early, gains, mine, got, low, two, table) + tuple(pair_parts)
    half = shape((2, rows // 4, normed.shape[1]), BF16)
    small = shape((SMALL, normed.shape[1]), BF16)
    out = [shape((BUNDLE, normed.shape[1]), BF16), small, small, half, half]
    return simple(weight_grads_kernel, "weight_grads", out, args, place, micros=4)


BUNDLE = 640


def fold_bundle_kernel(parts_ref, own_ref, a_ref, b_ref, c_ref, out_ref):
    height = parts_ref.shape[1]
    for half in range(2):
        total = parts_ref[4 * half].astype(F32)
        for block in range(4 * half + 1, 4 * half + 4):
            total = total + parts_ref[block].astype(F32)
        out_ref[half * height : (half + 1) * height, :] = total.astype(BF16)
    units = own_ref[0].astype(F32)
    for ref in (a_ref, b_ref, c_ref):
        units = units + ref[...].astype(F32)
    out_ref[2 * height :, :] = units.astype(BF16)


def fold_bundle(parts, own, others):
    out = shape((2 * parts.shape[1] + own.shape[1], LANES), BF16)
    return simple(fold_bundle_kernel, "fold_bundle", out, (parts, own) + tuple(others), micros=2)


def finish_kernel(place_ref, *refs):
    parts, outs, sides = refs[:4], refs[4:-1], refs[-1]
    pair = outs[0].shape[1] // 2
    height = sides.shape[1] // 4
    block = height + SMALL
    units = (parts[0].shape[0] - 2 * block) // 3
    small = jnp.zeros((SMALL, LANES), F32)
    for hop, part in zip(HOPS, parts):
        chunk = lax.rem(place_ref[2] - hop + 4, 4)
        here = pl.ds(pl.multiple_of(chunk * height, 16), height)
        for half in range(2):
            first = half * block
            sides[half, here, :] = part[first : first + height, :].astype(F32)
            small = small + part[first + height : first + block, :].astype(F32)
        here = pl.ds(pl.multiple_of(chunk * units, 16), units)
        for at, out_ref in enumerate(outs[4:7]):
            first = 2 * block + at * units
            out_ref[here, :] = part[first : first + units, :].astype(F32)
    for half in range(2):
        cols = slice(half * pair, (half + 1) * pair)
        for at in range(3):
            outs[at][:, cols] = jnp.transpose(sides[half, at * pair : (at + 1) * pair, :])
        rows = slice((3 + half) * pair, (4 + half) * pair)
        outs[3][:, cols] = jnp.transpose(sides[0, rows, :] + sides[1, rows, :])
    outs[7][...] = small


def finish(place, parts, pair):
    units = (parts[0].shape[0] - BUNDLE // 2 - 2 * SMALL) // 3
    out = [shape((LANES, 2 * pair), F32)] * 4 + [shape((4 * units, LANES), F32)] * 3
    out = out + [shape((SMALL, LANES), F32)]
    return pl.pallas_call(
        finish_kernel,
        grid=(1,),
        in_specs=[SMEM] + whole(*parts),
        out_specs=whole(*out),
        out_shape=out,
        scratch_shapes=[pltpu.VMEM((2, BUNDLE, LANES), F32)],
        compiler_params=params(),
        cost_estimate=cost(2),
        name="finish",
    )(place, *parts)


def spread_kernel(parts_ref, small_ref, one_ref, got_ref, out_ref):
    total = parts_ref[0].astype(F32)
    for at in range(1, 4):
        total = total + parts_ref[at].astype(F32)
    small = small_ref[...].astype(F32) + one_ref[...].astype(F32) + got_ref[...].astype(F32)
    total = jnp.concatenate([total.astype(BF16), small.astype(BF16)], axis=0)
    for block in range(8):
        out_ref[block] = total[:, block * LANES : (block + 1) * LANES]


def spread(parts, small, one, one_got, deps):
    out = shape((8, parts.shape[1] + SMALL, LANES), BF16)
    return simple(spread_kernel, "spread", out, (parts, small, one, one_got), deps=deps)


def swap(values, axis_name, count, bit):
    return lax.ppermute(values, axis_name, [(at, at ^ bit) for at in range(count)])


def swap_core(values):
    return swap(values, "mp", 4, 1)


def swap_chip(values):
    return swap(values, "mp", 4, 2)


def swap_side(values):
    return swap(values, "blk", 8, 4)


def turn_z(values, hop):
    return lax.ppermute(values, "blk", [(at, at // 4 * 4 + (at - hop) % 4) for at in range(8)])


def step_dp(values, hop):
    return lax.ppermute(values, "dp", [(at, (at + hop) % 4) for at in range(4)])


def turn_dp(values):
    return [step_dp(values, hop) for hop in (1, 3, 2)]


def turn_z(values, hop):
    return lax.ppermute(values, "blk", [(at, at // 4 * 4 + (at - hop) % 4) for at in range(8)])


def spread_gather(values, axis_name, count):
    wide = jnp.broadcast_to(values[None], (count,) + values.shape)
    return lax.all_to_all(wide, axis_name, 0, 0, tiled=False)


def sum_chips(values, core, meanwhile=()):
    return join_cores(values, after(swap(values, "mp", 4, 2), meanwhile), core)


def join_cores(values, got, core):
    total = (values.astype(F32) + got.astype(F32)).astype(BF16)
    got = swap(total, "mp", 4, 1)
    first = jnp.where(core == 0, total, got)
    second = jnp.where(core == 0, got, total)
    return jnp.concatenate([first, second], axis=0)


def pick(values, at, axis):
    return lax.dynamic_index_in_dim(values, at, axis, keepdims=False)


def sum_cores(values, core):
    rows, model = values.shape
    halves = values.reshape(2, rows // 2, model)
    got = swap(pick(halves, 1 - core, 0), "mp", 4, 1)
    return (pick(halves, core, 0).astype(F32) + got.astype(F32)).astype(BF16)


def shards(
    tokens,
    cotangent,
    seg_ids,
    token_boxes,
    norm1_gain,
    w_query,
    w_key,
    w_value,
    w_out_t,
    bias_table,
    norm2_gain,
    w_gate,
    w_up,
    w_down_t,
):
    rows = tokens.shape[0]
    pair = w_query.shape[1] // 2
    blk, mp, data = lax.axis_index("blk"), lax.axis_index("mp"), lax.axis_index("dp")
    place = jnp.stack([blk // 4, blk % 4, data, mp % 2]).astype(jnp.int32)

    tokens_other = swap_side(jnp.concatenate([tokens, unfold_rows(w_out_t)], axis=0))
    table = jnp.pad(bias_table.T, ((6, 6), (0, rows - bias_table.shape[0])))
    early, late = pack(
        place,
        (
            seg_ids.reshape(1, rows),
            token_boxes,
            norm1_gain.reshape(1, LANES),
            norm2_gain.reshape(1, LANES),
            table,
        ),
        (w_query, w_key, w_value),
        (w_gate.T, w_up.T, w_down_t.T),
    )
    early_all = lax.all_to_all(early, "blk", 0, 0, tiled=False)

    turned = [turn_z(late, hop) for hop in (1, 2, 3)]
    turned, tokens_other = lax.optimization_barrier((turned, tokens_other))
    near = stack([late] + turned)
    before_near, behind_near = step_dp(near, 1), step_dp(near, 3)
    normed_one, queries, own_pairs, gains, key_meta, meta, table = project(
        place, early_all, tokens, tokens_other, w_out_t, (near,)
    )
    own_pairs, before_near, behind_near = lax.optimization_barrier(
        (own_pairs, before_near, behind_near)
    )
    pairs = lax.all_to_all(
        own_pairs, "blk", 0, 0, axis_index_groups=[[0, 1, 2, 3], [4, 5, 6, 7]]
    )
    far = swap_side(near)
    after_near = step_dp(before_near, 1)
    bias = bias_scores(place, meta, key_meta, table, ())
    probs, attn_exact, attn_mine, attn_other = attend(
        place, queries, pairs, bias, (after_near, far)
    )
    before_far, behind_far = step_dp(far, 1), step_dp(far, 3)
    after_far = step_dp(behind_far, 3)

    attn_got = swap_side(attn_other)
    keep, send = branch_part(place, attn_mine, attn_got, pairs, (before_far, behind_far))
    pieces = [near, far, before_near, before_far, behind_near, behind_far, after_near, after_far]
    ffn_w, hidden_grad = ffn_prepare(place, cotangent, pieces)
    part = add(keep, swap_core(send))
    branch = add(part, swap_chip(part), (ffn_w,))
    branch_got = swap_core(branch)
    normed_two, parts, keep, send = ffn_forward(
        place, tokens, branch, branch_got, gains, hidden_grad, ffn_w
    )
    part = add(keep, swap_core(send))
    ffn_grads = ffn_back(place, parts, normed_two, cotangent, (part,))
    grad = add(part, swap_chip(part), (ffn_grads,))
    middle_grad, branch_low, gain_two_grad, grad_mine, grad_other = middle_back(
        place, tokens, branch, branch_got, cotangent, gains, grad, swap_core(grad), pairs
    )
    ffn_grads = lax.all_to_all(ffn_grads, "dp", 0, 0, tiled=False)
    keep, send = ffn_output(place, parts, ffn_w, (grad_other,))
    out_part = add(keep, swap_core(send))
    out_got = swap_chip(out_part)
    score_grad, *pair_grads, query_low = attend_back(
        place, queries, grad_mine, swap_side(grad_other), attn_exact, pairs, probs, (out_part,)
    )
    pair_parts = pair_grads[:1] + [turn_z(pair_grads[hop], -hop) for hop in (1, 2, 3)]
    table_grad = table_grad_sums(meta, key_meta, score_grad, (out_got,))
    bundle, small, one, keep, send = weight_grads(
        place,
        pair_parts,
        query_low,
        normed_one,
        early_all,
        gains,
        attn_mine,
        attn_got,
        branch_low,
        gain_two_grad,
        table_grad,
    )
    bundle = bundle.reshape(4, BUNDLE // 4, -1)
    bundle = lax.all_to_all(bundle, "dp", 0, 0, tiled=False)
    ffn_parts = fold_to_blocks(place, ffn_grads, (send,))
    ffn_near = add(ffn_parts[0], swap_side(ffn_parts[1]))
    one = add(one, swap_core(one))
    bundle = spread(bundle, small, one, swap_chip(one), (ffn_near,))
    bundle = lax.all_to_all(bundle, "blk", 0, 0, tiled=False)
    ffn_turned = [turn_z(ffn_near[hop], -hop) for hop in (1, 2, 3)]
    folded = fold_bundle(bundle, ffn_near, ffn_turned)
    grad_query, grad_key, grad_value, grad_out, *ffn_final, small = finish(
        place, [folded] + turn_dp(folded), pair
    )

    part = add(keep, swap_core(send))
    part = add(part[0], swap_side(part[1]))
    grad = add(part, swap_chip(part))
    tokens_grad = tokens_back(place, tokens, gains, grad, swap_core(grad), middle_grad)

    out_sum = add(out_part, out_got, (ffn_near,))
    mixed = simple(
        mixed_kernel,
        "mixed",
        shape(tokens.shape, BF16),
        (tokens, branch, branch_got, out_sum, swap_core(out_sum)),
        place,
    )

    return (
        mixed,
        tokens_grad,
        small[0],
        grad_query,
        grad_key,
        grad_value,
        grad_out,
        small[2:6, :12].T,
        small[1],
        ffn_final[0].T,
        ffn_final[1].T,
        ffn_final[2].T,
    )


def solution(mesh):
    rows = P(("dp", "blk"), None)
    weight = P("blk", "mp")
    in_specs = (
        rows,
        rows,
        P(("dp", "blk")),
        P(None, ("dp", "blk")),
        P("blk"),
        weight,
        weight,
        weight,
        weight,
        weight,
        P("blk"),
        weight,
        weight,
        weight,
    )
    out_specs = (
        rows,
        rows,
        P("blk"),
        weight,
        weight,
        weight,
        weight,
        weight,
        P("blk"),
        weight,
        weight,
        weight,
    )
    return jax.shard_map(shards, mesh=mesh, in_specs=in_specs, out_specs=out_specs, check_vma=False)
```

time: 369 us -> 244 us (0.66)
  waiting for transfers between devices: 151 us -> 60.1 us
  starting transfers between devices: 38.4 us -> 80.5 us
  blocking collectives: 33.4 us -> 0 us
  Pallas kernels: 64.6 us -> 81.9 us
  other arithmetic: 19.8 us -> 2.52 us
  local copies, waits for them, and re-layouts: 30.8 us -> 15.7 us
  matrix products: 14.9 us -> 0 us
  between operations: 14.5 us -> 1.25 us
    all_to_all x4 -> x5, waiting for transfers between devices: 81.8 us -> 0.01 us  [the longest x1 0.01 us: shards(): lax.all_to_all(own_pairs, 'blk', 0, 0, axis_index_groups=[[0, 1, 2, 3], [...]
    psum x1 -> x0, waiting for transfers between devices: 35.3 us -> none  [shards(): ffn_final = lax.psum(ffn_part, 'dp').astype(F32)]
    all_to_all x1 -> x0, blocking collectives: 33.4 us -> none  [shards(): lax.all_to_all(bundle.reshape(blocks, LANES, -1), 'blk', 0, 0, tiled=False)]
    ppermute x3 -> x18, starting transfers between devices: 3.9 us -> 32.2 us  [the longest x9 17.4 us: turn_z(): lax.ppermute(values, 'blk', [(at, at // 4 * 4 + (at - hop) % 4) for at in...]
    pallas_call x4 -> x31, Pallas kernels: 64.6 us -> 81.9 us  [the longest x20 18.9 us: simple(): pl.pallas_call(body, grid=(1,), in_specs=[SMEM] * (place is not None) + w...]
    ppermute x3 -> x18, waiting for transfers between devices: 11.6 us -> 27.5 us  [the longest x9 18.7 us: turn_z(): lax.ppermute(values, 'blk', [(at, at // 4 * 4 + (at - hop) % 4) for at in...]
    dot_general x15 -> x0, matrix products: 14.9 us -> none  [the longest x5 4.84 us: contract_cols(): lax.dot_general(left, right, (((1,), (1,)), ((), ())), preferred_element_...]
    ppermute x14 -> x20, waiting for transfers between devices: 22.5 us -> 32.6 us  [swap(): lax.ppermute(values, axis_name, [(at, at ^ bit) for at in range(count)])]
  transfers between devices with their start and end apart: 24 -> 43, of which waited for: 15 -> 19; matrix products, arithmetic and copies ran while one was open for 13% -> 1% of each run, Pallas kernels for 18% -> 30%
where the time goes in v2:
time: 244 us; the launch traced here: 242 us
  Pallas kernels  81.9 us (34%)
  starting transfers between devices  80.5 us (33%)
  waiting for transfers between devices  60.1 us (25%)
  local copies, waits for them, and re-layouts  15.7 us (6%)
  other arithmetic  2.52 us (1%)
    ppermute x20, waiting for transfers between devices, swap(): lax.ppermute(values, axis_name, [(at, at ^ bit) for at in range(count)])  32.6 us
    ppermute x20, starting transfers between devices, swap(): lax.ppermute(values, axis_name, [(at, at ^ bit) for at in range(count)])  25.3 us
    pallas_call x20, Pallas kernels, simple(): pl.pallas_call(body, grid=(1,), in_specs=[SMEM] * (place is not None) + w...  18.9 us
    ppermute x9, waiting for transfers between devices, turn_z(): lax.ppermute(values, 'blk', [(at, at // 4 * 4 + (at - hop) % 4) for at in...  18.7 us
    ppermute x9, starting transfers between devices, turn_z(): lax.ppermute(values, 'blk', [(at, at // 4 * 4 + (at - hop) % 4) for at in...  17.4 us
    ppermute x9, starting transfers between devices, step_dp(): return lax.ppermute(values, 'dp', [(at, (at + hop) % 4) for at in range(4)])  14.9 us
    pallas_call x1, Pallas kernels, table_grad_sums(): pl.pallas_call(table_grad_kernel, grid=(6,), in_specs=whole(meta, key_met...  14.8 us
    unnamed x78, local copies, waits for them, and re-layouts  13.1 us
  transfers between devices with their start and end apart: 43, of which 19 were waited for; matrix products, arithmetic and copies ran while one was open for 1% of the time, Pallas kernels for 30%

profile of v2, /device:TPU:0, one launch (start us, length us, event | category | flops | bytes accessed | tf_op | source)
XLA Modules:
  0.0 242.0 jit_solution(14168472608465397189)
XLA Ops:
  9.1 5.5 %all-to-all-start = ((bf16[8,144,384]{2,1,0:T(8,128)(2,1)}), bf16[8,144,384]{2,1,0:T(8,128)(2,1)S(1)}, u32[]{:S(2)}, u32[]{:S(2)}) async-start(bf16[8,144,384]{2,1,0:T(8,128)(2,1)} %get-tuple-element.66), calls=%async_computation | async-start | bytes 1769472 | tf_op jit(solution)/shard_map/all_to_all | solution.py:1147
  14.5 3.2 %collective-permute-start = (bf16[528,128]{1,0:T(8,128)(2,1)S(1)}, bf16[528,128]{1,0:T(8,128)(2,1)S(1)}, u32[]{:S(2)}, u32[]{:S(2)}) collective-permute-start(bf16[528,128]{1,0:T(8,128)(2,1)S(1)} %copy-done.9), channel_id=1, source_target_pairs={{0,12},{4,0},{8,4},{12,8},{16,28},{20,16},{24,20},{28,24},{1,13},{... | collective-permute-start | bytes 405512 | tf_op jit(solution)/shard_map/ppermute | solution.py:1081
  19.5 10.9 %collective-permute-done.refs_1_ = bf16[528,128]{1,0:T(8,128)(2,1)S(1)} collective-permute-done((bf16[528,128]{1,0:T(8,128)(2,1)S(1)}, bf16[528,128]{1,0:T(8,128)(2,1)S(1)}, u32[]{:S(2)}, u32[]{:S(2)}) %collective-permute-start) | collective-permute-done | bytes 135200 | tf_op jit(solution)/shard_map/ppermute | solution.py:1081
  37.9 3.4 %project.1 = (bf16[512,1024]{1,0:T(8,128)(2,1)S(1)}, bf16[512,128]{1,0:T(8,128)(2,1)S(1)}, bf16[4,768,256]{2,1,0:T(8,128)(2,1)}, f32[2,1024]{1,0:T(2,128)S(1)}, ...) custom-call(s32[4]{0:T(128)S(1)} %copy-done.10, ...), custom_call_target="tpu_custom_call" | custom-call | flops 55000000 | bytes 5000 | tf_op jit(solution)/shard_map/project/pallas_call | solution.py:41
  42.9 5.2 %collective-permute-done.4.refs_2_ = bf16[4,528,128]{2,1,0:T(8,128)(2,1)S(1)} collective-permute-done((bf16[4,528,128]{2,1,0:T(8,128)(2,1)S(1)}, bf16[4,528,128]{2,1,0:T(8,128)(2,1)S(1)}, u32[]{:S(2)}, u32[]{:S(2)}) %collective-permute-start.4) | collective-permute-done | bytes 540704 | tf_op jit(solution)/shard_map/ppermute | solution.py:1073
  48.2 4.5 %all-to-all-start.1 = ((bf16[4,768,256]{2,1,0:T(8,128)(2,1)}), bf16[4,768,256]{2,1,0:T(8,128)(2,1)}, u32[]{:S(2)}, u32[]{:S(2)}) async-start(bf16[4,768,256]{2,1,0:T(8,128)(2,1)} %get-tuple-element.77), calls=%async_computation.1 | async-start | bytes 3145728 | tf_op jit(solution)/shard_map/all_to_all | solution.py:1159
  56.0 10.5 %bias_scores.1.bias_ref = s32[512,2048]{1,0:T(8,128)S(1)} custom-call(s32[4]{0:T(128)S(1)} %copy-done.10, s32[3,512,128]{2,1,0:T(8,128)S(1)} %get-tuple-element.73.meta_ref, s32[8,2048]{1,0:T(8,128)S(1)} %copy-done.20, f32[8,128]{1,0:T(8,128)S(1)} %get-tuple-element.75.table_ref), custom_call_target="tpu_custom_call" | custom-call | flops 11000000512 | bytes 1000000 | tf_op jit(solution)/shard_map/bias_scores/pallas_call | solution.py:348
  75.9 8.3 %attend.1 = (bf16[2,512,2048]{2,1,0:T(8,128)(2,1)S(1)}, f32[512,128]{1,0:T(8,128)S(1)}, bf16[256,128]{1,0:T(8,128)(2,1)S(1)}, bf16[256,128]{1,0:T(8,128)(2,1)S(1)}) custom-call(s32[4]{0:T(128)S(1)} %copy-done.10, bf16[512,128]{1,0:T(8,128)(2,1)S(1)} %get-tuple-element.72.query_ref, s32[512,2048]{1,0:T(8,128)S(1)} %copy-done.31, ...), custom_call_target="tpu_custom_call" | custom-call | flops 9900000256 | bytes 900000 | tf_op jit(solution)/shard_map/attend/pallas_call | solution.py:430
  92.1 3.2 %collective-permute-start.12 = (bf16[128,1024]{1,0:T(8,128)(2,1)S(1)}, bf16[128,1024]{1,0:T(8,128)(2,1)S(1)}, u32[]{:S(2)}, u32[]{:S(2)}) collective-permute-start(bf16[128,1024]{1,0:T(8,128)(2,1)S(1)} %add.29.refs_0_), channel_id=1, source_target_pairs={{0,2},{1,3},{2,0},{3,1},{4,6},{5,7},{6,4},{7,5},{8,10},{9,11},{10,... | collective-permute-start | bytes 786440 | tf_op jit(solution)/shard_map/ppermute | solution.py:1053
  95.3 3.9 %ffn_prepare.1 = (bf16[4,528,1024]{2,1,0:T(8,128)(2,1)S(1)}, f32[4,176,256]{2,1,0:T(8,128)S(1)}) custom-call(s32[4]{0:T(128)S(1)} %copy-done.10, bf16[256,1024]{1,0:T(8,128)(2,1)S(1)} %copy-done.17, bf16[4,528,128]{2,1,0:T(8,128)(2,1)S(1)} %stack.21.refs_5_.refs_0_, bf16[4,528,128]{2,1,0:T(8,128)(2,1)} %collective-permute-done.7.refs_1_, ...), custom_call_target="tpu_custom_call" | custom-call | flops 4400000000 | bytes 400000 | tf_op jit(solution)/shard_map/ffn_prepare/pallas_call | solution.py:514
  103.9 5.7 %ffn_forward.1 = (bf16[256,1024]{1,0:T(8,128)(2,1)S(1)}, bf16[4,528,256]{2,1,0:T(8,128)(2,1)S(1)}, bf16[128,1024]{1,0:T(8,128)(2,1)S(1)}, bf16[128,1024]{1,0:T(8,128)(2,1)S(1)}) custom-call(s32[4]{0:T(128)S(1)} %copy-done.10, bf16[256,1024]{1,0:T(8,128)(2,1)S(1)} %copy-done.2, bf16[128,1024]{1,0:T(8,128)(2,1)S(1)} %add.30.total_ref.refs_2_, ...), custom_call_target="tpu_custom_call" | custom-call | flops 5500000256 | bytes 500000 | tf_op jit(solution)/shard_map/ffn_forward/pallas_call | solution.py:573
  116.7 5.0 %all-to-all-start.2 = ((bf16[4,528,1024]{2,1,0:T(8,128)(2,1)}), bf16[4,528,1024]{2,1,0:T(8,128)(2,1)}, u32[]{:S(2)}, u32[]{:S(2)}) async-start(bf16[4,528,1024]{2,1,0:T(8,128)(2,1)} %copy-done), calls=%async_computation.2 | async-start | bytes 8650752 | tf_op jit(solution)/shard_map/all_to_all | solution.py:1187
  121.8 3.2 %collective-permute-start.16 = (bf16[128,1024]{1,0:T(8,128)(2,1)S(1)}, bf16[128,1024]{1,0:T(8,128)(2,1)S(1)}, u32[]{:S(2)}, u32[]{:S(2)}) collective-permute-start(bf16[128,1024]{1,0:T(8,128)(2,1)S(1)} %add.31.refs_0_), channel_id=1, source_target_pairs={{0,2},{1,3},{2,0},{3,1},{4,6},{5,7},{6,4},{7,5},{8,10},{9,11},{10,... | collective-permute-start | bytes 786440 | tf_op jit(solution)/shard_map/ppermute | solution.py:1053
  124.9 6.8 %collective-permute-done.16.refs_1_ = bf16[128,1024]{1,0:T(8,128)(2,1)S(1)} collective-permute-done((bf16[128,1024]{1,0:T(8,128)(2,1)S(1)}, bf16[128,1024]{1,0:T(8,128)(2,1)S(1)}, u32[]{:S(2)}, u32[]{:S(2)}) %collective-permute-start.16) | collective-permute-done | bytes 262176 | tf_op jit(solution)/shard_map/ppermute | solution.py:1053
  142.2 3.1 %collective-permute-start.19 = (bf16[128,1024]{1,0:T(8,128)(2,1)S(1)}, bf16[128,1024]{1,0:T(8,128)(2,1)S(1)}, u32[]{:S(2)}, u32[]{:S(2)}) collective-permute-start(bf16[128,1024]{1,0:T(8,128)(2,1)S(1)} %add.33.refs_0_), channel_id=1, source_target_pairs={{0,2},{1,3},{2,0},{3,1},{4,6},{5,7},{6,4},{7,5},{8,10},{9,11},{10,... | collective-permute-start | bytes 786440 | tf_op jit(solution)/shard_map/ppermute | solution.py:1053
  145.3 7.4 %attend_back.1 = (bf16[2,512,2048]{2,1,0:T(8,128)(2,1)S(1)}, bf16[256,512]{1,0:T(8,128)(2,1)S(1)}, bf16[256,512]{1,0:T(8,128)(2,1)S(1)}, bf16[256,512]{1,0:T(8,1...) custom-call(s32[4]{0:T(128)S(1)} %copy-done.10, ...), custom_call_target="tpu_custom_call" | custom-call | flops 4400000000 | bytes 400000 | tf_op jit(solution)/shard_map/attend_back/pallas_call | solution.py:821
  159.1 14.8 %table_grad.1.refs_9_ = f32[8,128]{1,0:T(8,128)S(1)} custom-call(s32[3,512,128]{2,1,0:T(8,128)S(1)} %copy-done.14, s32[8,2048]{1,0:T(8,128)S(1)} %copy-done.21, bf16[2,512,2048]{2,1,0:T(8,128)(2,1)S(1)} %get-tuple-element.101.score_ref, bf16[128,1024]{1,0:T(8,128)(2,1)S(1)} %collective-permute-done.19.refs_0_.refs_1_), custom_call_target="tpu_custom_call" | custom-call | flops 8800000000 | bytes 800000 | tf_op jit(solution)/shard_map/table_grad/pallas_call | solution.py:909
  174.0 3.4 %weight_grads.1 = (bf16[640,1024]{1,0:T(8,128)(2,1)}, bf16[16,1024]{1,0:T(8,128)(2,1)S(1)}, bf16[16,1024]{1,0:T(8,128)(2,1)S(1)}, bf16[2,128,1024]{2,1,0:T(8,128)(2,1)S(1)}, bf16[2,128,1024]{2,1,0:T(8,128)(2,1)}) custom-call(s32[4]{0:T(128)S(1)} %copy-done.10, bf16[512,128]{1,0:T(8,128)(2,1)S(1)} %get-tuple-element.97.refs_1_, ...), custom_call_target="tpu_custom_call" | custom-call | flops 4400000000 | bytes 400000 | tf_op jit(solution)/shard_map/weight_grads/pallas_call | solution.py:41
  177.4 4.4 %all-to-all-start.3 = ((bf16[4,160,1024]{2,1,0:T(8,128)(2,1)}), bf16[4,160,1024]{2,1,0:T(8,128)(2,1)S(1)}, u32[]{:S(2)}, u32[]{:S(2)}) async-start(bf16[4,160,1024]{2,1,0:T(8,128)(2,1)} %bitcast.15), calls=%async_computation.3 | async-start | bytes 2621440 | tf_op jit(solution)/shard_map/all_to_all | solution.py:1210
  181.7 3.1 %fold_to_blocks.1 = bf16[2,4,528,128]{3,2,1,0:T(8,128)(2,1)S(1)} custom-call(s32[4]{0:T(128)S(1)} %copy-done.10, bf16[4,528,1024]{2,1,0:T(8,128)(2,1)} %all-to-all-done.2.parts_ref, bf16[2,128,1024]{2,1,0:T(8,128)(2,1)} %get-tuple-element.106.refs_0_), custom_call_target="tpu_custom_call" | custom-call | flops 4400000000 | bytes 400000 | tf_op jit(solution)/shard_map/fold_to_blocks/pallas_call | solution.py:739
  192.5 12.9 %collective-permute-done.27.refs_1_ = bf16[128,1024]{1,0:T(8,128)(2,1)S(1)} collective-permute-done((bf16[128,1024]{1,0:T(8,128)(2,1)S(1)}, bf16[128,1024]{1,0:T(8,128)(2,1)S(1)}, u32[]{:S(2)}, u32[]{:S(2)}) %collective-permute-start.27) | collective-permute-done | bytes 262176 | tf_op jit(solution)/shard_map/ppermute | solution.py:1053
  205.5 3.1 %collective-permute-start.28 = (bf16[128,1024]{1,0:T(8,128)(2,1)S(1)}, bf16[128,1024]{1,0:T(8,128)(2,1)}, u32[]{:S(2)}, u32[]{:S(2)}) collective-permute-start(bf16[128,1024]{1,0:T(8,128)(2,1)S(1)} %add.37.refs_0_), channel_id=1, source_target_pairs={{0,2},{1,3},{2,0},{3,1},{4,6},{5,7},{6,4},{7,5},{8,10},{9,11},{10,... | collective-permute-start | bytes 786440 | tf_op jit(solution)/shard_map/ppermute | solution.py:1053
  209.7 3.6 %all-to-all-start.4 = ((bf16[8,176,128]{2,1,0:T(8,128)(2,1)}), bf16[8,176,128]{2,1,0:T(8,128)(2,1)S(1)}, u32[]{:S(2)}, u32[]{:S(2)}) async-start(bf16[8,176,128]{2,1,0:T(8,128)(2,1)} %spread.1), calls=%async_computation.4 | async-start | bytes 720896 | tf_op jit(solution)/shard_map/all_to_all | solution.py:1215
  221.2 3.1 %collective-permute-done.32.refs_2_ = bf16[528,128]{1,0:T(8,128)(2,1)S(1)} collective-permute-done((bf16[528,128]{1,0:T(8,128)(2,1)S(1)}, bf16[528,128]{1,0:T(8,128)(2,1)S(1)}, u32[]{:S(2)}, u32[]{:S(2)}) %collective-permute-start.32) | collective-permute-done | bytes 135200 | tf_op jit(solution)/shard_map/ppermute | solution.py:1081
  (181 shorter events, 102.6 us)
Async XLA Ops:
  3.4 29.7 %collective-permute-start.3 = (bf16[288,1024]{1,0:T(8,128)(2,1)}, bf16[288,1024]{1,0:T(8,128)(2,1)}, u32[]{:S(2)}, u32[]{:S(2)}) collective-permute-start(bf16[288,1024]{1,0:T(8,128)(2,1)} %maximum_maximum_fusion), channel_id=1, source_target_pairs={{0,16},{4,20},{8,24},{12,28},{16,0},{20,4},{24,8},{28,12},{1,17},{... | collective-permute-start | bytes 1769480 | tf_op jit(solution)/shard_map/ppermute | solution.py:1053
  9.1 28.8 %all-to-all-start = ((bf16[8,144,384]{2,1,0:T(8,128)(2,1)}), bf16[8,144,384]{2,1,0:T(8,128)(2,1)S(1)}, u32[]{:S(2)}, u32[]{:S(2)}) async-start(bf16[8,144,384]{2,1,0:T(8,128)(2,1)} %get-tuple-element.66), calls=%async_computation | async-start | bytes 1769472 | tf_op jit(solution)/shard_map/all_to_all | solution.py:1147
  14.5 15.9 %collective-permute-start = (bf16[528,128]{1,0:T(8,128)(2,1)S(1)}, bf16[528,128]{1,0:T(8,128)(2,1)S(1)}, u32[]{:S(2)}, u32[]{:S(2)}) collective-permute-start(bf16[528,128]{1,0:T(8,128)(2,1)S(1)} %copy-done.9), channel_id=1, source_target_pairs={{0,12},{4,0},{8,4},{12,8},{16,28},{20,16},{24,20},{28,24},{1,13},{... | collective-permute-start | bytes 405512 | tf_op jit(solution)/shard_map/ppermute | solution.py:1081
  17.8 14.2 %collective-permute-start.1 = (bf16[528,128]{1,0:T(8,128)(2,1)S(1)}, bf16[528,128]{1,0:T(8,128)(2,1)S(1)}, u32[]{:S(2)}, u32[]{:S(2)}) collective-permute-start(bf16[528,128]{1,0:T(8,128)(2,1)S(1)} %copy-done.9), channel_id=1, source_target_pairs={{0,8},{4,12},{8,0},{12,4},{16,24},{20,28},{24,16},{28,20},{1,9},{5... | collective-permute-start | bytes 405512 | tf_op jit(solution)/shard_map/ppermute | solution.py:1081
  18.6 14.5 %collective-permute-start.2 = (bf16[528,128]{1,0:T(8,128)(2,1)S(1)}, bf16[528,128]{1,0:T(8,128)(2,1)S(1)}, u32[]{:S(2)}, u32[]{:S(2)}) collective-permute-start(bf16[528,128]{1,0:T(8,128)(2,1)S(1)} %copy-done.9), channel_id=1, source_target_pairs={{0,4},{4,8},{8,12},{12,0},{16,20},{20,24},{24,28},{28,16},{1,5},{5... | collective-permute-start | bytes 405512 | tf_op jit(solution)/shard_map/ppermute | solution.py:1081
  33.1 15.0 %collective-permute-start.4 = (bf16[4,528,128]{2,1,0:T(8,128)(2,1)S(1)}, bf16[4,528,128]{2,1,0:T(8,128)(2,1)S(1)}, u32[]{:S(2)}, u32[]{:S(2)}) collective-permute-start(bf16[4,528,128]{2,1,0:T(8,128)(2,1)S(1)} %stack.21.refs_5_.refs_0_), channel_id=1, source_target_pairs={{0,32},{32,64},{64,96},{96,0},{1,33},{33,65},{65,97},{97,1},{2,34}... | collective-permute-start | bytes 1622024 | tf_op jit(solution)/shard_map/ppermute | solution.py:1073
  34.7 13.5 %collective-permute-start.5 = (bf16[4,528,128]{2,1,0:T(8,128)(2,1)S(1)}, bf16[4,528,128]{2,1,0:T(8,128)(2,1)}, u32[]{:S(2)}, u32[]{:S(2)}) collective-permute-start(bf16[4,528,128]{2,1,0:T(8,128)(2,1)S(1)} %stack.21.refs_5_.refs_0_), channel_id=1, source_target_pairs={{0,96},{32,0},{64,32},{96,64},{1,97},{33,1},{65,33},{97,65},{2,98}... | collective-permute-start | bytes 1622024 | tf_op jit(solution)/shard_map/ppermute | solution.py:1073
  36.4 17.8 %collective-permute-start.7 = (bf16[4,528,128]{2,1,0:T(8,128)(2,1)S(1)}, bf16[4,528,128]{2,1,0:T(8,128)(2,1)}, u32[]{:S(2)}, u32[]{:S(2)}) collective-permute-start(bf16[4,528,128]{2,1,0:T(8,128)(2,1)S(1)} %stack.21.refs_5_.refs_0_), channel_id=1, source_target_pairs={{0,16},{4,20},{8,24},{12,28},{16,0},{20,4},{24,8},{28,12},{1,17},{... | collective-permute-start | bytes 1622024 | tf_op jit(solution)/shard_map/ppermute | solution.py:1053
  48.2 24.4 %all-to-all-start.1 = ((bf16[4,768,256]{2,1,0:T(8,128)(2,1)}), bf16[4,768,256]{2,1,0:T(8,128)(2,1)}, u32[]{:S(2)}, u32[]{:S(2)}) async-start(bf16[4,768,256]{2,1,0:T(8,128)(2,1)} %get-tuple-element.77), calls=%async_computation.1 | async-start | bytes 3145728 | tf_op jit(solution)/shard_map/all_to_all | solution.py:1159
  52.7 19.0 %collective-permute-start.6 = (bf16[4,528,128]{2,1,0:T(8,128)(2,1)S(1)}, bf16[4,528,128]{2,1,0:T(8,128)(2,1)S(1)}, u32[]{:S(2)}, u32[]{:S(2)}) collective-permute-start(bf16[4,528,128]{2,1,0:T(8,128)(2,1)S(1)} %collective-permute-done.4.refs_2_), channel_id=1, source_target_pairs={{0,32},{32,64},{64,96},{96,0},{1,33},{33,65},{65,97},{97,1},{2,34}... | collective-permute-start | bytes 1622024 | tf_op jit(solution)/shard_map/ppermute | solution.py:1073
  54.3 14.5 %collective-permute-start.10 = (bf16[4,528,128]{2,1,0:T(8,128)(2,1)}, bf16[4,528,128]{2,1,0:T(8,128)(2,1)}, u32[]{:S(2)}, u32[]{:S(2)}) collective-permute-start(bf16[4,528,128]{2,1,0:T(8,128)(2,1)} %collective-permute-done.7.refs_1_), channel_id=1, source_target_pairs={{0,96},{32,0},{64,32},{96,64},{1,97},{33,1},{65,33},{97,65},{2,98}... | collective-permute-start | bytes 1622024 | tf_op jit(solution)/shard_map/ppermute | solution.py:1073
  68.5 17.3 %collective-permute-start.9 = (bf16[4,528,128]{2,1,0:T(8,128)(2,1)}, bf16[4,528,128]{2,1,0:T(8,128)(2,1)S(1)}, u32[]{:S(2)}, u32[]{:S(2)}) collective-permute-start(bf16[4,528,128]{2,1,0:T(8,128)(2,1)} %collective-permute-done.7.refs_1_), channel_id=1, source_target_pairs={{0,32},{32,64},{64,96},{96,0},{1,33},{33,65},{65,97},{97,1},{2,34}... | collective-permute-start | bytes 1622024 | tf_op jit(solution)/shard_map/ppermute | solution.py:1073
  68.8 26.5 %collective-permute-start.13 = (bf16[4,528,128]{2,1,0:T(8,128)(2,1)}, bf16[4,528,128]{2,1,0:T(8,128)(2,1)}, u32[]{:S(2)}, u32[]{:S(2)}) collective-permute-start(bf16[4,528,128]{2,1,0:T(8,128)(2,1)} %collective-permute-done.10.refs_5_), channel_id=1, source_target_pairs={{0,96},{32,0},{64,32},{96,64},{1,97},{33,1},{65,33},{97,65},{2,98}... | collective-permute-start | bytes 1622024 | tf_op jit(solution)/shard_map/ppermute | solution.py:1073
  116.7 60.6 %all-to-all-start.2 = ((bf16[4,528,1024]{2,1,0:T(8,128)(2,1)}), bf16[4,528,1024]{2,1,0:T(8,128)(2,1)}, u32[]{:S(2)}, u32[]{:S(2)}) async-start(bf16[4,528,1024]{2,1,0:T(8,128)(2,1)} %copy-done), calls=%async_computation.2 | async-start | bytes 8650752 | tf_op jit(solution)/shard_map/all_to_all | solution.py:1187
  142.2 16.9 %collective-permute-start.19 = (bf16[128,1024]{1,0:T(8,128)(2,1)S(1)}, bf16[128,1024]{1,0:T(8,128)(2,1)S(1)}, u32[]{:S(2)}, u32[]{:S(2)}) collective-permute-start(bf16[128,1024]{1,0:T(8,128)(2,1)S(1)} %add.33.refs_0_), channel_id=1, source_target_pairs={{0,2},{1,3},{2,0},{3,1},{4,6},{5,7},{6,4},{7,5},{8,10},{9,11},{10,... | collective-permute-start | bytes 786440 | tf_op jit(solution)/shard_map/ppermute | solution.py:1053
  152.8 21.1 %collective-permute-start.21 = (bf16[256,512]{1,0:T(8,128)(2,1)S(1)}, bf16[256,512]{1,0:T(8,128)(2,1)S(1)}, u32[]{:S(2)}, u32[]{:S(2)}) collective-permute-start(bf16[256,512]{1,0:T(8,128)(2,1)S(1)} %get-tuple-element.103), channel_id=1, source_target_pairs={{0,4},{4,8},{8,12},{12,0},{16,20},{20,24},{24,28},{28,16},{1,5},{5... | collective-permute-start | bytes 786440 | tf_op jit(solution)/shard_map/ppermute | solution.py:1081
  154.9 19.0 %collective-permute-start.22 = (bf16[256,512]{1,0:T(8,128)(2,1)S(1)}, bf16[256,512]{1,0:T(8,128)(2,1)S(1)}, u32[]{:S(2)}, u32[]{:S(2)}) collective-permute-start(bf16[256,512]{1,0:T(8,128)(2,1)S(1)} %get-tuple-element.104), channel_id=1, source_target_pairs={{0,8},{4,12},{8,0},{12,4},{16,24},{20,28},{24,16},{28,20},{1,9},{5... | collective-permute-start | bytes 786440 | tf_op jit(solution)/shard_map/ppermute | solution.py:1081
  157.4 16.5 %collective-permute-start.23 = (bf16[256,512]{1,0:T(8,128)(2,1)S(1)}, bf16[256,512]{1,0:T(8,128)(2,1)S(1)}, u32[]{:S(2)}, u32[]{:S(2)}) collective-permute-start(bf16[256,512]{1,0:T(8,128)(2,1)S(1)} %get-tuple-element.105), channel_id=1, source_target_pairs={{0,12},{4,0},{8,4},{12,8},{16,28},{20,16},{24,20},{28,24},{1,13},{... | collective-permute-start | bytes 786440 | tf_op jit(solution)/shard_map/ppermute | solution.py:1081
  177.4 31.3 %all-to-all-start.3 = ((bf16[4,160,1024]{2,1,0:T(8,128)(2,1)}), bf16[4,160,1024]{2,1,0:T(8,128)(2,1)S(1)}, u32[]{:S(2)}, u32[]{:S(2)}) async-start(bf16[4,160,1024]{2,1,0:T(8,128)(2,1)} %bitcast.15), calls=%async_computation.3 | async-start | bytes 2621440 | tf_op jit(solution)/shard_map/all_to_all | solution.py:1210
  184.9 23.6 %collective-permute-start.24 = (bf16[4,528,128]{2,1,0:T(8,128)(2,1)S(1)}, bf16[4,528,128]{2,1,0:T(8,128)(2,1)S(1)}, u32[]{:S(2)}, u32[]{:S(2)}) collective-permute-start(bf16[4,528,128]{2,1,0:T(8,128)(2,1)S(1)} %get-tuple-element.120), channel_id=1, source_target_pairs={{0,16},{4,20},{8,24},{12,28},{16,0},{20,4},{24,8},{28,12},{1,17},{... | collective-permute-start | bytes 1622024 | tf_op jit(solution)/shard_map/ppermute | solution.py:1053
  187.3 18.0 %collective-permute-start.27 = (bf16[128,1024]{1,0:T(8,128)(2,1)S(1)}, bf16[128,1024]{1,0:T(8,128)(2,1)S(1)}, u32[]{:S(2)}, u32[]{:S(2)}) collective-permute-start(bf16[128,1024]{1,0:T(8,128)(2,1)S(1)} %get-tuple-element.125), channel_id=1, source_target_pairs={{0,16},{4,20},{8,24},{12,28},{16,0},{20,4},{24,8},{28,12},{1,17},{... | collective-permute-start | bytes 786440 | tf_op jit(solution)/shard_map/ppermute | solution.py:1053
  189.6 19.1 %collective-permute-start.31 = (bf16[16,1024]{1,0:T(8,128)(2,1)S(1)}, bf16[16,1024]{1,0:T(8,128)(2,1)S(1)}, u32[]{:S(2)}, u32[]{:S(2)}) collective-permute-start(bf16[16,1024]{1,0:T(8,128)(2,1)S(1)} %add.39.refs_2_), channel_id=1, source_target_pairs={{0,2},{1,3},{2,0},{3,1},{4,6},{5,7},{6,4},{7,5},{8,10},{9,11},{10,... | collective-permute-start | bytes 98312 | tf_op jit(solution)/shard_map/ppermute | solution.py:1053
  205.5 14.0 %collective-permute-start.28 = (bf16[128,1024]{1,0:T(8,128)(2,1)S(1)}, bf16[128,1024]{1,0:T(8,128)(2,1)}, u32[]{:S(2)}, u32[]{:S(2)}) collective-permute-start(bf16[128,1024]{1,0:T(8,128)(2,1)S(1)} %add.37.refs_0_), channel_id=1, source_target_pairs={{0,2},{1,3},{2,0},{3,1},{4,6},{5,7},{6,4},{7,5},{8,10},{9,11},{10,... | collective-permute-start | bytes 786440 | tf_op jit(solution)/shard_map/ppermute | solution.py:1053
  209.7 16.5 %all-to-all-start.4 = ((bf16[8,176,128]{2,1,0:T(8,128)(2,1)}), bf16[8,176,128]{2,1,0:T(8,128)(2,1)S(1)}, u32[]{:S(2)}, u32[]{:S(2)}) async-start(bf16[8,176,128]{2,1,0:T(8,128)(2,1)} %spread.1), calls=%async_computation.4 | async-start | bytes 720896 | tf_op jit(solution)/shard_map/all_to_all | solution.py:1215
  (58 other events, 477.4 us)

commit v3 on v2

--- a/solution.py
+++ b/solution.py
@@ -16,6 +16,7 @@
 LANES = 128
 MIB = 2**20
 VMEM_MIB = 32
+PREP = 10
 SMEM = pl.BlockSpec(memory_space=pltpu.SMEM)
 
 
@@ -30,7 +31,7 @@
 HBM = pl.BlockSpec(memory_space=pl.ANY)
 
 
-def simple(kernel, name, out, args, place=None, deps=(), micros=0.05):
+def simple(kernel, name, out, args, place=None, deps=(), micros=0.05, mib=VMEM_MIB):
     count = len(args) + (place is not None)
 
     def body(*refs):
@@ -44,7 +45,7 @@
         in_specs=[SMEM] * (place is not None) + whole(*args) + [HBM] * len(deps),
         out_specs=specs[0] if single else specs,
         out_shape=out,
-        compiler_params=params(),
+        compiler_params=params(mib),
         cost_estimate=cost(micros),
         name=name,
     )(*([place] if place is not None else []), *args, *deps)
@@ -194,10 +195,27 @@
     return jnp.concatenate(jnp.split(values, 4, axis=1), axis=0)
 
 
+def scale_tokens_kernel(place_ref, own_ref, other_ref, out_w_ref, scaled_ref, wide_ref):
+    rows = own_ref.shape[0]
+    side = place_ref[0]
+    for ref, half in ((own_ref, side), (other_ref, 1 - side)):
+        inputs = ref[:rows, :].astype(F32)
+        here = pl.ds(pl.multiple_of(half * rows, rows), rows)
+        scaled_ref[here, :] = inputs * rms_scale(inputs)
+    for values, half in ((out_w_ref[...], side), (fold_rows(other_ref[rows:, :]), 1 - side)):
+        wide_ref[pl.ds(pl.multiple_of(half * LANES, LANES), LANES), :] = values
+
+
+def scale_tokens(place, own, other, out_w):
+    rows, model = own.shape
+    out = [shape((2 * rows, model), F32), shape((2 * LANES, out_w.shape[1]), BF16)]
+    return simple(scale_tokens_kernel, "scale_tokens", out, (own, other, out_w), place, micros=PREP)
+
+
 def project_kernel(
-    place_ref, early_ref, own_ref, other_ref, out_w_ref, normed_ref, query_ref, pair_ref, gain_ref, key_ref, meta_ref, table_ref
+    place_ref, early_ref, scaled_ref, out_w_ref, normed_ref, query_ref, pair_ref, gain_ref, key_ref, meta_ref, table_ref
 ):
-    rows, model = own_ref.shape
+    rows = scaled_ref.shape[0] // 2
     pair = query_ref.shape[1]
     side, depth = place_ref[0], place_ref[1]
     small = [early_ref[block, LANES:, :rows].astype(F32) for block in range(8)]
@@ -208,22 +226,15 @@
         if at == 0:
             gain_one = gain
 
-    out_w_other = fold_rows(other_ref[rows:, :])
-    for values, half in ((out_w_ref[...], side), (out_w_other, 1 - side)):
-        here = pl.ds(pl.multiple_of(2 * rows + half * LANES, LANES), LANES)
-        for copy in range(4):
-            pair_ref[copy, here, :] = values
+    for copy in range(4):
+        pair_ref[copy, 2 * rows :, :] = out_w_ref[...]
     weight = jnp.concatenate([early_ref[block, :LANES, :] for block in range(8)], axis=0)
-    for ref, half in ((own_ref, side), (other_ref, 1 - side)):
-        inputs = ref[:rows, :].astype(F32)
-        scale = lax.rsqrt(jnp.mean(inputs * inputs, axis=1, keepdims=True) + EPS)
-        normed = (inputs * scale * gain_one).astype(BF16)
-        here = pl.ds(pl.multiple_of(half * rows, rows), rows)
-        normed_ref[here, :] = normed
-        result = jnp.dot(normed, weight, preferred_element_type=F32).astype(BF16)
-        query_ref[here, :] = result[:, :pair] * jnp.asarray(HEAD_DIM ** (-0.5), BF16)
-        for copy in range(4):
-            pair_ref[copy, here, :] = result[:, pair:]
+    normed = (scaled_ref[...] * gain_one).astype(BF16)
+    normed_ref[...] = normed
+    result = jnp.dot(normed, weight, preferred_element_type=F32).astype(BF16)
+    query_ref[...] = result[:, :pair] * jnp.asarray(HEAD_DIM ** (-0.5), BF16)
+    for copy in range(4):
+        pair_ref[copy, : 2 * rows, :] = result[:, pair:]
 
     time = lax.broadcasted_iota(jnp.int32, (1, rows), 1)
     for block in range(8):
@@ -259,8 +270,8 @@
     table_ref[...] = table
 
 
-def project(place, early, own, other, out_w, deps):
-    rows, model = own.shape
+def project(place, early, scaled, out_w, deps):
+    rows, model = scaled.shape[0] // 2, scaled.shape[1]
     pair = early.shape[2] // 3
     out = [
         shape((2 * rows, model), BF16),
@@ -272,7 +283,7 @@
         shape((8, LANES), F32),
     ]
     return simple(
-        project_kernel, "project", out, (early, own, other, out_w), place, deps
+        project_kernel, "project", out, (early, scaled, out_w), place, deps, 0.05, 64
     )
 
 
@@ -357,7 +368,7 @@
         + [HBM] * len(deps),
         out_specs=pl.BlockSpec((chunk, length), lambda s: (s, 0)),
         out_shape=jax.ShapeDtypeStruct((rows, length), jnp.int32),
-        compiler_params=params(),
+        compiler_params=params(64),
         cost_estimate=cost(10),
         name="bias_scores",
     )(place, meta, key_meta, table, *deps)
@@ -440,7 +451,7 @@
             half,
             half,
         ],
-        compiler_params=params(),
+        compiler_params=params(64),
         cost_estimate=cost(9),
         name="attend",
     )(place, queries, bias, pairs, *deps)
@@ -835,7 +846,7 @@
         ),
         out_shape=[shape((2, rows, length), BF16)] + pair_grads + [query_grad],
         compiler_params=params(),
-        cost_estimate=cost(4),
+        cost_estimate=cost(5),
         name="attend_back",
     )(place, queries, mine, got, exact, probs, pairs, *deps)
 
@@ -914,7 +925,7 @@
         out_shape=shape((8, LANES), F32),
         scratch_shapes=[pltpu.VMEM((3, 8, LANES), F32)],
         compiler_params=params(),
-        cost_estimate=cost(8),
+        cost_estimate=cost(11),
         name="table_grad",
     )(meta, key_meta, score_grad, *deps)
 
@@ -1147,29 +1158,26 @@
     early_all = lax.all_to_all(early, "blk", 0, 0, tiled=False)
 
     turned = [turn_z(late, hop) for hop in (1, 2, 3)]
-    turned, tokens_other = lax.optimization_barrier((turned, tokens_other))
-    near = stack([late] + turned)
+    scaled, out_w_both = scale_tokens(place, tokens, tokens_other, w_out_t)
+    near = stack([late] + turned, (scaled,))
     before_near, behind_near = step_dp(near, 1), step_dp(near, 3)
     normed_one, queries, own_pairs, gains, key_meta, meta, table = project(
-        place, early_all, tokens, tokens_other, w_out_t, (near,)
-    )
-    own_pairs, before_near, behind_near = lax.optimization_barrier(
-        (own_pairs, before_near, behind_near)
+        place, early_all, scaled, out_w_both, ()
     )
     pairs = lax.all_to_all(
         own_pairs, "blk", 0, 0, axis_index_groups=[[0, 1, 2, 3], [4, 5, 6, 7]]
     )
     far = swap_side(near)
     after_near = step_dp(before_near, 1)
-    bias = bias_scores(place, meta, key_meta, table, ())
+    bias = bias_scores(place, meta, key_meta, table, (before_near, behind_near))
     probs, attn_exact, attn_mine, attn_other = attend(
-        place, queries, pairs, bias, (after_near, far)
+        place, queries, pairs, bias, (far,)
     )
     before_far, behind_far = step_dp(far, 1), step_dp(far, 3)
     after_far = step_dp(behind_far, 3)
 
     attn_got = swap_side(attn_other)
-    keep, send = branch_part(place, attn_mine, attn_got, pairs, (before_far, behind_far))
+    keep, send = branch_part(place, attn_mine, attn_got, pairs, (before_far, behind_far, after_near))
     pieces = [near, far, before_near, before_far, behind_near, behind_far, after_near, after_far]
     ffn_w, hidden_grad = ffn_prepare(place, cotangent, pieces)
     part = add(keep, swap_core(send))
@@ -1219,7 +1227,7 @@
         place, [folded] + turn_dp(folded), pair
     )
 
-    part = add(keep, swap_core(send))
+    part = add(keep, swap_core(send), (ffn_near,))
     part = add(part[0], swap_side(part[1]))
     grad = add(part, swap_chip(part))
     tokens_grad = tokens_back(place, tokens, gains, grad, swap_core(grad), middle_grad)

time: 244 us -> 221 us (0.906)
  starting transfers between devices: 80.5 us -> 65.6 us
  waiting for transfers between devices: 60.1 us -> 53.9 us
  local copies, waits for them, and re-layouts: 15.7 us -> 9.62 us
  Pallas kernels: 81.9 us -> 86.6 us
    ppermute x9, waiting for transfers between devices: 18.7 us -> 5.52 us  [turn_z(): lax.ppermute(values, 'blk', [(at, at // 4 * 4 + (at - hop) % 4) for at in...]
    ppermute x20, starting transfers between devices: 25.3 us -> 15.9 us  [swap(): lax.ppermute(values, axis_name, [(at, at ^ bit) for at in range(count)])]
    unnamed x78 -> x68, local copies, waits for them, and re-layouts: 13.1 us -> 7 us
    all_to_all x1, waiting for transfers between devices: 0.01 us -> 5.46 us  [shards(): ffn_grads = lax.all_to_all(ffn_grads, 'dp', 0, 0, tiled=False)]
    pallas_call x20 -> x21, Pallas kernels: 18.9 us -> 20.9 us  [simple(): pl.pallas_call(body, grid=(1,), in_specs=[SMEM] * (place is not None) + w...]
  transfers between devices with their start and end apart: 43 -> 43, of which waited for: 19 -> 21; matrix products, arithmetic and copies ran while one was open for 1% -> 1% of each run, Pallas kernels for 30% -> 36%
where the time goes in v3:
time: 221 us; the launch traced here: 220 us
  Pallas kernels  86.6 us (39%)
  starting transfers between devices  65.6 us (30%)
  waiting for transfers between devices  53.9 us (24%)
  local copies, waits for them, and re-layouts  9.62 us (4%)
  other arithmetic  2.48 us (1%)
    ppermute x20, waiting for transfers between devices, swap(): lax.ppermute(values, axis_name, [(at, at ^ bit) for at in range(count)])  31.5 us
    pallas_call x21, Pallas kernels, simple(): pl.pallas_call(body, grid=(1,), in_specs=[SMEM] * (place is not None) + w...  20.9 us
    ppermute x20, starting transfers between devices, swap(): lax.ppermute(values, axis_name, [(at, at ^ bit) for at in range(count)])  15.9 us
    ppermute x9, starting transfers between devices, turn_z(): lax.ppermute(values, 'blk', [(at, at // 4 * 4 + (at - hop) % 4) for at in...  15.2 us
    pallas_call x1, Pallas kernels, table_grad_sums(): pl.pallas_call(table_grad_kernel, grid=(6,), in_specs=whole(meta, key_met...  14.8 us
    ppermute x9, starting transfers between devices, step_dp(): return lax.ppermute(values, 'dp', [(at, (at + hop) % 4) for at in range(4)])  13.8 us
    pallas_call x1, Pallas kernels, bias_scores(): pl.pallas_call(bias_kernel, grid=(rows // chunk,), in_specs=[pl.BlockSpec...  11.9 us
    pallas_call x1, Pallas kernels, attend(): pl.pallas_call(attend_kernel, grid=(rows // tile,), in_specs=[SMEM, slim,...  9.5 us
  transfers between devices with their start and end apart: 43, of which 21 were waited for; matrix products, arithmetic and copies ran while one was open for 1% of the time, Pallas kernels for 36%

profile of v3, /device:TPU:0, one launch (start us, length us, event | category | flops | bytes accessed | tf_op | source)
XLA Modules:
  0.0 219.5 jit_solution(8492190361435369237)
XLA Ops:
  9.0 4.1 %collective-permute-start.1 = (bf16[528,128]{1,0:T(8,128)(2,1)}, bf16[528,128]{1,0:T(8,128)(2,1)S(1)}, u32[]{:S(2)}, u32[]{:S(2)}) collective-permute-start(bf16[528,128]{1,0:T(8,128)(2,1)} %get-tuple-element.68.refs_0_), channel_id=1, source_target_pairs={{0,12},{4,0},{8,4},{12,8},{16,28},{20,16},{24,20},{28,24},{1,13},{... | collective-permute-start | bytes 405512 | tf_op jit(solution)/shard_map/ppermute | solution.py:1092
  14.4 4.2 %all-to-all-start = ((bf16[8,144,384]{2,1,0:T(8,128)(2,1)}), bf16[8,144,384]{2,1,0:T(8,128)(2,1)}, u32[]{:S(2)}, u32[]{:S(2)}) async-start(bf16[8,144,384]{2,1,0:T(8,128)(2,1)} %get-tuple-element.61), calls=%async_computation | async-start | bytes 1769472 | tf_op jit(solution)/shard_map/all_to_all | solution.py:1158
  21.1 4.5 %collective-permute-done.3.refs_3_ = bf16[528,128]{1,0:T(8,128)(2,1)S(1)} collective-permute-done((bf16[528,128]{1,0:T(8,128)(2,1)}, bf16[528,128]{1,0:T(8,128)(2,1)S(1)}, u32[]{:S(2)}, u32[]{:S(2)}) %collective-permute-start.3) | collective-permute-done | bytes 135200 | tf_op jit(solution)/shard_map/ppermute | solution.py:1092
  31.9 4.2 %project.1 = (bf16[512,1024]{1,0:T(8,128)(2,1)}, bf16[512,128]{1,0:T(8,128)(2,1)}, bf16[4,768,256]{2,1,0:T(8,128)(2,1)}, f32[2,1024]{1,0:T(2,128)}, s32[8,2048]{...) custom-call(s32[4]{0:T(128)} %pad_add_fusion.place_ref.refs_0_, ...), custom_call_target="tpu_custom_call" | custom-call | flops 55000000 | bytes 5000 | tf_op jit(solution)/shard_map/project/pallas_call | solution.py:42
  36.2 4.4 %all-to-all-start.1 = ((bf16[4,768,256]{2,1,0:T(8,128)(2,1)}), bf16[4,768,256]{2,1,0:T(8,128)(2,1)}, u32[]{:S(2)}, u32[]{:S(2)}) async-start(bf16[4,768,256]{2,1,0:T(8,128)(2,1)} %get-tuple-element.69), calls=%async_computation.1 | async-start | bytes 3145728 | tf_op jit(solution)/shard_map/all_to_all | solution.py:1167
  44.8 11.9 %bias_scores.1.bias_ref = s32[512,2048]{1,0:T(8,128)} custom-call(s32[4]{0:T(128)} %pad_add_fusion.place_ref.refs_0_, s32[3,512,128]{2,1,0:T(8,128)} %get-tuple-element.65.meta_ref, s32[8,2048]{1,0:T(8,128)} %get-tuple-element.66.key_ref, f32[8,128]{1,0:T(8,128)} %get-tuple-element.67.table_ref, bf16[4,528,128]{2,1,0:T(8,128)(2,1)} %collective-permute-done.4.refs_0_.refs_2_, ...), custom_call_target="tpu_custom_call" | custom-call | flops 11000000512 | bytes 1000000 | tf_op jit(solution)/shard_map/bias_scores/pallas_call | solution.py:359
  60.9 9.5 %attend.1 = (bf16[2,512,2048]{2,1,0:T(8,128)(2,1)}, f32[512,128]{1,0:T(8,128)}, bf16[256,128]{1,0:T(8,128)(2,1)}, bf16[256,128]{1,0:T(8,128)(2,1)}) custom-call(s32[4]{0:T(128)} %pad_add_fusion.place_ref.refs_0_, bf16[512,128]{1,0:T(8,128)(2,1)} %get-tuple-element.64.query_ref, s32[512,2048]{1,0:T(8,128)} %bias_scores.1.bias_ref, ...), custom_call_target="tpu_custom_call" | custom-call | flops 9900000256 | bytes 900000 | tf_op jit(solution)/shard_map/attend/pallas_call | solution.py:441
  70.5 4.4 %collective-permute-done.7.refs_2_.refs_6_ = bf16[256,128]{1,0:T(8,128)(2,1)S(1)} collective-permute-done((bf16[256,128]{1,0:T(8,128)(2,1)}, bf16[256,128]{1,0:T(8,128)(2,1)S(1)}, u32[]{:S(2)}, u32[]{:S(2)}) %collective-permute-start.7) | collective-permute-done | bytes 65568 | tf_op jit(solution)/shard_map/ppermute | solution.py:1064
  80.0 3.0 %collective-permute-start.12 = (bf16[128,1024]{1,0:T(8,128)(2,1)S(1)}, bf16[128,1024]{1,0:T(8,128)(2,1)S(1)}, u32[]{:S(2)}, u32[]{:S(2)}) collective-permute-start(bf16[128,1024]{1,0:T(8,128)(2,1)S(1)} %add.29.refs_0_), channel_id=1, source_target_pairs={{0,2},{1,3},{2,0},{3,1},{4,6},{5,7},{6,4},{7,5},{8,10},{9,11},{10,... | collective-permute-start | bytes 786440 | tf_op jit(solution)/shard_map/ppermute | solution.py:1064
  83.0 3.9 %ffn_prepare.1 = (bf16[4,528,1024]{2,1,0:T(8,128)(2,1)S(1)}, f32[4,176,256]{2,1,0:T(8,128)S(1)}) custom-call(s32[4]{0:T(128)S(1)} %copy-done.16, bf16[256,1024]{1,0:T(8,128)(2,1)S(1)} %copy-done.19, bf16[4,528,128]{2,1,0:T(8,128)(2,1)} %stack.21.refs_0_, bf16[4,528,128]{2,1,0:T(8,128)(2,1)} %collective-permute-done.6.refs_0_.refs_1_, ...), custom_call_target="tpu_custom_call" | custom-call | flops 4400000000 | bytes 400000 | tf_op jit(solution)/shard_map/ffn_prepare/pallas_call | solution.py:525
  86.9 3.0 %collective-permute-done.12.refs_1_ = bf16[128,1024]{1,0:T(8,128)(2,1)S(1)} collective-permute-done((bf16[128,1024]{1,0:T(8,128)(2,1)S(1)}, bf16[128,1024]{1,0:T(8,128)(2,1)S(1)}, u32[]{:S(2)}, u32[]{:S(2)}) %collective-permute-start.12) | collective-permute-done | bytes 262176 | tf_op jit(solution)/shard_map/ppermute | solution.py:1064
  91.6 5.7 %ffn_forward.1 = (bf16[256,1024]{1,0:T(8,128)(2,1)S(1)}, bf16[4,528,256]{2,1,0:T(8,128)(2,1)S(1)}, bf16[128,1024]{1,0:T(8,128)(2,1)S(1)}, bf16[128,1024]{1,0:T(8,128)(2,1)S(1)}) custom-call(s32[4]{0:T(128)S(1)} %copy-done.16, bf16[256,1024]{1,0:T(8,128)(2,1)S(1)} %copy-done.5, bf16[128,1024]{1,0:T(8,128)(2,1)S(1)} %add.30.total_ref.refs_2_, ...), custom_call_target="tpu_custom_call" | custom-call | flops 5500000256 | bytes 500000 | tf_op jit(solution)/shard_map/ffn_forward/pallas_call | solution.py:584
  99.2 3.0 %collective-permute-start.16 = (bf16[128,1024]{1,0:T(8,128)(2,1)S(1)}, bf16[128,1024]{1,0:T(8,128)(2,1)S(1)}, u32[]{:S(2)}, u32[]{:S(2)}) collective-permute-start(bf16[128,1024]{1,0:T(8,128)(2,1)S(1)} %add.31.refs_0_), channel_id=1, source_target_pairs={{0,2},{1,3},{2,0},{3,1},{4,6},{5,7},{6,4},{7,5},{8,10},{9,11},{10,... | collective-permute-start | bytes 786440 | tf_op jit(solution)/shard_map/ppermute | solution.py:1064
  106.6 4.9 %all-to-all-start.2 = ((bf16[4,528,1024]{2,1,0:T(8,128)(2,1)}), bf16[4,528,1024]{2,1,0:T(8,128)(2,1)}, u32[]{:S(2)}, u32[]{:S(2)}) async-start(bf16[4,528,1024]{2,1,0:T(8,128)(2,1)} %copy-done), calls=%async_computation.2 | async-start | bytes 8650752 | tf_op jit(solution)/shard_map/all_to_all | solution.py:1195
  125.4 7.4 %attend_back.1 = (bf16[2,512,2048]{2,1,0:T(8,128)(2,1)S(1)}, bf16[256,512]{1,0:T(8,128)(2,1)S(1)}, bf16[256,512]{1,0:T(8,128)(2,1)S(1)}, bf16[256,512]{1,0:T(8,1...) custom-call(s32[4]{0:T(128)S(1)} %copy-done.16, bf16[512,128]{1,0:T(8,128)(2,1)S(1)} %copy-done.20, ...), custom_call_target="tpu_custom_call" | custom-call | flops 5500000256 | bytes 500000 | tf_op jit(solution)/shard_map/attend_back/pallas_call | solution.py:832
  137.0 14.8 %table_grad.1.refs_9_ = f32[8,128]{1,0:T(8,128)S(1)} custom-call(s32[3,512,128]{2,1,0:T(8,128)S(1)} %copy-done.18, s32[8,2048]{1,0:T(8,128)S(1)} %copy-done.21, bf16[2,512,2048]{2,1,0:T(8,128)(2,1)S(1)} %get-tuple-element.91.score_ref, bf16[128,1024]{1,0:T(8,128)(2,1)S(1)} %collective-permute-done.19.refs_0_.refs_1_), custom_call_target="tpu_custom_call" | custom-call | flops 12099999744 | bytes 1100000 | tf_op jit(solution)/shard_map/table_grad/pallas_call | solution.py:920
  151.9 3.7 %weight_grads.1 = (bf16[640,1024]{1,0:T(8,128)(2,1)S(1)}, bf16[16,1024]{1,0:T(8,128)(2,1)S(1)}, bf16[16,1024]{1,0:T(8,128)(2,1)S(1)}, bf16[2,128,1024]{2,1,0:T(8,128)(2,1)S(1)}, bf16[2,128,1024]{2,1,0:T(8,128)(2,1)}) custom-call(s32[4]{0:T(128)S(1)} %copy-done.16, bf16[512,128]{1,0:T(8,128)(2,1)S(1)} %get-tuple-element.87.refs_1_, ...), custom_call_target="tpu_custom_call" | custom-call | flops 4400000000 | bytes 400000 | tf_op jit(solution)/shard_map/weight_grads/pallas_call | solution.py:42
  156.6 5.5 %all-to-all-done.2.parts_ref = bf16[4,528,1024]{2,1,0:T(8,128)(2,1)} async-done(((bf16[4,528,1024]{2,1,0:T(8,128)(2,1)}), bf16[4,528,1024]{2,1,0:T(8,128)(2,1)}, u32[]{:S(2)}, u32[]{:S(2)}) %all-to-all-start.2) | async-done | bytes 4325408 | tf_op jit(solution)/shard_map/all_to_all | solution.py:1195
  162.1 3.8 %all-to-all-start.3 = ((bf16[4,160,1024]{2,1,0:T(8,128)(2,1)}), bf16[4,160,1024]{2,1,0:T(8,128)(2,1)S(1)}, u32[]{:S(2)}, u32[]{:S(2)}) async-start(bf16[4,160,1024]{2,1,0:T(8,128)(2,1)} %bitcast.37), calls=%async_computation.3 | async-start | bytes 2621440 | tf_op jit(solution)/shard_map/all_to_all | solution.py:1218
  165.8 3.1 %fold_to_blocks.1 = bf16[2,4,528,128]{3,2,1,0:T(8,128)(2,1)S(1)} custom-call(s32[4]{0:T(128)S(1)} %copy-done.16, bf16[4,528,1024]{2,1,0:T(8,128)(2,1)} %all-to-all-done.2.parts_ref, bf16[2,128,1024]{2,1,0:T(8,128)(2,1)} %get-tuple-element.96.refs_0_), custom_call_target="tpu_custom_call" | custom-call | flops 4400000000 | bytes 400000 | tf_op jit(solution)/shard_map/fold_to_blocks/pallas_call | solution.py:750
  172.0 10.6 %collective-permute-done.24.refs_1_ = bf16[4,528,128]{2,1,0:T(8,128)(2,1)S(1)} collective-permute-done((bf16[4,528,128]{2,1,0:T(8,128)(2,1)S(1)}, bf16[4,528,128]{2,1,0:T(8,128)(2,1)S(1)}, u32[]{:S(2)}, u32[]{:S(2)}) %collective-permute-start.24) | collective-permute-done | bytes 540704 | tf_op jit(solution)/shard_map/ppermute | solution.py:1064
  183.9 3.4 %all-to-all-start.4 = ((bf16[8,176,128]{2,1,0:T(8,128)(2,1)}), bf16[8,176,128]{2,1,0:T(8,128)(2,1)S(1)}, u32[]{:S(2)}, u32[]{:S(2)}) async-start(bf16[8,176,128]{2,1,0:T(8,128)(2,1)} %spread.1), calls=%async_computation.4 | async-start | bytes 720896 | tf_op jit(solution)/shard_map/all_to_all | solution.py:1223
  197.7 2.9 %collective-permute-start.28 = (bf16[128,1024]{1,0:T(8,128)(2,1)S(1)}, bf16[128,1024]{1,0:T(8,128)(2,1)S(1)}, u32[]{:S(2)}, u32[]{:S(2)}) collective-permute-start(bf16[128,1024]{1,0:T(8,128)(2,1)S(1)} %add.37.refs_0_), channel_id=1, source_target_pairs={{0,2},{1,3},{2,0},{3,1},{4,6},{5,7},{6,4},{7,5},{8,10},{9,11},{10,... | collective-permute-start | bytes 786440 | tf_op jit(solution)/shard_map/ppermute | solution.py:1064
  208.8 4.0 %collective-permute-done.36.refs_2_ = bf16[880,128]{1,0:T(8,128)(2,1)S(1)} collective-permute-done((bf16[880,128]{1,0:T(8,128)(2,1)S(1)}, bf16[880,128]{1,0:T(8,128)(2,1)S(1)}, u32[]{:S(2)}, u32[]{:S(2)}) %collective-permute-start.36) | collective-permute-done | bytes 225312 | tf_op jit(solution)/shard_map/ppermute | solution.py:1084
  (172 shorter events, 88.4 us)
Async XLA Ops:
  3.3 15.3 %collective-permute-start = (bf16[288,1024]{1,0:T(8,128)(2,1)}, bf16[288,1024]{1,0:T(8,128)(2,1)}, u32[]{:S(2)}, u32[]{:S(2)}) collective-permute-start(bf16[288,1024]{1,0:T(8,128)(2,1)} %maximum_maximum_fusion), channel_id=1, source_target_pairs={{0,16},{4,20},{8,24},{12,28},{16,0},{20,4},{24,8},{28,12},{1,17},{... | collective-permute-start | bytes 1769480 | tf_op jit(solution)/shard_map/ppermute | solution.py:1064
  9.0 11.1 %collective-permute-start.1 = (bf16[528,128]{1,0:T(8,128)(2,1)}, bf16[528,128]{1,0:T(8,128)(2,1)S(1)}, u32[]{:S(2)}, u32[]{:S(2)}) collective-permute-start(bf16[528,128]{1,0:T(8,128)(2,1)} %get-tuple-element.68.refs_0_), channel_id=1, source_target_pairs={{0,12},{4,0},{8,4},{12,8},{16,28},{20,16},{24,20},{28,24},{1,13},{... | collective-permute-start | bytes 405512 | tf_op jit(solution)/shard_map/ppermute | solution.py:1092
  13.1 12.5 %collective-permute-start.3 = (bf16[528,128]{1,0:T(8,128)(2,1)}, bf16[528,128]{1,0:T(8,128)(2,1)S(1)}, u32[]{:S(2)}, u32[]{:S(2)}) collective-permute-start(bf16[528,128]{1,0:T(8,128)(2,1)} %get-tuple-element.68.refs_0_), channel_id=1, source_target_pairs={{0,4},{4,8},{8,12},{12,0},{16,20},{20,24},{24,28},{28,16},{1,5},{5... | collective-permute-start | bytes 405512 | tf_op jit(solution)/shard_map/ppermute | solution.py:1092
  14.4 17.5 %all-to-all-start = ((bf16[8,144,384]{2,1,0:T(8,128)(2,1)}), bf16[8,144,384]{2,1,0:T(8,128)(2,1)}, u32[]{:S(2)}, u32[]{:S(2)}) async-start(bf16[8,144,384]{2,1,0:T(8,128)(2,1)} %get-tuple-element.61), calls=%async_computation | async-start | bytes 1769472 | tf_op jit(solution)/shard_map/all_to_all | solution.py:1158
  26.5 14.8 %collective-permute-start.6 = (bf16[4,528,128]{2,1,0:T(8,128)(2,1)}, bf16[4,528,128]{2,1,0:T(8,128)(2,1)}, u32[]{:S(2)}, u32[]{:S(2)}) collective-permute-start(bf16[4,528,128]{2,1,0:T(8,128)(2,1)} %stack.21.refs_0_), channel_id=1, source_target_pairs={{0,16},{4,20},{8,24},{12,28},{16,0},{20,4},{24,8},{28,12},{1,17},{... | collective-permute-start | bytes 1622024 | tf_op jit(solution)/shard_map/ppermute | solution.py:1064
  26.5 17.5 %collective-permute-start.4 = (bf16[4,528,128]{2,1,0:T(8,128)(2,1)}, bf16[4,528,128]{2,1,0:T(8,128)(2,1)}, u32[]{:S(2)}, u32[]{:S(2)}) collective-permute-start(bf16[4,528,128]{2,1,0:T(8,128)(2,1)} %stack.21.refs_0_), channel_id=1, source_target_pairs={{0,32},{32,64},{64,96},{96,0},{1,33},{33,65},{65,97},{97,1},{2,34}... | collective-permute-start | bytes 1622024 | tf_op jit(solution)/shard_map/ppermute | solution.py:1084
  28.1 16.7 %collective-permute-start.5 = (bf16[4,528,128]{2,1,0:T(8,128)(2,1)}, bf16[4,528,128]{2,1,0:T(8,128)(2,1)}, u32[]{:S(2)}, u32[]{:S(2)}) collective-permute-start(bf16[4,528,128]{2,1,0:T(8,128)(2,1)} %stack.21.refs_0_), channel_id=1, source_target_pairs={{0,96},{32,0},{64,32},{96,64},{1,97},{33,1},{65,33},{97,65},{2,98}... | collective-permute-start | bytes 1622024 | tf_op jit(solution)/shard_map/ppermute | solution.py:1084
  36.2 24.7 %all-to-all-start.1 = ((bf16[4,768,256]{2,1,0:T(8,128)(2,1)}), bf16[4,768,256]{2,1,0:T(8,128)(2,1)}, u32[]{:S(2)}, u32[]{:S(2)}) async-start(bf16[4,768,256]{2,1,0:T(8,128)(2,1)} %get-tuple-element.69), calls=%async_computation.1 | async-start | bytes 3145728 | tf_op jit(solution)/shard_map/all_to_all | solution.py:1167
  41.3 15.4 %collective-permute-start.9 = (bf16[4,528,128]{2,1,0:T(8,128)(2,1)}, bf16[4,528,128]{2,1,0:T(8,128)(2,1)}, u32[]{:S(2)}, u32[]{:S(2)}) collective-permute-start(bf16[4,528,128]{2,1,0:T(8,128)(2,1)} %collective-permute-done.6.refs_0_.refs_1_), channel_id=1, source_target_pairs={{0,96},{32,0},{64,32},{96,64},{1,97},{33,1},{65,33},{97,65},{2,98}... | collective-permute-start | bytes 1622024 | tf_op jit(solution)/shard_map/ppermute | solution.py:1084
  44.1 26.5 %collective-permute-start.8 = (bf16[4,528,128]{2,1,0:T(8,128)(2,1)}, bf16[4,528,128]{2,1,0:T(8,128)(2,1)}, u32[]{:S(2)}, u32[]{:S(2)}) collective-permute-start(bf16[4,528,128]{2,1,0:T(8,128)(2,1)} %collective-permute-done.6.refs_0_.refs_1_), channel_id=1, source_target_pairs={{0,32},{32,64},{64,96},{96,0},{1,33},{33,65},{65,97},{97,1},{2,34}... | collective-permute-start | bytes 1622024 | tf_op jit(solution)/shard_map/ppermute | solution.py:1084
  44.1 26.4 %collective-permute-start.10 = (bf16[4,528,128]{2,1,0:T(8,128)(2,1)}, bf16[4,528,128]{2,1,0:T(8,128)(2,1)}, u32[]{:S(2)}, u32[]{:S(2)}) collective-permute-start(bf16[4,528,128]{2,1,0:T(8,128)(2,1)} %collective-permute-done.4.refs_0_.refs_2_), channel_id=1, source_target_pairs={{0,32},{32,64},{64,96},{96,0},{1,33},{33,65},{65,97},{97,1},{2,34}... | collective-permute-start | bytes 1622024 | tf_op jit(solution)/shard_map/ppermute | solution.py:1084
  56.7 26.2 %collective-permute-start.13 = (bf16[4,528,128]{2,1,0:T(8,128)(2,1)}, bf16[4,528,128]{2,1,0:T(8,128)(2,1)}, u32[]{:S(2)}, u32[]{:S(2)}) collective-permute-start(bf16[4,528,128]{2,1,0:T(8,128)(2,1)} %collective-permute-done.9.refs_5_), channel_id=1, source_target_pairs={{0,96},{32,0},{64,32},{96,64},{1,97},{33,1},{65,33},{97,65},{2,98}... | collective-permute-start | bytes 1622024 | tf_op jit(solution)/shard_map/ppermute | solution.py:1084
  99.2 12.3 %collective-permute-start.16 = (bf16[128,1024]{1,0:T(8,128)(2,1)S(1)}, bf16[128,1024]{1,0:T(8,128)(2,1)S(1)}, u32[]{:S(2)}, u32[]{:S(2)}) collective-permute-start(bf16[128,1024]{1,0:T(8,128)(2,1)S(1)} %add.31.refs_0_), channel_id=1, source_target_pairs={{0,2},{1,3},{2,0},{3,1},{4,6},{5,7},{6,4},{7,5},{8,10},{9,11},{10,... | collective-permute-start | bytes 786440 | tf_op jit(solution)/shard_map/ppermute | solution.py:1064
  106.6 55.4 %all-to-all-start.2 = ((bf16[4,528,1024]{2,1,0:T(8,128)(2,1)}), bf16[4,528,1024]{2,1,0:T(8,128)(2,1)}, u32[]{:S(2)}, u32[]{:S(2)}) async-start(bf16[4,528,1024]{2,1,0:T(8,128)(2,1)} %copy-done), calls=%async_computation.2 | async-start | bytes 8650752 | tf_op jit(solution)/shard_map/all_to_all | solution.py:1195
  121.9 15.1 %collective-permute-start.19 = (bf16[128,1024]{1,0:T(8,128)(2,1)S(1)}, bf16[128,1024]{1,0:T(8,128)(2,1)S(1)}, u32[]{:S(2)}, u32[]{:S(2)}) collective-permute-start(bf16[128,1024]{1,0:T(8,128)(2,1)S(1)} %add.33.refs_0_), channel_id=1, source_target_pairs={{0,2},{1,3},{2,0},{3,1},{4,6},{5,7},{6,4},{7,5},{8,10},{9,11},{10,... | collective-permute-start | bytes 786440 | tf_op jit(solution)/shard_map/ppermute | solution.py:1064
  132.8 19.0 %collective-permute-start.21 = (bf16[256,512]{1,0:T(8,128)(2,1)S(1)}, bf16[256,512]{1,0:T(8,128)(2,1)S(1)}, u32[]{:S(2)}, u32[]{:S(2)}) collective-permute-start(bf16[256,512]{1,0:T(8,128)(2,1)S(1)} %get-tuple-element.93), channel_id=1, source_target_pairs={{0,4},{4,8},{8,12},{12,0},{16,20},{20,24},{24,28},{28,16},{1,5},{5... | collective-permute-start | bytes 786440 | tf_op jit(solution)/shard_map/ppermute | solution.py:1092
  133.4 18.4 %collective-permute-start.22 = (bf16[256,512]{1,0:T(8,128)(2,1)S(1)}, bf16[256,512]{1,0:T(8,128)(2,1)S(1)}, u32[]{:S(2)}, u32[]{:S(2)}) collective-permute-start(bf16[256,512]{1,0:T(8,128)(2,1)S(1)} %get-tuple-element.94), channel_id=1, source_target_pairs={{0,8},{4,12},{8,0},{12,4},{16,24},{20,28},{24,16},{28,20},{1,9},{5... | collective-permute-start | bytes 786440 | tf_op jit(solution)/shard_map/ppermute | solution.py:1092
  135.4 16.5 %collective-permute-start.23 = (bf16[256,512]{1,0:T(8,128)(2,1)S(1)}, bf16[256,512]{1,0:T(8,128)(2,1)S(1)}, u32[]{:S(2)}, u32[]{:S(2)}) collective-permute-start(bf16[256,512]{1,0:T(8,128)(2,1)S(1)} %get-tuple-element.95), channel_id=1, source_target_pairs={{0,12},{4,0},{8,4},{12,8},{16,28},{20,16},{24,20},{28,24},{1,13},{... | collective-permute-start | bytes 786440 | tf_op jit(solution)/shard_map/ppermute | solution.py:1092
  162.1 20.9 %all-to-all-start.3 = ((bf16[4,160,1024]{2,1,0:T(8,128)(2,1)}), bf16[4,160,1024]{2,1,0:T(8,128)(2,1)S(1)}, u32[]{:S(2)}, u32[]{:S(2)}) async-start(bf16[4,160,1024]{2,1,0:T(8,128)(2,1)} %bitcast.37), calls=%async_computation.3 | async-start | bytes 2621440 | tf_op jit(solution)/shard_map/all_to_all | solution.py:1218
  169.0 13.6 %collective-permute-start.24 = (bf16[4,528,128]{2,1,0:T(8,128)(2,1)S(1)}, bf16[4,528,128]{2,1,0:T(8,128)(2,1)S(1)}, u32[]{:S(2)}, u32[]{:S(2)}) collective-permute-start(bf16[4,528,128]{2,1,0:T(8,128)(2,1)S(1)} %get-tuple-element.110), channel_id=1, source_target_pairs={{0,16},{4,20},{8,24},{12,28},{16,0},{20,4},{24,8},{28,12},{1,17},{... | collective-permute-start | bytes 1622024 | tf_op jit(solution)/shard_map/ppermute | solution.py:1064
  169.1 18.2 %collective-permute-start.26 = (bf16[2,128,1024]{2,1,0:T(8,128)(2,1)}, bf16[2,128,1024]{2,1,0:T(8,128)(2,1)}, u32[]{:S(2)}, u32[]{:S(2)}) collective-permute-start(bf16[2,128,1024]{2,1,0:T(8,128)(2,1)} %get-tuple-element.96.refs_0_), channel_id=1, source_target_pairs={{0,1},{1,0},{2,3},{3,2},{4,5},{5,4},{6,7},{7,6},{8,9},{9,8},{10,11... | collective-permute-start | bytes 1572872 | tf_op jit(solution)/shard_map/ppermute | solution.py:1064
  171.1 11.6 %collective-permute-start.31 = (bf16[16,1024]{1,0:T(8,128)(2,1)S(1)}, bf16[16,1024]{1,0:T(8,128)(2,1)S(1)}, u32[]{:S(2)}, u32[]{:S(2)}) collective-permute-start(bf16[16,1024]{1,0:T(8,128)(2,1)S(1)} %add.39.refs_2_), channel_id=1, source_target_pairs={{0,2},{1,3},{2,0},{3,1},{4,6},{5,7},{6,4},{7,5},{8,10},{9,11},{10,... | collective-permute-start | bytes 98312 | tf_op jit(solution)/shard_map/ppermute | solution.py:1064
  183.9 16.7 %all-to-all-start.4 = ((bf16[8,176,128]{2,1,0:T(8,128)(2,1)}), bf16[8,176,128]{2,1,0:T(8,128)(2,1)S(1)}, u32[]{:S(2)}, u32[]{:S(2)}) async-start(bf16[8,176,128]{2,1,0:T(8,128)(2,1)} %spread.1), calls=%async_computation.4 | async-start | bytes 720896 | tf_op jit(solution)/shard_map/all_to_all | solution.py:1223
  201.7 11.2 %collective-permute-start.36 = (bf16[880,128]{1,0:T(8,128)(2,1)S(1)}, bf16[880,128]{1,0:T(8,128)(2,1)S(1)}, u32[]{:S(2)}, u32[]{:S(2)}) collective-permute-start(bf16[880,128]{1,0:T(8,128)(2,1)S(1)} %fold_bundle.1.refs_0_), channel_id=1, source_target_pairs={{0,96},{32,0},{64,32},{96,64},{1,97},{33,1},{65,33},{97,65},{2,98}... | collective-permute-start | bytes 675848 | tf_op jit(solution)/shard_map/ppermute | solution.py:1084
  (53 other events, 367.7 us)

commit v4 on v3

--- a/solution.py
+++ b/solution.py
@@ -506,29 +506,37 @@
 
 
 def ffn_prepare_kernel(place_ref, dy_ref, *refs):
-    piece_refs, (weight_ref, grad_ref, sems) = refs[:8], refs[8:]
-    copies = [piece_copies(place_ref, piece_refs, weight_ref, sems, hop, 0) for hop in range(4)]
-    units = weight_ref.shape[1] // 3
-    for group in copies:
+    piece_refs, (weight_ref, down_ref, grad_ref, sems, down_sems) = refs[:8], refs[8:]
+    units = down_ref.shape[1]
+    copies = [piece_copies(place_ref, piece_refs, down_ref, down_sems, hop, 2 * units) for hop in range(4)]
+    late = [piece_copies(place_ref, piece_refs, weight_ref, sems, hop, 0) for hop in range(4)]
+    for group in copies + late:
         for copy in group:
             copy.start()
     for hop in range(4):
         for copy in copies[hop]:
             copy.wait()
-        grad_ref[hop] = contract_cols(weight_ref[hop, 2 * units :, :], dy_ref[...])
+        grad_ref[hop] = contract_cols(down_ref[hop], dy_ref[...])
+    for group in late:
+        for copy in group:
+            copy.wait()
 
 
 def ffn_prepare(place, dy, pieces):
     rows, model = dy.shape
-    height = pieces[0].shape[1]
-    out = [shape((4, height, model), BF16), shape((4, height // 3, rows), F32)]
+    units = pieces[0].shape[1] // 3
+    out = [
+        shape((4, 2 * units, model), BF16),
+        shape((4, units, model), BF16),
+        shape((4, units, rows), F32),
+    ]
     return pl.pallas_call(
         ffn_prepare_kernel,
         grid=(1,),
         in_specs=[SMEM] + whole(dy) + [HBM] * 8,
         out_specs=whole(*out),
         out_shape=out,
-        scratch_shapes=[pltpu.SemaphoreType.DMA((4, 8))],
+        scratch_shapes=[pltpu.SemaphoreType.DMA((4, 8)), pltpu.SemaphoreType.DMA((4, 8))],
         compiler_params=params(),
         cost_estimate=cost(4),
         name="ffn_prepare",
@@ -576,7 +584,8 @@
     rows, model = tokens.shape
     hops, height, _ = weights.shape
     half = shape((rows // 2, model), BF16)
-    out = [shape((rows, model), BF16), shape((hops, height, rows), BF16), half, half]
+    parts = shape((hops, height // 2 * 3, rows), BF16)
+    out = [shape((rows, model), BF16), parts, half, half]
 
     def chunk(item):
         return pl.BlockSpec((1,) + item.shape[1:], lambda s: (s, 0, 0))
@@ -586,7 +595,7 @@
         grid=(hops,),
         in_specs=[SMEM]
         + whole(tokens, total, got, gains)
-        + [chunk(hidden_grad), pl.BlockSpec((1, height // 3 * 2, model), lambda s: (s, 0, 0))],
+        + [chunk(hidden_grad), chunk(weights)],
         out_specs=whole(out[0]) + [chunk(out[1])] + whole(half, half),
         out_shape=out,
         scratch_shapes=[pltpu.VMEM((rows, model), F32), pltpu.VMEM((model, rows), BF16)],
@@ -635,7 +644,7 @@
         in_specs=[
             SMEM,
             pl.BlockSpec((1, height // 3, rows), lambda s: (s, 2, 0)),
-            pl.BlockSpec((1, height // 3, model), lambda s: (s, 2, 0)),
+            pl.BlockSpec((1, height // 3, model), lambda s: (s, 0, 0)),
         ]
         + [HBM] * len(deps),
         out_specs=whole(half, half),
@@ -1179,7 +1188,7 @@
     attn_got = swap_side(attn_other)
     keep, send = branch_part(place, attn_mine, attn_got, pairs, (before_far, behind_far, after_near))
     pieces = [near, far, before_near, before_far, behind_near, behind_far, after_near, after_far]
-    ffn_w, hidden_grad = ffn_prepare(place, cotangent, pieces)
+    ffn_w, down_w, hidden_grad = ffn_prepare(place, cotangent, pieces)
     part = add(keep, swap_core(send))
     branch = add(part, swap_chip(part), (ffn_w,))
     branch_got = swap_core(branch)
@@ -1193,7 +1202,7 @@
         place, tokens, branch, branch_got, cotangent, gains, grad, swap_core(grad), pairs
     )
     ffn_grads = lax.all_to_all(ffn_grads, "dp", 0, 0, tiled=False)
-    keep, send = ffn_output(place, parts, ffn_w, (grad_other,))
+    keep, send = ffn_output(place, parts, down_w, (grad_other,))
     out_part = add(keep, swap_core(send))
     out_got = swap_chip(out_part)
     score_grad, *pair_grads, query_low = attend_back(

time: 221 us -> 220 us (level)
  waiting for transfers between devices: 53.9 us -> 39.3 us
  starting transfers between devices: 65.6 us -> 77.9 us
    ppermute x20, starting transfers between devices: 15.9 us -> 25.1 us  [swap(): lax.ppermute(values, axis_name, [(at, at ^ bit) for at in range(count)])]
    ppermute x9, waiting for transfers between devices: 5.52 us -> 0.04 us  [turn_z(): lax.ppermute(values, 'blk', [(at, at // 4 * 4 + (at - hop) % 4) for at in...]
    ppermute x20, waiting for transfers between devices: 31.5 us -> 26.4 us  [swap(): lax.ppermute(values, axis_name, [(at, at ^ bit) for at in range(count)])]
    all_to_all x1, waiting for transfers between devices: 2.1 us -> 5.14 us  [shards(): early_all = lax.all_to_all(early, 'blk', 0, 0, tiled=False)]
    ppermute x9, waiting for transfers between devices: 7.51 us -> 4.87 us  [step_dp(): return lax.ppermute(values, 'dp', [(at, (at + hop) % 4) for at in range(4)])]
    all_to_all x1, waiting for transfers between devices: 5.46 us -> 2.87 us  [shards(): ffn_grads = lax.all_to_all(ffn_grads, 'dp', 0, 0, tiled=False)]
    ppermute x9, starting transfers between devices: 15.2 us -> 17.4 us  [turn_z(): lax.ppermute(values, 'blk', [(at, at // 4 * 4 + (at - hop) % 4) for at in...]
    unnamed x68 -> x66, local copies, waits for them, and re-layouts: 7 us -> 8.46 us
  transfers between devices with their start and end apart: 43 -> 43, of which waited for: 21 -> 17; matrix products, arithmetic and copies ran while one was open for 1% -> 1% of each run, Pallas kernels for 36% -> 35%
where the time goes in v4:
time: 220 us; the launch traced here: 219 us
  Pallas kernels  85.9 us (39%)
  starting transfers between devices  77.9 us (35%)
  waiting for transfers between devices  39.3 us (18%)
  local copies, waits for them, and re-layouts  11.8 us (5%)
  other arithmetic  2.49 us (1%)
    ppermute x20, waiting for transfers between devices, swap(): lax.ppermute(values, axis_name, [(at, at ^ bit) for at in range(count)])  26.4 us
    ppermute x20, starting transfers between devices, swap(): lax.ppermute(values, axis_name, [(at, at ^ bit) for at in range(count)])  25.1 us
    pallas_call x21, Pallas kernels, simple(): pl.pallas_call(body, grid=(1,), in_specs=[SMEM] * (place is not None) + w...  19.9 us
    ppermute x9, starting transfers between devices, turn_z(): lax.ppermute(values, 'blk', [(at, at // 4 * 4 + (at - hop) % 4) for at in...  17.4 us
    pallas_call x1, Pallas kernels, table_grad_sums(): pl.pallas_call(table_grad_kernel, grid=(6,), in_specs=whole(meta, key_met...  14.8 us
    ppermute x9, starting transfers between devices, step_dp(): return lax.ppermute(values, 'dp', [(at, (at + hop) % 4) for at in range(4)])  14.5 us
    pallas_call x1, Pallas kernels, bias_scores(): pl.pallas_call(bias_kernel, grid=(rows // chunk,), in_specs=[pl.BlockSpec...  11.9 us
    pallas_call x1, Pallas kernels, attend(): pl.pallas_call(attend_kernel, grid=(rows // tile,), in_specs=[SMEM, slim,...  9.52 us
  transfers between devices with their start and end apart: 43, of which 17 were waited for; matrix products, arithmetic and copies ran while one was open for 1% of the time, Pallas kernels for 35%

profile of v4, /device:TPU:0, one launch (start us, length us, event | category | flops | bytes accessed | tf_op | source)
XLA Modules:
  0.0 218.6 jit_solution(6075678820443758782)
XLA Ops:
  11.0 3.6 %collective-permute-start.2 = (bf16[528,128]{1,0:T(8,128)(2,1)}, bf16[528,128]{1,0:T(8,128)(2,1)S(1)}, u32[]{:S(2)}, u32[]{:S(2)}) collective-permute-start(bf16[528,128]{1,0:T(8,128)(2,1)} %get-tuple-element.69.refs_0_), channel_id=1, source_target_pairs={{0,8},{4,12},{8,0},{12,4},{16,24},{20,28},{24,16},{28,20},{1,9},{5... | collective-permute-start | bytes 405512 | tf_op jit(solution)/shard_map/ppermute | solution.py:1101
  15.6 4.2 %all-to-all-start = ((bf16[8,144,384]{2,1,0:T(8,128)(2,1)}), bf16[8,144,384]{2,1,0:T(8,128)(2,1)}, u32[]{:S(2)}, u32[]{:S(2)}) async-start(bf16[8,144,384]{2,1,0:T(8,128)(2,1)} %get-tuple-element.62), calls=%async_computation | async-start | bytes 1769472 | tf_op jit(solution)/shard_map/all_to_all | solution.py:1167
  28.0 5.1 %all-to-all-done.refs_1_.refs_3_ = bf16[8,144,384]{2,1,0:T(8,128)(2,1)} async-done(((bf16[8,144,384]{2,1,0:T(8,128)(2,1)}), bf16[8,144,384]{2,1,0:T(8,128)(2,1)}, u32[]{:S(2)}, u32[]{:S(2)}) %all-to-all-start) | async-done | bytes 884768 | tf_op jit(solution)/shard_map/all_to_all | solution.py:1167
  33.1 4.2 %project.1 = (bf16[512,1024]{1,0:T(8,128)(2,1)}, bf16[512,128]{1,0:T(8,128)(2,1)}, bf16[4,768,256]{2,1,0:T(8,128)(2,1)}, f32[2,1024]{1,0:T(2,128)}, s32[8,2048]{...) custom-call(s32[4]{0:T(128)} %pad_add_fusion.place_ref.refs_0_, ...), custom_call_target="tpu_custom_call" | custom-call | flops 55000000 | bytes 5000 | tf_op jit(solution)/shard_map/project/pallas_call | solution.py:42
  37.4 4.3 %all-to-all-start.1 = ((bf16[4,768,256]{2,1,0:T(8,128)(2,1)}), bf16[4,768,256]{2,1,0:T(8,128)(2,1)}, u32[]{:S(2)}, u32[]{:S(2)}) async-start(bf16[4,768,256]{2,1,0:T(8,128)(2,1)} %get-tuple-element.70), calls=%async_computation.1 | async-start | bytes 3145728 | tf_op jit(solution)/shard_map/all_to_all | solution.py:1176
  46.0 11.9 %bias_scores.1.bias_ref = s32[512,2048]{1,0:T(8,128)} custom-call(s32[4]{0:T(128)} %pad_add_fusion.place_ref.refs_0_, s32[3,512,128]{2,1,0:T(8,128)} %get-tuple-element.66.meta_ref, s32[8,2048]{1,0:T(8,128)} %get-tuple-element.67.key_ref, f32[8,128]{1,0:T(8,128)} %get-tuple-element.68.table_ref, bf16[4,528,128]{2,1,0:T(8,128)(2,1)} %collective-permute-done.4.refs_0_.refs_2_, ...), custom_call_target="tpu_custom_call" | custom-call | flops 11000000512 | bytes 1000000 | tf_op jit(solution)/shard_map/bias_scores/pallas_call | solution.py:359
  60.5 9.5 %attend.1 = (bf16[2,512,2048]{2,1,0:T(8,128)(2,1)}, f32[512,128]{1,0:T(8,128)}, bf16[256,128]{1,0:T(8,128)(2,1)}, bf16[256,128]{1,0:T(8,128)(2,1)}) custom-call(s32[4]{0:T(128)} %pad_add_fusion.place_ref.refs_0_, bf16[512,128]{1,0:T(8,128)(2,1)} %get-tuple-element.65.query_ref, s32[512,2048]{1,0:T(8,128)} %bias_scores.1.bias_ref, ...), custom_call_target="tpu_custom_call" | custom-call | flops 9900000256 | bytes 900000 | tf_op jit(solution)/shard_map/attend/pallas_call | solution.py:441
  79.6 3.0 %collective-permute-start.12 = (bf16[128,1024]{1,0:T(8,128)(2,1)S(1)}, bf16[128,1024]{1,0:T(8,128)(2,1)S(1)}, u32[]{:S(2)}, u32[]{:S(2)}) collective-permute-start(bf16[128,1024]{1,0:T(8,128)(2,1)S(1)} %add.29.refs_0_), channel_id=1, source_target_pairs={{0,2},{1,3},{2,0},{3,1},{4,6},{5,7},{6,4},{7,5},{8,10},{9,11},{10,... | collective-permute-start | bytes 786440 | tf_op jit(solution)/shard_map/ppermute | solution.py:1073
  82.6 4.1 %ffn_prepare.1 = (bf16[4,352,1024]{2,1,0:T(8,128)(2,1)S(1)}, bf16[4,176,1024]{2,1,0:T(8,128)(2,1)S(1)}, f32[4,176,256]{2,1,0:T(8,128)S(1)}) custom-call(s32[4]{0:T(128)S(1)} %copy-done.15, bf16[256,1024]{1,0:T(8,128)(2,1)S(1)} %copy-done.18, bf16[4,528,128]{2,1,0:T(8,128)(2,1)} %stack.21.refs_0_, ...), custom_call_target="tpu_custom_call" | custom-call | flops 4400000000 | bytes 400000 | tf_op jit(solution)/shard_map/ffn_prepare/pallas_call | solution.py:533
  86.7 2.8 %collective-permute-done.12.refs_1_ = bf16[128,1024]{1,0:T(8,128)(2,1)S(1)} collective-permute-done((bf16[128,1024]{1,0:T(8,128)(2,1)S(1)}, bf16[128,1024]{1,0:T(8,128)(2,1)S(1)}, u32[]{:S(2)}, u32[]{:S(2)}) %collective-permute-start.12) | collective-permute-done | bytes 262176 | tf_op jit(solution)/shard_map/ppermute | solution.py:1073
  91.4 5.7 %ffn_forward.1 = (bf16[256,1024]{1,0:T(8,128)(2,1)S(1)}, bf16[4,528,256]{2,1,0:T(8,128)(2,1)S(1)}, bf16[128,1024]{1,0:T(8,128)(2,1)S(1)}, bf16[128,1024]{1,0:T(8,128)(2,1)S(1)}) custom-call(s32[4]{0:T(128)S(1)} %copy-done.15, bf16[256,1024]{1,0:T(8,128)(2,1)S(1)} %copy-done.4, bf16[128,1024]{1,0:T(8,128)(2,1)S(1)} %add.30.total_ref.refs_2_, ...), custom_call_target="tpu_custom_call" | custom-call | flops 5500000256 | bytes 500000 | tf_op jit(solution)/shard_map/ffn_forward/pallas_call | solution.py:593
  98.8 3.0 %collective-permute-start.16 = (bf16[128,1024]{1,0:T(8,128)(2,1)S(1)}, bf16[128,1024]{1,0:T(8,128)(2,1)S(1)}, u32[]{:S(2)}, u32[]{:S(2)}) collective-permute-start(bf16[128,1024]{1,0:T(8,128)(2,1)S(1)} %add.31.refs_0_), channel_id=1, source_target_pairs={{0,2},{1,3},{2,0},{3,1},{4,6},{5,7},{6,4},{7,5},{8,10},{9,11},{10,... | collective-permute-start | bytes 786440 | tf_op jit(solution)/shard_map/ppermute | solution.py:1073
  106.2 4.9 %all-to-all-start.2 = ((bf16[4,528,1024]{2,1,0:T(8,128)(2,1)}), bf16[4,528,1024]{2,1,0:T(8,128)(2,1)}, u32[]{:S(2)}, u32[]{:S(2)}) async-start(bf16[4,528,1024]{2,1,0:T(8,128)(2,1)} %copy-done), calls=%async_computation.2 | async-start | bytes 8650752 | tf_op jit(solution)/shard_map/all_to_all | solution.py:1204
  125.3 7.4 %attend_back.1 = (bf16[2,512,2048]{2,1,0:T(8,128)(2,1)S(1)}, bf16[256,512]{1,0:T(8,128)(2,1)S(1)}, bf16[256,512]{1,0:T(8,128)(2,1)S(1)}, bf16[256,512]{1,0:T(8,1...) custom-call(s32[4]{0:T(128)S(1)} %copy-done.15, bf16[512,128]{1,0:T(8,128)(2,1)S(1)} %copy-done.19, ...), custom_call_target="tpu_custom_call" | custom-call | flops 5500000256 | bytes 500000 | tf_op jit(solution)/shard_map/attend_back/pallas_call | solution.py:841
  139.2 14.8 %table_grad.1.refs_9_ = f32[8,128]{1,0:T(8,128)S(1)} custom-call(s32[3,512,128]{2,1,0:T(8,128)S(1)} %copy-done.17, s32[8,2048]{1,0:T(8,128)S(1)} %copy-done.20, bf16[2,512,2048]{2,1,0:T(8,128)(2,1)S(1)} %get-tuple-element.93.score_ref, bf16[128,1024]{1,0:T(8,128)(2,1)S(1)} %collective-permute-done.19.refs_0_.refs_1_), custom_call_target="tpu_custom_call" | custom-call | flops 12099999744 | bytes 1100000 | tf_op jit(solution)/shard_map/table_grad/pallas_call | solution.py:929
  154.0 3.7 %weight_grads.1 = (bf16[640,1024]{1,0:T(8,128)(2,1)S(1)}, bf16[16,1024]{1,0:T(8,128)(2,1)S(1)}, bf16[16,1024]{1,0:T(8,128)(2,1)S(1)}, bf16[2,128,1024]{2,1,0:T(8,128)(2,1)S(1)}, bf16[2,128,1024]{2,1,0:T(8,128)(2,1)}) custom-call(s32[4]{0:T(128)S(1)} %copy-done.15, bf16[512,128]{1,0:T(8,128)(2,1)S(1)} %get-tuple-element.89.refs_1_, ...), custom_call_target="tpu_custom_call" | custom-call | flops 4400000000 | bytes 400000 | tf_op jit(solution)/shard_map/weight_grads/pallas_call | solution.py:42
  158.7 2.9 %all-to-all-done.2.parts_ref = bf16[4,528,1024]{2,1,0:T(8,128)(2,1)} async-done(((bf16[4,528,1024]{2,1,0:T(8,128)(2,1)}), bf16[4,528,1024]{2,1,0:T(8,128)(2,1)}, u32[]{:S(2)}, u32[]{:S(2)}) %all-to-all-start.2) | async-done | bytes 4325408 | tf_op jit(solution)/shard_map/all_to_all | solution.py:1204
  161.6 3.5 %all-to-all-start.3 = ((bf16[4,160,1024]{2,1,0:T(8,128)(2,1)}), bf16[4,160,1024]{2,1,0:T(8,128)(2,1)S(1)}, u32[]{:S(2)}, u32[]{:S(2)}) async-start(bf16[4,160,1024]{2,1,0:T(8,128)(2,1)} %bitcast.35), calls=%async_computation.3 | async-start | bytes 2621440 | tf_op jit(solution)/shard_map/all_to_all | solution.py:1227
  165.2 3.1 %fold_to_blocks.1 = bf16[2,4,528,128]{3,2,1,0:T(8,128)(2,1)S(1)} custom-call(s32[4]{0:T(128)S(1)} %copy-done.15, bf16[4,528,1024]{2,1,0:T(8,128)(2,1)} %all-to-all-done.2.parts_ref, bf16[2,128,1024]{2,1,0:T(8,128)(2,1)} %get-tuple-element.98.refs_0_), custom_call_target="tpu_custom_call" | custom-call | flops 4400000000 | bytes 400000 | tf_op jit(solution)/shard_map/fold_to_blocks/pallas_call | solution.py:759
  173.4 8.6 %collective-permute-done.24.refs_1_ = bf16[4,528,128]{2,1,0:T(8,128)(2,1)S(1)} collective-permute-done((bf16[4,528,128]{2,1,0:T(8,128)(2,1)S(1)}, bf16[4,528,128]{2,1,0:T(8,128)(2,1)S(1)}, u32[]{:S(2)}, u32[]{:S(2)}) %collective-permute-start.24) | collective-permute-done | bytes 540704 | tf_op jit(solution)/shard_map/ppermute | solution.py:1073
  184.5 4.0 %all-to-all-start.4 = ((bf16[8,176,128]{2,1,0:T(8,128)(2,1)}), bf16[8,176,128]{2,1,0:T(8,128)(2,1)S(1)}, u32[]{:S(2)}, u32[]{:S(2)}) async-start(bf16[8,176,128]{2,1,0:T(8,128)(2,1)} %spread.1), calls=%async_computation.4 | async-start | bytes 720896 | tf_op jit(solution)/shard_map/all_to_all | solution.py:1232
  195.2 3.2 %collective-permute-done.27.refs_1_ = bf16[128,1024]{1,0:T(8,128)(2,1)S(1)} collective-permute-done((bf16[128,1024]{1,0:T(8,128)(2,1)}, bf16[128,1024]{1,0:T(8,128)(2,1)S(1)}, u32[]{:S(2)}, u32[]{:S(2)}) %collective-permute-start.27) | collective-permute-done | bytes 262176 | tf_op jit(solution)/shard_map/ppermute | solution.py:1073
  198.4 3.1 %collective-permute-start.28 = (bf16[128,1024]{1,0:T(8,128)(2,1)S(1)}, bf16[128,1024]{1,0:T(8,128)(2,1)S(1)}, u32[]{:S(2)}, u32[]{:S(2)}) collective-permute-start(bf16[128,1024]{1,0:T(8,128)(2,1)S(1)} %add.37.refs_0_), channel_id=1, source_target_pairs={{0,2},{1,3},{2,0},{3,1},{4,6},{5,7},{6,4},{7,5},{8,10},{9,11},{10,... | collective-permute-start | bytes 786440 | tf_op jit(solution)/shard_map/ppermute | solution.py:1073
  201.7 3.2 %collective-permute-start.37 = (bf16[880,128]{1,0:T(8,128)(2,1)S(1)}, bf16[880,128]{1,0:T(8,128)(2,1)S(1)}, u32[]{:S(2)}, u32[]{:S(2)}) collective-permute-start(bf16[880,128]{1,0:T(8,128)(2,1)S(1)} %fold_bundle.1.refs_0_), channel_id=1, source_target_pairs={{0,64},{32,96},{64,0},{96,32},{1,65},{33,97},{65,1},{97,33},{2,66}... | collective-permute-start | bytes 675848 | tf_op jit(solution)/shard_map/ppermute | solution.py:1093
  (169 shorter events, 93.6 us)
Async XLA Ops:
  3.3 16.5 %collective-permute-start = (bf16[288,1024]{1,0:T(8,128)(2,1)}, bf16[288,1024]{1,0:T(8,128)(2,1)}, u32[]{:S(2)}, u32[]{:S(2)}) collective-permute-start(bf16[288,1024]{1,0:T(8,128)(2,1)} %maximum_maximum_fusion), channel_id=1, source_target_pairs={{0,16},{4,20},{8,24},{12,28},{16,0},{20,4},{24,8},{28,12},{1,17},{... | collective-permute-start | bytes 1769480 | tf_op jit(solution)/shard_map/ppermute | solution.py:1073
  9.0 12.3 %collective-permute-start.3 = (bf16[528,128]{1,0:T(8,128)(2,1)}, bf16[528,128]{1,0:T(8,128)(2,1)S(1)}, u32[]{:S(2)}, u32[]{:S(2)}) collective-permute-start(bf16[528,128]{1,0:T(8,128)(2,1)} %get-tuple-element.69.refs_0_), channel_id=1, source_target_pairs={{0,4},{4,8},{8,12},{12,0},{16,20},{20,24},{24,28},{28,16},{1,5},{5... | collective-permute-start | bytes 405512 | tf_op jit(solution)/shard_map/ppermute | solution.py:1101
  15.6 17.5 %all-to-all-start = ((bf16[8,144,384]{2,1,0:T(8,128)(2,1)}), bf16[8,144,384]{2,1,0:T(8,128)(2,1)}, u32[]{:S(2)}, u32[]{:S(2)}) async-start(bf16[8,144,384]{2,1,0:T(8,128)(2,1)} %get-tuple-element.62), calls=%async_computation | async-start | bytes 1769472 | tf_op jit(solution)/shard_map/all_to_all | solution.py:1167
  22.9 19.6 %collective-permute-start.6 = (bf16[4,528,128]{2,1,0:T(8,128)(2,1)}, bf16[4,528,128]{2,1,0:T(8,128)(2,1)}, u32[]{:S(2)}, u32[]{:S(2)}) collective-permute-start(bf16[4,528,128]{2,1,0:T(8,128)(2,1)} %stack.21.refs_0_), channel_id=1, source_target_pairs={{0,16},{4,20},{8,24},{12,28},{16,0},{20,4},{24,8},{28,12},{1,17},{... | collective-permute-start | bytes 1622024 | tf_op jit(solution)/shard_map/ppermute | solution.py:1073
  24.8 20.5 %collective-permute-start.4 = (bf16[4,528,128]{2,1,0:T(8,128)(2,1)}, bf16[4,528,128]{2,1,0:T(8,128)(2,1)}, u32[]{:S(2)}, u32[]{:S(2)}) collective-permute-start(bf16[4,528,128]{2,1,0:T(8,128)(2,1)} %stack.21.refs_0_), channel_id=1, source_target_pairs={{0,32},{32,64},{64,96},{96,0},{1,33},{33,65},{65,97},{97,1},{2,34}... | collective-permute-start | bytes 1622024 | tf_op jit(solution)/shard_map/ppermute | solution.py:1093
  26.3 19.8 %collective-permute-start.5 = (bf16[4,528,128]{2,1,0:T(8,128)(2,1)}, bf16[4,528,128]{2,1,0:T(8,128)(2,1)}, u32[]{:S(2)}, u32[]{:S(2)}) collective-permute-start(bf16[4,528,128]{2,1,0:T(8,128)(2,1)} %stack.21.refs_0_), channel_id=1, source_target_pairs={{0,96},{32,0},{64,32},{96,64},{1,97},{33,1},{65,33},{97,65},{2,98}... | collective-permute-start | bytes 1622024 | tf_op jit(solution)/shard_map/ppermute | solution.py:1093
  37.4 23.1 %all-to-all-start.1 = ((bf16[4,768,256]{2,1,0:T(8,128)(2,1)}), bf16[4,768,256]{2,1,0:T(8,128)(2,1)}, u32[]{:S(2)}, u32[]{:S(2)}) async-start(bf16[4,768,256]{2,1,0:T(8,128)(2,1)} %get-tuple-element.70), calls=%async_computation.1 | async-start | bytes 3145728 | tf_op jit(solution)/shard_map/all_to_all | solution.py:1176
  42.5 15.4 %collective-permute-start.9 = (bf16[4,528,128]{2,1,0:T(8,128)(2,1)}, bf16[4,528,128]{2,1,0:T(8,128)(2,1)}, u32[]{:S(2)}, u32[]{:S(2)}) collective-permute-start(bf16[4,528,128]{2,1,0:T(8,128)(2,1)} %collective-permute-done.6.refs_0_.refs_1_), channel_id=1, source_target_pairs={{0,96},{32,0},{64,32},{96,64},{1,97},{33,1},{65,33},{97,65},{2,98}... | collective-permute-start | bytes 1622024 | tf_op jit(solution)/shard_map/ppermute | solution.py:1093
  45.3 26.9 %collective-permute-start.8 = (bf16[4,528,128]{2,1,0:T(8,128)(2,1)}, bf16[4,528,128]{2,1,0:T(8,128)(2,1)}, u32[]{:S(2)}, u32[]{:S(2)}) collective-permute-start(bf16[4,528,128]{2,1,0:T(8,128)(2,1)} %collective-permute-done.6.refs_0_.refs_1_), channel_id=1, source_target_pairs={{0,32},{32,64},{64,96},{96,0},{1,33},{33,65},{65,97},{97,1},{2,34}... | collective-permute-start | bytes 1622024 | tf_op jit(solution)/shard_map/ppermute | solution.py:1093
  45.3 26.9 %collective-permute-start.10 = (bf16[4,528,128]{2,1,0:T(8,128)(2,1)}, bf16[4,528,128]{2,1,0:T(8,128)(2,1)}, u32[]{:S(2)}, u32[]{:S(2)}) collective-permute-start(bf16[4,528,128]{2,1,0:T(8,128)(2,1)} %collective-permute-done.4.refs_0_.refs_2_), channel_id=1, source_target_pairs={{0,32},{32,64},{64,96},{96,0},{1,33},{33,65},{65,97},{97,1},{2,34}... | collective-permute-start | bytes 1622024 | tf_op jit(solution)/shard_map/ppermute | solution.py:1093
  57.9 24.6 %collective-permute-start.13 = (bf16[4,528,128]{2,1,0:T(8,128)(2,1)}, bf16[4,528,128]{2,1,0:T(8,128)(2,1)}, u32[]{:S(2)}, u32[]{:S(2)}) collective-permute-start(bf16[4,528,128]{2,1,0:T(8,128)(2,1)} %collective-permute-done.9.refs_5_), channel_id=1, source_target_pairs={{0,96},{32,0},{64,32},{96,64},{1,97},{33,1},{65,33},{97,65},{2,98}... | collective-permute-start | bytes 1622024 | tf_op jit(solution)/shard_map/ppermute | solution.py:1093
  98.8 12.3 %collective-permute-start.16 = (bf16[128,1024]{1,0:T(8,128)(2,1)S(1)}, bf16[128,1024]{1,0:T(8,128)(2,1)S(1)}, u32[]{:S(2)}, u32[]{:S(2)}) collective-permute-start(bf16[128,1024]{1,0:T(8,128)(2,1)S(1)} %add.31.refs_0_), channel_id=1, source_target_pairs={{0,2},{1,3},{2,0},{3,1},{4,6},{5,7},{6,4},{7,5},{8,10},{9,11},{10,... | collective-permute-start | bytes 786440 | tf_op jit(solution)/shard_map/ppermute | solution.py:1073
  106.2 55.4 %all-to-all-start.2 = ((bf16[4,528,1024]{2,1,0:T(8,128)(2,1)}), bf16[4,528,1024]{2,1,0:T(8,128)(2,1)}, u32[]{:S(2)}, u32[]{:S(2)}) async-start(bf16[4,528,1024]{2,1,0:T(8,128)(2,1)} %copy-done), calls=%async_computation.2 | async-start | bytes 8650752 | tf_op jit(solution)/shard_map/all_to_all | solution.py:1204
  122.4 16.7 %collective-permute-start.19 = (bf16[128,1024]{1,0:T(8,128)(2,1)S(1)}, bf16[128,1024]{1,0:T(8,128)(2,1)S(1)}, u32[]{:S(2)}, u32[]{:S(2)}) collective-permute-start(bf16[128,1024]{1,0:T(8,128)(2,1)S(1)} %add.33.refs_0_), channel_id=1, source_target_pairs={{0,2},{1,3},{2,0},{3,1},{4,6},{5,7},{6,4},{7,5},{8,10},{9,11},{10,... | collective-permute-start | bytes 786440 | tf_op jit(solution)/shard_map/ppermute | solution.py:1073
  132.8 21.2 %collective-permute-start.21 = (bf16[256,512]{1,0:T(8,128)(2,1)S(1)}, bf16[256,512]{1,0:T(8,128)(2,1)S(1)}, u32[]{:S(2)}, u32[]{:S(2)}) collective-permute-start(bf16[256,512]{1,0:T(8,128)(2,1)S(1)} %get-tuple-element.95), channel_id=1, source_target_pairs={{0,4},{4,8},{8,12},{12,0},{16,20},{20,24},{24,28},{28,16},{1,5},{5... | collective-permute-start | bytes 786440 | tf_op jit(solution)/shard_map/ppermute | solution.py:1101
  134.8 19.1 %collective-permute-start.22 = (bf16[256,512]{1,0:T(8,128)(2,1)S(1)}, bf16[256,512]{1,0:T(8,128)(2,1)S(1)}, u32[]{:S(2)}, u32[]{:S(2)}) collective-permute-start(bf16[256,512]{1,0:T(8,128)(2,1)S(1)} %get-tuple-element.96), channel_id=1, source_target_pairs={{0,8},{4,12},{8,0},{12,4},{16,24},{20,28},{24,16},{28,20},{1,9},{5... | collective-permute-start | bytes 786440 | tf_op jit(solution)/shard_map/ppermute | solution.py:1101
  137.4 16.6 %collective-permute-start.23 = (bf16[256,512]{1,0:T(8,128)(2,1)S(1)}, bf16[256,512]{1,0:T(8,128)(2,1)S(1)}, u32[]{:S(2)}, u32[]{:S(2)}) collective-permute-start(bf16[256,512]{1,0:T(8,128)(2,1)S(1)} %get-tuple-element.97), channel_id=1, source_target_pairs={{0,12},{4,0},{8,4},{12,8},{16,28},{20,16},{24,20},{28,24},{1,13},{... | collective-permute-start | bytes 786440 | tf_op jit(solution)/shard_map/ppermute | solution.py:1101
  161.6 21.9 %all-to-all-start.3 = ((bf16[4,160,1024]{2,1,0:T(8,128)(2,1)}), bf16[4,160,1024]{2,1,0:T(8,128)(2,1)S(1)}, u32[]{:S(2)}, u32[]{:S(2)}) async-start(bf16[4,160,1024]{2,1,0:T(8,128)(2,1)} %bitcast.35), calls=%async_computation.3 | async-start | bytes 2621440 | tf_op jit(solution)/shard_map/all_to_all | solution.py:1227
  168.4 13.6 %collective-permute-start.24 = (bf16[4,528,128]{2,1,0:T(8,128)(2,1)S(1)}, bf16[4,528,128]{2,1,0:T(8,128)(2,1)S(1)}, u32[]{:S(2)}, u32[]{:S(2)}) collective-permute-start(bf16[4,528,128]{2,1,0:T(8,128)(2,1)S(1)} %get-tuple-element.112), channel_id=1, source_target_pairs={{0,16},{4,20},{8,24},{12,28},{16,0},{20,4},{24,8},{28,12},{1,17},{... | collective-permute-start | bytes 1622024 | tf_op jit(solution)/shard_map/ppermute | solution.py:1073
  169.8 12.2 %collective-permute-start.26 = (bf16[2,128,1024]{2,1,0:T(8,128)(2,1)}, bf16[2,128,1024]{2,1,0:T(8,128)(2,1)S(1)}, u32[]{:S(2)}, u32[]{:S(2)}) collective-permute-start(bf16[2,128,1024]{2,1,0:T(8,128)(2,1)} %get-tuple-element.98.refs_0_), channel_id=1, source_target_pairs={{0,1},{1,0},{2,3},{3,2},{4,5},{5,4},{6,7},{7,6},{8,9},{9,8},{10,11... | collective-permute-start | bytes 1572872 | tf_op jit(solution)/shard_map/ppermute | solution.py:1073
  171.5 12.1 %collective-permute-start.31 = (bf16[16,1024]{1,0:T(8,128)(2,1)S(1)}, bf16[16,1024]{1,0:T(8,128)(2,1)S(1)}, u32[]{:S(2)}, u32[]{:S(2)}) collective-permute-start(bf16[16,1024]{1,0:T(8,128)(2,1)S(1)} %add.39.refs_2_), channel_id=1, source_target_pairs={{0,2},{1,3},{2,0},{3,1},{4,6},{5,7},{6,4},{7,5},{8,10},{9,11},{10,... | collective-permute-start | bytes 98312 | tf_op jit(solution)/shard_map/ppermute | solution.py:1073
  184.5 17.1 %all-to-all-start.4 = ((bf16[8,176,128]{2,1,0:T(8,128)(2,1)}), bf16[8,176,128]{2,1,0:T(8,128)(2,1)S(1)}, u32[]{:S(2)}, u32[]{:S(2)}) async-start(bf16[8,176,128]{2,1,0:T(8,128)(2,1)} %spread.1), calls=%async_computation.4 | async-start | bytes 720896 | tf_op jit(solution)/shard_map/all_to_all | solution.py:1232
  190.6 11.0 %collective-permute-start.34 = (bf16[528,128]{1,0:T(8,128)(2,1)S(1)}, bf16[528,128]{1,0:T(8,128)(2,1)S(1)}, u32[]{:S(2)}, u32[]{:S(2)}) collective-permute-start(bf16[528,128]{1,0:T(8,128)(2,1)S(1)} %get-tuple-element.114), channel_id=1, source_target_pairs={{0,12},{4,0},{8,4},{12,8},{16,28},{20,16},{24,20},{28,24},{1,13},{... | collective-permute-start | bytes 405512 | tf_op jit(solution)/shard_map/ppermute | solution.py:1101
  195.1 11.8 %collective-permute-start.25 = (bf16[128,1024]{1,0:T(8,128)(2,1)S(1)}, bf16[128,1024]{1,0:T(8,128)(2,1)S(1)}, u32[]{:S(2)}, u32[]{:S(2)}) collective-permute-start(bf16[128,1024]{1,0:T(8,128)(2,1)S(1)} %add.35.refs_4_), channel_id=1, source_target_pairs={{0,1},{1,0},{2,3},{3,2},{4,5},{5,4},{6,7},{7,6},{8,9},{9,8},{10,11... | collective-permute-start | bytes 786440 | tf_op jit(solution)/shard_map/ppermute | solution.py:1073
  (52 other events, 348.9 us)

commit v5 on v4

--- a/solution.py
+++ b/solution.py
@@ -566,14 +566,16 @@
         turned[...] = jnp.transpose(normed)
         sums[...] = jnp.zeros_like(sums)
 
-    gates = jnp.dot(weight_ref[0], turned[...], preferred_element_type=F32)
-    gate, upward = gates[:units], gates[units:]
-    hidden_grad = hidden_grad_ref[0]
-    value, slope = gelu_parts(gate)
-    grads = jnp.concatenate([hidden_grad * upward * slope, hidden_grad * value], axis=0).astype(BF16)
-    parts_ref[0, : 2 * units, :] = grads
-    parts_ref[0, 2 * units :, :] = (value * upward).astype(BF16)
-    sums[...] += contract_rows(grads, weight_ref[0])
+    for hop in range(weight_ref.shape[0]):
+        gates = jnp.dot(weight_ref[hop], turned[...], preferred_element_type=F32)
+        gate, upward = gates[:units], gates[units:]
+        hidden_grad = hidden_grad_ref[hop]
+        value, slope = gelu_parts(gate)
+        grads = jnp.concatenate([hidden_grad * upward * slope, hidden_grad * value], axis=0)
+        grads = grads.astype(BF16)
+        parts_ref[hop, : 2 * units, :] = grads
+        parts_ref[hop, 2 * units :, :] = (value * upward).astype(BF16)
+        sums[...] += contract_rows(grads, weight_ref[hop])
 
     @pl.when(step == pl.num_programs(0) - 1)
     def _():
@@ -588,11 +590,11 @@
     out = [shape((rows, model), BF16), parts, half, half]
 
     def chunk(item):
-        return pl.BlockSpec((1,) + item.shape[1:], lambda s: (s, 0, 0))
+        return pl.BlockSpec((2,) + item.shape[1:], lambda s: (s, 0, 0))
 
     return pl.pallas_call(
         ffn_kernel,
-        grid=(hops,),
+        grid=(hops // 2,),
         in_specs=[SMEM]
         + whole(tokens, total, got, gains)
         + [chunk(hidden_grad), chunk(weights)],
@@ -619,7 +621,7 @@
 def ffn_output_kernel(place_ref, parts_ref, weight_ref, *refs):
     keep_ref, send_ref, sums = refs[-3:]
     step = pl.program_id(0)
-    part = contract_rows(parts_ref[0], weight_ref[0])
+    part = contract_rows(parts_ref[0], weight_ref[0]) + contract_rows(parts_ref[1], weight_ref[1])
 
     @pl.when(step == 0)
     def _():
@@ -640,11 +642,11 @@
     half = shape((rows // 2, model), BF16)
     return pl.pallas_call(
         ffn_output_kernel,
-        grid=(hops,),
+        grid=(hops // 2,),
         in_specs=[
             SMEM,
-            pl.BlockSpec((1, height // 3, rows), lambda s: (s, 2, 0)),
-            pl.BlockSpec((1, height // 3, model), lambda s: (s, 0, 0)),
+            pl.BlockSpec((2, height // 3, rows), lambda s: (s, 2, 0)),
+            pl.BlockSpec((2, height // 3, model), lambda s: (s, 0, 0)),
         ]
         + [HBM] * len(deps),
         out_specs=whole(half, half),

time: 220 us -> 219 us (level)
  no operation moved by 1% of the time
where the time goes in v5:
time: 219 us; the launch traced here: 218 us
  Pallas kernels  84.5 us (39%)
  starting transfers between devices  77.9 us (36%)
  waiting for transfers between devices  39.9 us (18%)
  local copies, waits for them, and re-layouts  11.8 us (5%)
  other arithmetic  2.49 us (1%)
    ppermute x20, waiting for transfers between devices, swap(): lax.ppermute(values, axis_name, [(at, at ^ bit) for at in range(count)])  26.4 us
    ppermute x20, starting transfers between devices, swap(): lax.ppermute(values, axis_name, [(at, at ^ bit) for at in range(count)])  25.1 us
    pallas_call x21, Pallas kernels, simple(): pl.pallas_call(body, grid=(1,), in_specs=[SMEM] * (place is not None) + w...  19.9 us
    ppermute x9, starting transfers between devices, turn_z(): lax.ppermute(values, 'blk', [(at, at // 4 * 4 + (at - hop) % 4) for at in...  17.4 us
    pallas_call x1, Pallas kernels, table_grad_sums(): pl.pallas_call(table_grad_kernel, grid=(6,), in_specs=whole(meta, key_met...  14.8 us
    ppermute x9, starting transfers between devices, step_dp(): return lax.ppermute(values, 'dp', [(at, (at + hop) % 4) for at in range(4)])  14.5 us
    pallas_call x1, Pallas kernels, bias_scores(): pl.pallas_call(bias_kernel, grid=(rows // chunk,), in_specs=[pl.BlockSpec...  11.9 us
    pallas_call x1, Pallas kernels, attend(): pl.pallas_call(attend_kernel, grid=(rows // tile,), in_specs=[SMEM, slim,...  9.52 us
  transfers between devices with their start and end apart: 43, of which 17 were waited for; matrix products, arithmetic and copies ran while one was open for 1% of the time, Pallas kernels for 35%

profile of v5, /device:TPU:0, one launch (start us, length us, event | category | flops | bytes accessed | tf_op | source)
XLA Modules:
  0.0 217.8 jit_solution(17046061603341394870)
XLA Ops:
  11.0 3.6 %collective-permute-start.2 = (bf16[528,128]{1,0:T(8,128)(2,1)}, bf16[528,128]{1,0:T(8,128)(2,1)S(1)}, u32[]{:S(2)}, u32[]{:S(2)}) collective-permute-start(bf16[528,128]{1,0:T(8,128)(2,1)} %get-tuple-element.69.refs_0_), channel_id=1, source_target_pairs={{0,8},{4,12},{8,0},{12,4},{16,24},{20,28},{24,16},{28,20},{1,9},{5... | collective-permute-start | bytes 405512 | tf_op jit(solution)/shard_map/ppermute | solution.py:1103
  15.6 4.2 %all-to-all-start = ((bf16[8,144,384]{2,1,0:T(8,128)(2,1)}), bf16[8,144,384]{2,1,0:T(8,128)(2,1)}, u32[]{:S(2)}, u32[]{:S(2)}) async-start(bf16[8,144,384]{2,1,0:T(8,128)(2,1)} %get-tuple-element.62), calls=%async_computation | async-start | bytes 1769472 | tf_op jit(solution)/shard_map/all_to_all | solution.py:1169
  28.0 5.1 %all-to-all-done.refs_1_.refs_3_ = bf16[8,144,384]{2,1,0:T(8,128)(2,1)} async-done(((bf16[8,144,384]{2,1,0:T(8,128)(2,1)}), bf16[8,144,384]{2,1,0:T(8,128)(2,1)}, u32[]{:S(2)}, u32[]{:S(2)}) %all-to-all-start) | async-done | bytes 884768 | tf_op jit(solution)/shard_map/all_to_all | solution.py:1169
  33.1 4.2 %project.1 = (bf16[512,1024]{1,0:T(8,128)(2,1)}, bf16[512,128]{1,0:T(8,128)(2,1)}, bf16[4,768,256]{2,1,0:T(8,128)(2,1)}, f32[2,1024]{1,0:T(2,128)}, s32[8,2048]{...) custom-call(s32[4]{0:T(128)} %pad_add_fusion.place_ref.refs_0_, ...), custom_call_target="tpu_custom_call" | custom-call | flops 55000000 | bytes 5000 | tf_op jit(solution)/shard_map/project/pallas_call | solution.py:42
  37.4 4.3 %all-to-all-start.1 = ((bf16[4,768,256]{2,1,0:T(8,128)(2,1)}), bf16[4,768,256]{2,1,0:T(8,128)(2,1)}, u32[]{:S(2)}, u32[]{:S(2)}) async-start(bf16[4,768,256]{2,1,0:T(8,128)(2,1)} %get-tuple-element.70), calls=%async_computation.1 | async-start | bytes 3145728 | tf_op jit(solution)/shard_map/all_to_all | solution.py:1178
  46.0 11.9 %bias_scores.1.bias_ref = s32[512,2048]{1,0:T(8,128)} custom-call(s32[4]{0:T(128)} %pad_add_fusion.place_ref.refs_0_, s32[3,512,128]{2,1,0:T(8,128)} %get-tuple-element.66.meta_ref, s32[8,2048]{1,0:T(8,128)} %get-tuple-element.67.key_ref, f32[8,128]{1,0:T(8,128)} %get-tuple-element.68.table_ref, bf16[4,528,128]{2,1,0:T(8,128)(2,1)} %collective-permute-done.4.refs_0_.refs_2_, ...), custom_call_target="tpu_custom_call" | custom-call | flops 11000000512 | bytes 1000000 | tf_op jit(solution)/shard_map/bias_scores/pallas_call | solution.py:359
  60.5 9.5 %attend.1 = (bf16[2,512,2048]{2,1,0:T(8,128)(2,1)}, f32[512,128]{1,0:T(8,128)}, bf16[256,128]{1,0:T(8,128)(2,1)}, bf16[256,128]{1,0:T(8,128)(2,1)}) custom-call(s32[4]{0:T(128)} %pad_add_fusion.place_ref.refs_0_, bf16[512,128]{1,0:T(8,128)(2,1)} %get-tuple-element.65.query_ref, s32[512,2048]{1,0:T(8,128)} %bias_scores.1.bias_ref, ...), custom_call_target="tpu_custom_call" | custom-call | flops 9900000256 | bytes 900000 | tf_op jit(solution)/shard_map/attend/pallas_call | solution.py:441
  79.6 3.0 %collective-permute-start.12 = (bf16[128,1024]{1,0:T(8,128)(2,1)S(1)}, bf16[128,1024]{1,0:T(8,128)(2,1)S(1)}, u32[]{:S(2)}, u32[]{:S(2)}) collective-permute-start(bf16[128,1024]{1,0:T(8,128)(2,1)S(1)} %add.29.refs_0_), channel_id=1, source_target_pairs={{0,2},{1,3},{2,0},{3,1},{4,6},{5,7},{6,4},{7,5},{8,10},{9,11},{10,... | collective-permute-start | bytes 786440 | tf_op jit(solution)/shard_map/ppermute | solution.py:1075
  82.6 4.1 %ffn_prepare.1 = (bf16[4,352,1024]{2,1,0:T(8,128)(2,1)S(1)}, bf16[4,176,1024]{2,1,0:T(8,128)(2,1)S(1)}, f32[4,176,256]{2,1,0:T(8,128)S(1)}) custom-call(s32[4]{0:T(128)S(1)} %copy-done.15, bf16[256,1024]{1,0:T(8,128)(2,1)S(1)} %copy-done.18, bf16[4,528,128]{2,1,0:T(8,128)(2,1)} %stack.21.refs_0_, ...), custom_call_target="tpu_custom_call" | custom-call | flops 4400000000 | bytes 400000 | tf_op jit(solution)/shard_map/ffn_prepare/pallas_call | solution.py:533
  86.7 2.8 %collective-permute-done.12.refs_1_ = bf16[128,1024]{1,0:T(8,128)(2,1)S(1)} collective-permute-done((bf16[128,1024]{1,0:T(8,128)(2,1)S(1)}, bf16[128,1024]{1,0:T(8,128)(2,1)S(1)}, u32[]{:S(2)}, u32[]{:S(2)}) %collective-permute-start.12) | collective-permute-done | bytes 262176 | tf_op jit(solution)/shard_map/ppermute | solution.py:1075
  91.4 4.9 %ffn_forward.1 = (bf16[256,1024]{1,0:T(8,128)(2,1)S(1)}, bf16[4,528,256]{2,1,0:T(8,128)(2,1)S(1)}, bf16[128,1024]{1,0:T(8,128)(2,1)S(1)}, bf16[128,1024]{1,0:T(8,128)(2,1)S(1)}) custom-call(s32[4]{0:T(128)S(1)} %copy-done.15, bf16[256,1024]{1,0:T(8,128)(2,1)S(1)} %copy-done.4, bf16[128,1024]{1,0:T(8,128)(2,1)S(1)} %add.30.total_ref.refs_2_, ...), custom_call_target="tpu_custom_call" | custom-call | flops 5500000256 | bytes 500000 | tf_op jit(solution)/shard_map/ffn_forward/pallas_call | solution.py:595
  98.0 3.0 %collective-permute-start.16 = (bf16[128,1024]{1,0:T(8,128)(2,1)S(1)}, bf16[128,1024]{1,0:T(8,128)(2,1)S(1)}, u32[]{:S(2)}, u32[]{:S(2)}) collective-permute-start(bf16[128,1024]{1,0:T(8,128)(2,1)S(1)} %add.31.refs_0_), channel_id=1, source_target_pairs={{0,2},{1,3},{2,0},{3,1},{4,6},{5,7},{6,4},{7,5},{8,10},{9,11},{10,... | collective-permute-start | bytes 786440 | tf_op jit(solution)/shard_map/ppermute | solution.py:1075
  105.4 4.9 %all-to-all-start.2 = ((bf16[4,528,1024]{2,1,0:T(8,128)(2,1)}), bf16[4,528,1024]{2,1,0:T(8,128)(2,1)}, u32[]{:S(2)}, u32[]{:S(2)}) async-start(bf16[4,528,1024]{2,1,0:T(8,128)(2,1)} %copy-done), calls=%async_computation.2 | async-start | bytes 8650752 | tf_op jit(solution)/shard_map/all_to_all | solution.py:1206
  124.0 7.4 %attend_back.1 = (bf16[2,512,2048]{2,1,0:T(8,128)(2,1)S(1)}, bf16[256,512]{1,0:T(8,128)(2,1)S(1)}, bf16[256,512]{1,0:T(8,128)(2,1)S(1)}, bf16[256,512]{1,0:T(8,1...) custom-call(s32[4]{0:T(128)S(1)} %copy-done.15, bf16[512,128]{1,0:T(8,128)(2,1)S(1)} %copy-done.19, ...), custom_call_target="tpu_custom_call" | custom-call | flops 5500000256 | bytes 500000 | tf_op jit(solution)/shard_map/attend_back/pallas_call | solution.py:843
  137.9 14.8 %table_grad.1.refs_9_ = f32[8,128]{1,0:T(8,128)S(1)} custom-call(s32[3,512,128]{2,1,0:T(8,128)S(1)} %copy-done.17, s32[8,2048]{1,0:T(8,128)S(1)} %copy-done.20, bf16[2,512,2048]{2,1,0:T(8,128)(2,1)S(1)} %get-tuple-element.93.score_ref, bf16[128,1024]{1,0:T(8,128)(2,1)S(1)} %collective-permute-done.19.refs_0_.refs_1_), custom_call_target="tpu_custom_call" | custom-call | flops 12099999744 | bytes 1100000 | tf_op jit(solution)/shard_map/table_grad/pallas_call | solution.py:931
  152.7 3.7 %weight_grads.1 = (bf16[640,1024]{1,0:T(8,128)(2,1)S(1)}, bf16[16,1024]{1,0:T(8,128)(2,1)S(1)}, bf16[16,1024]{1,0:T(8,128)(2,1)S(1)}, bf16[2,128,1024]{2,1,0:T(8,128)(2,1)S(1)}, bf16[2,128,1024]{2,1,0:T(8,128)(2,1)}) custom-call(s32[4]{0:T(128)S(1)} %copy-done.15, bf16[512,128]{1,0:T(8,128)(2,1)S(1)} %get-tuple-element.89.refs_1_, ...), custom_call_target="tpu_custom_call" | custom-call | flops 4400000000 | bytes 400000 | tf_op jit(solution)/shard_map/weight_grads/pallas_call | solution.py:42
  157.4 3.4 %all-to-all-done.2.parts_ref = bf16[4,528,1024]{2,1,0:T(8,128)(2,1)} async-done(((bf16[4,528,1024]{2,1,0:T(8,128)(2,1)}), bf16[4,528,1024]{2,1,0:T(8,128)(2,1)}, u32[]{:S(2)}, u32[]{:S(2)}) %all-to-all-start.2) | async-done | bytes 4325408 | tf_op jit(solution)/shard_map/all_to_all | solution.py:1206
  160.9 3.5 %all-to-all-start.3 = ((bf16[4,160,1024]{2,1,0:T(8,128)(2,1)}), bf16[4,160,1024]{2,1,0:T(8,128)(2,1)S(1)}, u32[]{:S(2)}, u32[]{:S(2)}) async-start(bf16[4,160,1024]{2,1,0:T(8,128)(2,1)} %bitcast.35), calls=%async_computation.3 | async-start | bytes 2621440 | tf_op jit(solution)/shard_map/all_to_all | solution.py:1229
  164.4 3.1 %fold_to_blocks.1 = bf16[2,4,528,128]{3,2,1,0:T(8,128)(2,1)S(1)} custom-call(s32[4]{0:T(128)S(1)} %copy-done.15, bf16[4,528,1024]{2,1,0:T(8,128)(2,1)} %all-to-all-done.2.parts_ref, bf16[2,128,1024]{2,1,0:T(8,128)(2,1)} %get-tuple-element.98.refs_0_), custom_call_target="tpu_custom_call" | custom-call | flops 4400000000 | bytes 400000 | tf_op jit(solution)/shard_map/fold_to_blocks/pallas_call | solution.py:761
  172.6 8.6 %collective-permute-done.24.refs_1_ = bf16[4,528,128]{2,1,0:T(8,128)(2,1)S(1)} collective-permute-done((bf16[4,528,128]{2,1,0:T(8,128)(2,1)S(1)}, bf16[4,528,128]{2,1,0:T(8,128)(2,1)S(1)}, u32[]{:S(2)}, u32[]{:S(2)}) %collective-permute-start.24) | collective-permute-done | bytes 540704 | tf_op jit(solution)/shard_map/ppermute | solution.py:1075
  183.8 4.0 %all-to-all-start.4 = ((bf16[8,176,128]{2,1,0:T(8,128)(2,1)}), bf16[8,176,128]{2,1,0:T(8,128)(2,1)S(1)}, u32[]{:S(2)}, u32[]{:S(2)}) async-start(bf16[8,176,128]{2,1,0:T(8,128)(2,1)} %spread.1), calls=%async_computation.4 | async-start | bytes 720896 | tf_op jit(solution)/shard_map/all_to_all | solution.py:1234
  194.4 3.2 %collective-permute-done.27.refs_1_ = bf16[128,1024]{1,0:T(8,128)(2,1)S(1)} collective-permute-done((bf16[128,1024]{1,0:T(8,128)(2,1)}, bf16[128,1024]{1,0:T(8,128)(2,1)S(1)}, u32[]{:S(2)}, u32[]{:S(2)}) %collective-permute-start.27) | collective-permute-done | bytes 262176 | tf_op jit(solution)/shard_map/ppermute | solution.py:1075
  197.7 3.1 %collective-permute-start.28 = (bf16[128,1024]{1,0:T(8,128)(2,1)S(1)}, bf16[128,1024]{1,0:T(8,128)(2,1)S(1)}, u32[]{:S(2)}, u32[]{:S(2)}) collective-permute-start(bf16[128,1024]{1,0:T(8,128)(2,1)S(1)} %add.37.refs_0_), channel_id=1, source_target_pairs={{0,2},{1,3},{2,0},{3,1},{4,6},{5,7},{6,4},{7,5},{8,10},{9,11},{10,... | collective-permute-start | bytes 786440 | tf_op jit(solution)/shard_map/ppermute | solution.py:1075
  200.9 3.2 %collective-permute-start.37 = (bf16[880,128]{1,0:T(8,128)(2,1)S(1)}, bf16[880,128]{1,0:T(8,128)(2,1)S(1)}, u32[]{:S(2)}, u32[]{:S(2)}) collective-permute-start(bf16[880,128]{1,0:T(8,128)(2,1)S(1)} %fold_bundle.1.refs_0_), channel_id=1, source_target_pairs={{0,64},{32,96},{64,0},{96,32},{1,65},{33,97},{65,1},{97,33},{2,66}... | collective-permute-start | bytes 675848 | tf_op jit(solution)/shard_map/ppermute | solution.py:1095
  (169 shorter events, 93.1 us)
Async XLA Ops:
  3.3 16.5 %collective-permute-start = (bf16[288,1024]{1,0:T(8,128)(2,1)}, bf16[288,1024]{1,0:T(8,128)(2,1)}, u32[]{:S(2)}, u32[]{:S(2)}) collective-permute-start(bf16[288,1024]{1,0:T(8,128)(2,1)} %maximum_maximum_fusion), channel_id=1, source_target_pairs={{0,16},{4,20},{8,24},{12,28},{16,0},{20,4},{24,8},{28,12},{1,17},{... | collective-permute-start | bytes 1769480 | tf_op jit(solution)/shard_map/ppermute | solution.py:1075
  9.0 12.3 %collective-permute-start.3 = (bf16[528,128]{1,0:T(8,128)(2,1)}, bf16[528,128]{1,0:T(8,128)(2,1)S(1)}, u32[]{:S(2)}, u32[]{:S(2)}) collective-permute-start(bf16[528,128]{1,0:T(8,128)(2,1)} %get-tuple-element.69.refs_0_), channel_id=1, source_target_pairs={{0,4},{4,8},{8,12},{12,0},{16,20},{20,24},{24,28},{28,16},{1,5},{5... | collective-permute-start | bytes 405512 | tf_op jit(solution)/shard_map/ppermute | solution.py:1103
  15.6 17.5 %all-to-all-start = ((bf16[8,144,384]{2,1,0:T(8,128)(2,1)}), bf16[8,144,384]{2,1,0:T(8,128)(2,1)}, u32[]{:S(2)}, u32[]{:S(2)}) async-start(bf16[8,144,384]{2,1,0:T(8,128)(2,1)} %get-tuple-element.62), calls=%async_computation | async-start | bytes 1769472 | tf_op jit(solution)/shard_map/all_to_all | solution.py:1169
  22.9 19.6 %collective-permute-start.6 = (bf16[4,528,128]{2,1,0:T(8,128)(2,1)}, bf16[4,528,128]{2,1,0:T(8,128)(2,1)}, u32[]{:S(2)}, u32[]{:S(2)}) collective-permute-start(bf16[4,528,128]{2,1,0:T(8,128)(2,1)} %stack.21.refs_0_), channel_id=1, source_target_pairs={{0,16},{4,20},{8,24},{12,28},{16,0},{20,4},{24,8},{28,12},{1,17},{... | collective-permute-start | bytes 1622024 | tf_op jit(solution)/shard_map/ppermute | solution.py:1075
  24.8 20.5 %collective-permute-start.4 = (bf16[4,528,128]{2,1,0:T(8,128)(2,1)}, bf16[4,528,128]{2,1,0:T(8,128)(2,1)}, u32[]{:S(2)}, u32[]{:S(2)}) collective-permute-start(bf16[4,528,128]{2,1,0:T(8,128)(2,1)} %stack.21.refs_0_), channel_id=1, source_target_pairs={{0,32},{32,64},{64,96},{96,0},{1,33},{33,65},{65,97},{97,1},{2,34}... | collective-permute-start | bytes 1622024 | tf_op jit(solution)/shard_map/ppermute | solution.py:1095
  26.3 19.8 %collective-permute-start.5 = (bf16[4,528,128]{2,1,0:T(8,128)(2,1)}, bf16[4,528,128]{2,1,0:T(8,128)(2,1)}, u32[]{:S(2)}, u32[]{:S(2)}) collective-permute-start(bf16[4,528,128]{2,1,0:T(8,128)(2,1)} %stack.21.refs_0_), channel_id=1, source_target_pairs={{0,96},{32,0},{64,32},{96,64},{1,97},{33,1},{65,33},{97,65},{2,98}... | collective-permute-start | bytes 1622024 | tf_op jit(solution)/shard_map/ppermute | solution.py:1095
  37.4 23.1 %all-to-all-start.1 = ((bf16[4,768,256]{2,1,0:T(8,128)(2,1)}), bf16[4,768,256]{2,1,0:T(8,128)(2,1)}, u32[]{:S(2)}, u32[]{:S(2)}) async-start(bf16[4,768,256]{2,1,0:T(8,128)(2,1)} %get-tuple-element.70), calls=%async_computation.1 | async-start | bytes 3145728 | tf_op jit(solution)/shard_map/all_to_all | solution.py:1178
  42.5 15.4 %collective-permute-start.9 = (bf16[4,528,128]{2,1,0:T(8,128)(2,1)}, bf16[4,528,128]{2,1,0:T(8,128)(2,1)}, u32[]{:S(2)}, u32[]{:S(2)}) collective-permute-start(bf16[4,528,128]{2,1,0:T(8,128)(2,1)} %collective-permute-done.6.refs_0_.refs_1_), channel_id=1, source_target_pairs={{0,96},{32,0},{64,32},{96,64},{1,97},{33,1},{65,33},{97,65},{2,98}... | collective-permute-start | bytes 1622024 | tf_op jit(solution)/shard_map/ppermute | solution.py:1095
  45.3 26.9 %collective-permute-start.8 = (bf16[4,528,128]{2,1,0:T(8,128)(2,1)}, bf16[4,528,128]{2,1,0:T(8,128)(2,1)}, u32[]{:S(2)}, u32[]{:S(2)}) collective-permute-start(bf16[4,528,128]{2,1,0:T(8,128)(2,1)} %collective-permute-done.6.refs_0_.refs_1_), channel_id=1, source_target_pairs={{0,32},{32,64},{64,96},{96,0},{1,33},{33,65},{65,97},{97,1},{2,34}... | collective-permute-start | bytes 1622024 | tf_op jit(solution)/shard_map/ppermute | solution.py:1095
  45.3 26.9 %collective-permute-start.10 = (bf16[4,528,128]{2,1,0:T(8,128)(2,1)}, bf16[4,528,128]{2,1,0:T(8,128)(2,1)}, u32[]{:S(2)}, u32[]{:S(2)}) collective-permute-start(bf16[4,528,128]{2,1,0:T(8,128)(2,1)} %collective-permute-done.4.refs_0_.refs_2_), channel_id=1, source_target_pairs={{0,32},{32,64},{64,96},{96,0},{1,33},{33,65},{65,97},{97,1},{2,34}... | collective-permute-start | bytes 1622024 | tf_op jit(solution)/shard_map/ppermute | solution.py:1095
  57.9 24.6 %collective-permute-start.13 = (bf16[4,528,128]{2,1,0:T(8,128)(2,1)}, bf16[4,528,128]{2,1,0:T(8,128)(2,1)}, u32[]{:S(2)}, u32[]{:S(2)}) collective-permute-start(bf16[4,528,128]{2,1,0:T(8,128)(2,1)} %collective-permute-done.9.refs_5_), channel_id=1, source_target_pairs={{0,96},{32,0},{64,32},{96,64},{1,97},{33,1},{65,33},{97,65},{2,98}... | collective-permute-start | bytes 1622024 | tf_op jit(solution)/shard_map/ppermute | solution.py:1095
  98.0 12.3 %collective-permute-start.16 = (bf16[128,1024]{1,0:T(8,128)(2,1)S(1)}, bf16[128,1024]{1,0:T(8,128)(2,1)S(1)}, u32[]{:S(2)}, u32[]{:S(2)}) collective-permute-start(bf16[128,1024]{1,0:T(8,128)(2,1)S(1)} %add.31.refs_0_), channel_id=1, source_target_pairs={{0,2},{1,3},{2,0},{3,1},{4,6},{5,7},{6,4},{7,5},{8,10},{9,11},{10,... | collective-permute-start | bytes 786440 | tf_op jit(solution)/shard_map/ppermute | solution.py:1075
  105.4 55.4 %all-to-all-start.2 = ((bf16[4,528,1024]{2,1,0:T(8,128)(2,1)}), bf16[4,528,1024]{2,1,0:T(8,128)(2,1)}, u32[]{:S(2)}, u32[]{:S(2)}) async-start(bf16[4,528,1024]{2,1,0:T(8,128)(2,1)} %copy-done), calls=%async_computation.2 | async-start | bytes 8650752 | tf_op jit(solution)/shard_map/all_to_all | solution.py:1206
  121.1 16.7 %collective-permute-start.19 = (bf16[128,1024]{1,0:T(8,128)(2,1)S(1)}, bf16[128,1024]{1,0:T(8,128)(2,1)S(1)}, u32[]{:S(2)}, u32[]{:S(2)}) collective-permute-start(bf16[128,1024]{1,0:T(8,128)(2,1)S(1)} %add.33.refs_0_), channel_id=1, source_target_pairs={{0,2},{1,3},{2,0},{3,1},{4,6},{5,7},{6,4},{7,5},{8,10},{9,11},{10,... | collective-permute-start | bytes 786440 | tf_op jit(solution)/shard_map/ppermute | solution.py:1075
  131.4 21.2 %collective-permute-start.21 = (bf16[256,512]{1,0:T(8,128)(2,1)S(1)}, bf16[256,512]{1,0:T(8,128)(2,1)S(1)}, u32[]{:S(2)}, u32[]{:S(2)}) collective-permute-start(bf16[256,512]{1,0:T(8,128)(2,1)S(1)} %get-tuple-element.95), channel_id=1, source_target_pairs={{0,4},{4,8},{8,12},{12,0},{16,20},{20,24},{24,28},{28,16},{1,5},{5... | collective-permute-start | bytes 786440 | tf_op jit(solution)/shard_map/ppermute | solution.py:1103
  133.5 19.1 %collective-permute-start.22 = (bf16[256,512]{1,0:T(8,128)(2,1)S(1)}, bf16[256,512]{1,0:T(8,128)(2,1)S(1)}, u32[]{:S(2)}, u32[]{:S(2)}) collective-permute-start(bf16[256,512]{1,0:T(8,128)(2,1)S(1)} %get-tuple-element.96), channel_id=1, source_target_pairs={{0,8},{4,12},{8,0},{12,4},{16,24},{20,28},{24,16},{28,20},{1,9},{5... | collective-permute-start | bytes 786440 | tf_op jit(solution)/shard_map/ppermute | solution.py:1103
  136.1 16.6 %collective-permute-start.23 = (bf16[256,512]{1,0:T(8,128)(2,1)S(1)}, bf16[256,512]{1,0:T(8,128)(2,1)S(1)}, u32[]{:S(2)}, u32[]{:S(2)}) collective-permute-start(bf16[256,512]{1,0:T(8,128)(2,1)S(1)} %get-tuple-element.97), channel_id=1, source_target_pairs={{0,12},{4,0},{8,4},{12,8},{16,28},{20,16},{24,20},{28,24},{1,13},{... | collective-permute-start | bytes 786440 | tf_op jit(solution)/shard_map/ppermute | solution.py:1103
  160.9 21.9 %all-to-all-start.3 = ((bf16[4,160,1024]{2,1,0:T(8,128)(2,1)}), bf16[4,160,1024]{2,1,0:T(8,128)(2,1)S(1)}, u32[]{:S(2)}, u32[]{:S(2)}) async-start(bf16[4,160,1024]{2,1,0:T(8,128)(2,1)} %bitcast.35), calls=%async_computation.3 | async-start | bytes 2621440 | tf_op jit(solution)/shard_map/all_to_all | solution.py:1229
  167.6 13.6 %collective-permute-start.24 = (bf16[4,528,128]{2,1,0:T(8,128)(2,1)S(1)}, bf16[4,528,128]{2,1,0:T(8,128)(2,1)S(1)}, u32[]{:S(2)}, u32[]{:S(2)}) collective-permute-start(bf16[4,528,128]{2,1,0:T(8,128)(2,1)S(1)} %get-tuple-element.112), channel_id=1, source_target_pairs={{0,16},{4,20},{8,24},{12,28},{16,0},{20,4},{24,8},{28,12},{1,17},{... | collective-permute-start | bytes 1622024 | tf_op jit(solution)/shard_map/ppermute | solution.py:1075
  169.1 12.2 %collective-permute-start.26 = (bf16[2,128,1024]{2,1,0:T(8,128)(2,1)}, bf16[2,128,1024]{2,1,0:T(8,128)(2,1)S(1)}, u32[]{:S(2)}, u32[]{:S(2)}) collective-permute-start(bf16[2,128,1024]{2,1,0:T(8,128)(2,1)} %get-tuple-element.98.refs_0_), channel_id=1, source_target_pairs={{0,1},{1,0},{2,3},{3,2},{4,5},{5,4},{6,7},{7,6},{8,9},{9,8},{10,11... | collective-permute-start | bytes 1572872 | tf_op jit(solution)/shard_map/ppermute | solution.py:1075
  170.7 12.1 %collective-permute-start.31 = (bf16[16,1024]{1,0:T(8,128)(2,1)S(1)}, bf16[16,1024]{1,0:T(8,128)(2,1)S(1)}, u32[]{:S(2)}, u32[]{:S(2)}) collective-permute-start(bf16[16,1024]{1,0:T(8,128)(2,1)S(1)} %add.39.refs_2_), channel_id=1, source_target_pairs={{0,2},{1,3},{2,0},{3,1},{4,6},{5,7},{6,4},{7,5},{8,10},{9,11},{10,... | collective-permute-start | bytes 98312 | tf_op jit(solution)/shard_map/ppermute | solution.py:1075
  183.8 17.1 %all-to-all-start.4 = ((bf16[8,176,128]{2,1,0:T(8,128)(2,1)}), bf16[8,176,128]{2,1,0:T(8,128)(2,1)S(1)}, u32[]{:S(2)}, u32[]{:S(2)}) async-start(bf16[8,176,128]{2,1,0:T(8,128)(2,1)} %spread.1), calls=%async_computation.4 | async-start | bytes 720896 | tf_op jit(solution)/shard_map/all_to_all | solution.py:1234
  189.8 11.0 %collective-permute-start.34 = (bf16[528,128]{1,0:T(8,128)(2,1)S(1)}, bf16[528,128]{1,0:T(8,128)(2,1)S(1)}, u32[]{:S(2)}, u32[]{:S(2)}) collective-permute-start(bf16[528,128]{1,0:T(8,128)(2,1)S(1)} %get-tuple-element.114), channel_id=1, source_target_pairs={{0,12},{4,0},{8,4},{12,8},{16,28},{20,16},{24,20},{28,24},{1,13},{... | collective-permute-start | bytes 405512 | tf_op jit(solution)/shard_map/ppermute | solution.py:1103
  194.3 11.8 %collective-permute-start.25 = (bf16[128,1024]{1,0:T(8,128)(2,1)S(1)}, bf16[128,1024]{1,0:T(8,128)(2,1)S(1)}, u32[]{:S(2)}, u32[]{:S(2)}) collective-permute-start(bf16[128,1024]{1,0:T(8,128)(2,1)S(1)} %add.35.refs_4_), channel_id=1, source_target_pairs={{0,1},{1,0},{2,3},{3,2},{4,5},{5,4},{6,7},{7,6},{8,9},{9,8},{10,11... | collective-permute-start | bytes 786440 | tf_op jit(solution)/shard_map/ppermute | solution.py:1075
  (52 other events, 346.5 us)
